TPU v7x, 32 devices: a whole 2x2x4 slice. The times are simulated.
32 devices in a mesh: gx: 8 (over z, y), gy: 4 (over x, core).
Axes of the slice: x: 2, y: 2, z: 4, core: 2. Of those that a mesh axis runs over, the one named last changes fastest.
Arguments:
- tokens: bfloat16 [4096, 2048], P('gx', 'gy'), may hold values from -40 to 40
- norm_gain: float32 [2048], replicated, may hold values from 0.25 to 1.75
- expert_ids: int32 [4096, 6], P('gx'), may hold values from 0 to 63, all different within a row; in each aligned block of 512 rows (0 to 511, 512 to 1023, ...) at most 64 rows name the same one
- gate_weights: float32 [4096, 6], P('gx'), may hold values from 0.05 to 0.35
- shared_in: bfloat16 [2, 2048, 2816], P(None, 'gx', 'gy'), may hold values from -0.125 to 0.125
- shared_out: bfloat16 [2816, 2048], P('gy', 'gx'), may hold values from -0.109375 to 0.109375
- expert_in: bfloat16 [64, 2048, 2816], P(('gx', 'gy')), may hold values from -0.125 to 0.125
- expert_out: bfloat16 [64, 1408, 2048], P(('gx', 'gy')), may hold values from -0.15625 to 0.15625
Outputs:
- combined: bfloat16 [4096, 2048], P('gx', 'gy')
Inputs may be any that keep to these rules, and one draw needn't show every extreme that they name: `expert_ids`: each row names 6 different experts. In each aligned block of 512 rows (the tokens of one index of gx) no expert is named by more than 64 rows, and in some block one expert is named by exactly 64.
All inputs are finite; a program needn't handle non-finite values.
Results may differ from a plain program's by a relative error of at most 0.017.
Values may be sent and summed in bfloat16 or wider, within the bound.
No kernel may reach another device: no remote copies, remote signals or barrier semaphores. Data moves between devices by JAX's collectives and lax.ppermute only.
A program may use at most 128 MiB of HBM per device.

v0:
```python
import jax
import jax.numpy as jnp
from jax import lax
from jax.sharding import PartitionSpec as P

FF = 1408
EXPERTS = 64
CAP = 64


epsilon = 1e-06


def on_device(
    tokens, norm_gain, expert_ids, gate_weights, shared_in, shared_out, expert_in, expert_out
):
    row_count = lax.axis_size("gx")
    column_count = lax.axis_size("gy")
    column_index = lax.axis_index("gy")
    token_count = tokens.shape[0]
    top_count = expert_ids.shape[1]
    features = norm_gain.shape[0]
    held_rows = expert_in.shape[0]
    part_units = expert_out.shape[1]
    slice_count = FF // part_units
    gathered = lax.all_gather(tokens, "gy", axis=1, tiled=True)
    values = gathered.astype(jnp.float32)
    inverse_rms = lax.rsqrt(jnp.mean(values * values, axis=1, keepdims=True) + epsilon)
    normed = (values * inverse_rms * norm_gain).astype(jnp.bfloat16)
    shared_gate_up = jnp.einsum(
        "td,gdf->gtf",
        normed,
        lax.all_gather(shared_in, "gx", axis=1, tiled=True),
        preferred_element_type=jnp.float32,
    )
    shared_hidden = (jax.nn.silu(shared_gate_up[0]) * shared_gate_up[1]).astype(jnp.bfloat16)
    shared_term = jnp.dot(
        shared_hidden,
        lax.all_gather(shared_out, "gx", axis=1, tiled=True),
        preferred_element_type=jnp.float32,
    )
    flat_routes = expert_ids.reshape(-1)
    one_hot = (flat_routes[:, None] == jnp.arange(EXPERTS, dtype=jnp.int32)[None, :]).astype(
        jnp.int32
    )
    earlier_count = jnp.cumsum(one_hot, axis=0) - one_hot
    slot_index = jnp.sum(earlier_count * one_hot, axis=1)
    slice_here = column_index % slice_count
    weight_row = flat_routes * slice_count + slice_here
    owner_index = weight_row // held_rows
    on_column = owner_index % column_count == column_index
    target_row = owner_index // column_count
    member = weight_row % held_rows
    buffer_rows = row_count * held_rows * CAP
    position = (target_row * held_rows + member) * CAP + slot_index
    position = jnp.where(on_column, position, buffer_rows)
    token_number = jnp.arange(token_count * top_count, dtype=jnp.int32) // top_count
    token_slot = (
        jnp.full((buffer_rows + 1,), token_count, jnp.int32)
        .at[position]
        .set(token_number)[:buffer_rows]
    )
    padded = jnp.concatenate([normed, jnp.zeros((1, features), jnp.bfloat16)], axis=0)
    outgoing = padded[token_slot].reshape(row_count, held_rows, CAP, features)
    gate_up = jnp.einsum(
        "shcd,hdf->shcf",
        lax.all_to_all(outgoing, "gx", split_axis=0, concat_axis=0, tiled=True),
        expert_in,
        preferred_element_type=jnp.float32,
    )
    hidden = (jax.nn.silu(gate_up[..., :part_units]) * gate_up[..., part_units:]).astype(
        jnp.bfloat16
    )
    partial_value = jnp.einsum(
        "shcf,hfd->shcd", hidden, expert_out, preferred_element_type=jnp.float32
    )
    returned = lax.all_to_all(
        partial_value.astype(jnp.bfloat16), "gx", split_axis=0, concat_axis=0, tiled=True
    )
    results = returned.reshape(buffer_rows, features)
    padded_results = jnp.concatenate([results, jnp.zeros((1, features), jnp.bfloat16)], axis=0)
    place_grid = position.reshape(token_count, top_count)
    group_sum = shared_term
    for route_number in range(top_count):
        picked = padded_results[place_grid[:, route_number]].astype(jnp.float32)
        group_sum = group_sum + gate_weights[:, route_number : route_number + 1] * picked
    combined = lax.psum_scatter(
        group_sum.astype(jnp.bfloat16), "gy", scatter_dimension=1, tiled=True
    )
    return combined


def solution(mesh):
    in_specs = (
        P("gx", "gy"),
        P(),
        P("gx", None),
        P("gx", None),
        P(None, "gx", "gy"),
        P("gy", "gx"),
        P(("gx", "gy"), None, None),
        P(("gx", "gy"), None, None),
    )
    out_specs = P("gx", "gy")
    return jax.shard_map(
        on_device, mesh=mesh, in_specs=in_specs, out_specs=out_specs, check_vma=False
    )
```

profile of v0, /device:TPU:0, one launch (start us, length us, event | category | flops | bytes accessed | tf_op | source)
XLA Modules:
  0.0 472.1 jit_solution(6530120505374446393)
XLA Ops:
  8.1 0.9 copy.31
  9.6 18.3 %reduce-window.6 = s32[64,24,128]{2,1,0:T(8,128)S(1)} reduce-window(s32[64,24,128]{2,1,0:T(8,128)S(1)} %fusion.26, s32[]{:T(128)} %constant.93.clone.1), window={size=1x1x128 pad=0_0x0_0x127_0}, to_apply=%region_1.2 | reduce-window | flops 24969216 | bytes 1572868 | tf_op jit(solution)/shard_map/reduce-window
  29.5 11.8 %scatter_custom_fusion = s32[1025]{0:T(1024)S(1)} fusion(s32[3072]{0:T(1024)S(1)} %bitcast.75, s32[3072]{0:T(1024)S(1)} %add_select_fusion.4, s32[]{:T(128)} %constant.91.clone.1), kind=kCustom, calls=%fused_computation.101 | custom fusion | bytes 4104 | tf_op jit(solution)/shard_map/scatter | solution.py:61
  41.4 2.1 fusion.8
  43.4 2.1 fusion.10
  45.6 1.4 copy-done
  47.2 6.0 %gather_fusion = bf16[1024,2048]{1,0:T(8,128)(2,1)} fusion(bf16[513,2048]{1,0:T(8,128)(2,1)S(1)} %concatenate.6, s32[1024]{0:T(1024)S(1)} %fusion.48), kind=kCustom, calls=%fused_computation | custom fusion | bytes 8392704 | tf_op jit(solution)/shard_map/gather | solution.py:64
  53.2 7.3 %all-to-all-start = ((bf16[8,2,64,2048]{3,2,1,0:T(8,128)(2,1)}), bf16[8,2,64,2048]{3,2,1,0:T(8,128)(2,1)}, u32[]{:S(2)}, u32[]{:S(2)}) async-start(bf16[8,2,64,2048]{3,2,1,0:T(8,128)(2,1)} %bitcast.70), calls=%async_computation | async-start | bytes 8388608 | tf_op jit(solution)/shard_map/all_to_all | solution.py:67
  61.1 143.6 %all-to-all-done = bf16[8,2,64,2048]{3,2,1,0:T(8,128)(2,1)} async-done(((bf16[8,2,64,2048]{3,2,1,0:T(8,128)(2,1)}), bf16[8,2,64,2048]{3,2,1,0:T(8,128)(2,1)}, u32[]{:S(2)}, u32[]{:S(2)}) %all-to-all-start) | async-done | bytes 4194336 | tf_op jit(solution)/shard_map/all_to_all | solution.py:67
  204.7 21.6 %fusion.4 = f32[8,2,64,2816]{3,2,0,1:T(8,128)} fusion(bf16[2,2048,2816]{2,1,0:T(8,128)(2,1)} %param.14, bf16[8,2,64,2048]{3,2,1,0:T(8,128)(2,1)} %all-to-all-done), kind=kOutput, calls=%fused_computation.12 | convolution fusion | flops 11811160064 | bytes 38797312 | tf_op jit(solution)/shard_map/shcd,hdf->shcf/dot_general | solution.py:65
  226.4 13.0 %convert_bitcast_fusion = bf16[8,2,64,2048]{3,2,0,1:T(8,128)(2,1)S(1)} fusion(bf16[2,1408,2048]{2,1,0:T(8,128)(2,1)} %param.15, f32[8,2,64,2816]{3,2,0,1:T(8,128)} %fusion.4), kind=kOutput, calls=%fused_computation.22 | convolution fusion | flops 5916327936 | bytes 27262976 | tf_op jit(solution)/shard_map/shcf,hfd->shcd/dot_general | solution.py:74
  239.4 2.2 copy.37
  241.6 4.9 %all-to-all-start.1 = ((bf16[8,2,64,2048]{3,2,1,0:T(8,128)(2,1)}), bf16[8,2,64,2048]{3,2,1,0:T(8,128)(2,1)}, u32[]{:S(2)}, u32[]{:S(2)}) async-start(bf16[8,2,64,2048]{3,2,1,0:T(8,128)(2,1)} %copy.37), calls=%async_computation.1 | async-start | bytes 8388608 | tf_op jit(solution)/shard_map/all_to_all | solution.py:77
  248.8 7.4 %fusion.18 = f32[2,512,704]{1,2,0:T(8,128)} fusion(bf16[2,2048,704]{1,2,0:T(8,128)(2,1)} %all-gather.6.cloned.1.call-done, bf16[512,2048]{1,0:T(8,128)(2,1)S(1)} %copy-done.1), kind=kOutput, calls=%fused_computation.26 | convolution fusion | flops 2952790016 | bytes 10747904 | tf_op jit(solution)/shard_map/td,gdf->gtf/dot_general | solution.py:30
  256.2 115.8 %all-to-all-done.1 = bf16[8,2,64,2048]{3,2,1,0:T(8,128)(2,1)} async-done(((bf16[8,2,64,2048]{3,2,1,0:T(8,128)(2,1)}), bf16[8,2,64,2048]{3,2,1,0:T(8,128)(2,1)}, u32[]{:S(2)}, u32[]{:S(2)}) %all-to-all-start.1) | async-done | bytes 4194336 | tf_op jit(solution)/shard_map/all_to_all | solution.py:77
  372.1 4.7 concatenate.7
  376.8 7.1 %gather_fusion.6 = bf16[512,2048]{1,0:T(8,128)(2,1)S(1)} fusion(bf16[1025,2048]{1,0:T(8,128)(2,1)} %concatenate.7, s32[1024]{0:T(1024)S(1)} %get-tuple-element.17), kind=kCustom, calls=%fused_computation.6 | custom fusion | bytes 4196352 | tf_op jit(solution)/shard_map/gather | solution.py:85
  384.0 8.0 %gather_fusion.5 = bf16[512,2048]{1,0:T(8,128)(2,1)} fusion(bf16[1025,2048]{1,0:T(8,128)(2,1)} %concatenate.7, s32[1024]{0:T(1024)S(1)} %get-tuple-element.18), kind=kCustom, calls=%fused_computation.5 | custom fusion | bytes 4196352 | tf_op jit(solution)/shard_map/gather | solution.py:85
  391.9 8.0 %gather_fusion.4 = bf16[512,2048]{1,0:T(8,128)(2,1)} fusion(bf16[1025,2048]{1,0:T(8,128)(2,1)} %concatenate.7, s32[1024]{0:T(1024)S(1)} %get-tuple-element.19), kind=kCustom, calls=%fused_computation.4 | custom fusion | bytes 4196352 | tf_op jit(solution)/shard_map/gather | solution.py:85
  399.9 8.0 %gather_fusion.3 = bf16[512,2048]{1,0:T(8,128)(2,1)} fusion(bf16[1025,2048]{1,0:T(8,128)(2,1)} %concatenate.7, s32[1024]{0:T(1024)S(1)} %get-tuple-element.20), kind=kCustom, calls=%fused_computation.3 | custom fusion | bytes 4196352 | tf_op jit(solution)/shard_map/gather | solution.py:85
  407.9 8.2 %gather_fusion.2 = bf16[512,2048]{1,0:T(8,128)(2,1)} fusion(bf16[1025,2048]{1,0:T(8,128)(2,1)} %concatenate.7, s32[1024]{0:T(1024)S(1)} %get-tuple-element.21), kind=kCustom, calls=%fused_computation.2 | custom fusion | bytes 4196352 | tf_op jit(solution)/shard_map/gather | solution.py:85
  416.1 8.0 %gather_fusion.1 = bf16[512,2048]{1,0:T(8,128)(2,1)} fusion(bf16[1025,2048]{1,0:T(8,128)(2,1)} %concatenate.7, s32[1024]{0:T(1024)S(1)} %get-tuple-element.22), kind=kCustom, calls=%fused_computation.1 | custom fusion | bytes 4196352 | tf_op jit(solution)/shard_map/gather | solution.py:85
  424.1 10.0 %add_convert_fusion = bf16[512,2048]{1,0:T(8,128)(2,1)} fusion(bf16[512,2048]{1,0:T(8,128)(2,1)S(1)} %gather_fusion.6, bf16[512,2048]{1,0:T(8,128)(2,1)} %gather_fusion.5, bf16[512,2048]{1,0:T(8,128)(2,1)} %gather_fusion.4, bf16[512,2048]{1,0:T(8,128)(2,1)} %gather_fusion.3, bf16[512,2048]{1,0:T(8,128)(2,1)} %gather_fusion.2, ...), kind=kOutput, calls=%fused_computation.21 | convolution fusion | flops 1498480640 | bytes 20459520 | tf_op jit(solution)/shard_map/dot_general | solution.py:37
  434.2 30.5 %reduce-scatter.2.cloned.1.call-done = bf16[512,512]{1,0:T(8,128)(2,1)} async-done(((bf16[512,2048]{1,0:T(8,128)(2,1)}), bf16[512,512]{1,0:T(8,128)(2,1)}) %reduce-scatter.2.cloned.1.call-update) | async-done | bytes 524304 | tf_op jit(solution)/shard_map/reduce_scatter | solution.py:87
  (39 shorter events, 6.0 us)
Async XLA Ops:
  7.4 34.0 %all-gather.4.cloned.1.call-start = ((), (), s32[]{:S(2)}) async-start(), calls=%async_computation.3 | async-start | bytes 2621440 | tf_op jit(solution)/shard_map/all_gather | solution.py:26
  9.5 33.9 %copy-start.3 = (f32[2048]{0:T(1024)S(1)}, f32[2048]{0:T(1024)}, u32[]{:S(2)}) copy-start(f32[2048]{0:T(1024)} %param.9) | copy-start | bytes 24580
  45.6 1.4 copy-start
  53.2 151.5 %all-to-all-start = ((bf16[8,2,64,2048]{3,2,1,0:T(8,128)(2,1)}), bf16[8,2,64,2048]{3,2,1,0:T(8,128)(2,1)}, u32[]{:S(2)}, u32[]{:S(2)}) async-start(bf16[8,2,64,2048]{3,2,1,0:T(8,128)(2,1)} %bitcast.70), calls=%async_computation | async-start | bytes 8388608 | tf_op jit(solution)/shard_map/all_to_all | solution.py:67
  60.5 188.3 %all-gather.6.cloned.1.call-start = ((), (), s32[]{:S(2)}) async-start(), calls=%async_computation.4 | async-start | bytes 6488064 | tf_op jit(solution)/shard_map/all_gather | solution.py:33
  241.6 7.1 %copy-start.2 = (f32[512,6]{0,1:T(8,128)S(1)}, f32[512,6]{0,1:T(8,128)}, u32[]{:S(2)}) copy-start(f32[512,6]{0,1:T(8,128)} %param.11) | copy-start | bytes 36868
  241.6 7.2 %copy-start.1 = (bf16[512,2048]{1,0:T(8,128)(2,1)S(1)}, bf16[512,2048]{1,0:T(8,128)(2,1)}, u32[]{:S(2)}) copy-start(bf16[512,2048]{1,0:T(8,128)(2,1)} %copy-done) | copy-start | bytes 6291460
  241.6 130.4 %all-to-all-start.1 = ((bf16[8,2,64,2048]{3,2,1,0:T(8,128)(2,1)}), bf16[8,2,64,2048]{3,2,1,0:T(8,128)(2,1)}, u32[]{:S(2)}, u32[]{:S(2)}) async-start(bf16[8,2,64,2048]{3,2,1,0:T(8,128)(2,1)} %copy.37), calls=%async_computation.1 | async-start | bytes 8388608 | tf_op jit(solution)/shard_map/all_to_all | solution.py:77
  246.5 177.6 %all-gather.8.cloned.1.call-start = ((), (), s32[]{:S(2)}) async-start(), calls=%async_computation.5 | async-start | bytes 3244032 | tf_op jit(solution)/shard_map/all_gather | solution.py:39
  247.1 217.5 %reduce-scatter.2.cloned.1.call-start = ((), (), s32[]{:S(2)}) async-start(), calls=%async_computation.6 | async-start | bytes 2621440 | tf_op jit(solution)/shard_map/reduce_scatter | solution.py:87
Sparse Core Ops, SparseCore 0:
  9.8 25.3 all-gather.3
  434.3 30.2 reduce-scatter.1
Sparse Core Ops, SparseCore 1:
  63.0 160.5 all-gather.5
  249.0 113.2 all-gather.7
where the time goes:
time: 473 us; the launch traced here: 472 us
  waiting for transfers between devices  292 us (62%)
  local copies, waits for them, and re-layouts  76 us (16%)
  matrix products  52.1 us (11%)
  other arithmetic  24.9 us (5%)
  between operations  15.1 us (3%)
  starting transfers between devices  12.3 us (3%)
    all_to_all x1, waiting for transfers between devices, on_device(): lax.all_to_all(outgoing, 'gx', split_axis=0, concat_axis=0, tiled=True)  144 us
    all_to_all x1, waiting for transfers between devices, on_device(): lax.all_to_all(partial_value.astype(jnp.bfloat16), 'gx', split_axis=0, co...  116 us
    gather x6, local copies, waits for them, and re-layouts, on_device(): picked = padded_results[place_grid[:, route_number]].astype(jnp.float32)  47.3 us
    reduce_scatter x1, waiting for transfers between devices, on_device(): lax.psum_scatter(group_sum.astype(jnp.bfloat16), 'gy', scatter_dimension=...  30.5 us
    dot_general x1, matrix products, on_device(): jnp.einsum('shcd,hdf->shcf', lax.all_to_all(outgoing, 'gx', split_axis=0,...  21.6 us
    another operation x3, other arithmetic  18.8 us
    dot_general x1, matrix products, on_device(): jnp.einsum('shcf,hfd->shcd', hidden, expert_out, preferred_element_type=j...  13 us
    scatter x1, local copies, waits for them, and re-layouts, on_device(): token_slot = jnp.full((buffer_rows + 1,), token_count, jnp.int32).at[posi...  11.8 us
  transfers between devices with their start and end apart: 6, of which 3 were waited for; matrix products, arithmetic and copies ran while one was open for 28% of the time, Pallas kernels for 0%

commit v1 on v0

v1 whole, which is shorter than its diff:
```python
import jax
import jax.numpy as jnp
from jax import lax
from jax.experimental import pallas as pl
from jax.experimental.pallas import tpu as pltpu
from jax.sharding import PartitionSpec as P

FF = 1408
CAP = 64
META_ROWS = 16
BF16 = jnp.bfloat16
F32 = jnp.float32

epsilon = 1e-06

whole = pl.BlockSpec(memory_space=pltpu.VMEM)


def ring_of(count):
    order = list(range(0, count, 2)) + list(range(1, count, 2))[::-1]
    right = [(order[p], order[(p + 1) % count]) for p in range(count)]
    left = [(b, a) for a, b in right]
    return right, left


def slot_ranks(meta, named, top_count):
    token_count = meta.shape[1]
    hit = jnp.zeros((named.shape[0], token_count), F32)
    for r in range(top_count):
        hit = hit + jnp.where(meta[r : r + 1, :] == named[:, :1], 1.0, 0.0)
    before = lax.broadcasted_iota(jnp.int32, (token_count, token_count), 0) < (
        lax.broadcasted_iota(jnp.int32, (token_count, token_count), 1)
    )
    rank = jnp.dot(hit.astype(BF16), jnp.where(before, 1.0, 0.0).astype(BF16), preferred_element_type=F32)
    return jnp.where(hit > 0.0, rank, -1.0)


def dispatch_kernel(blocks, peers, held, top_count, *refs):
    named_ref = refs[0]
    payloads = refs[1 : 1 + blocks]
    metas = refs[1 + blocks : 1 + 2 * blocks]
    outs = refs[1 + 2 * blocks : 1 + 2 * blocks + peers]
    choose = refs[-1]
    for b in range(blocks):
        meta = metas[b][...].astype(F32)
        token_count = meta.shape[1]
        ranks = slot_ranks(meta, named_ref[...], top_count)
        slot = lax.broadcasted_iota(jnp.int32, (CAP, token_count), 0).astype(F32)
        for c in range(peers * held):
            choose[c * CAP : (c + 1) * CAP, :] = jnp.where(slot == ranks[c : c + 1, :], 1.0, 0.0).astype(BF16)
        rows = jnp.dot(choose[...], payloads[b][:token_count, :], preferred_element_type=F32).astype(BF16)
        for k in range(peers):
            outs[k][b] = rows[k * held * CAP : (k + 1) * held * CAP, :]


def combine_kernel(blocks, incoming, peers, held, top_count, *refs):
    named_ref = refs[0]
    metas = refs[1 : 1 + blocks]
    results = refs[1 + blocks : 1 + blocks + peers]
    coming = refs[1 + blocks + peers : 1 + blocks + peers + incoming]
    outs = refs[1 + blocks + peers + incoming : -2]
    choose, gathered = refs[-2:]
    for b in range(blocks):
        meta = metas[b][...].astype(F32)
        token_count = meta.shape[1]
        named = named_ref[...]
        ranks = slot_ranks(meta, named, top_count)
        weight = jnp.zeros((named.shape[0], token_count), F32)
        for r in range(top_count):
            weight = weight + jnp.where(
                meta[r : r + 1, :] == named[:, :1], meta[top_count + r : top_count + r + 1, :], 0.0
            )
        slot = lax.broadcasted_iota(jnp.int32, (CAP, token_count), 0).astype(F32)
        for c in range(peers * held):
            choose[c * CAP : (c + 1) * CAP, :] = jnp.where(
                slot == ranks[c : c + 1, :], weight[c : c + 1, :], 0.0
            ).astype(BF16)
        for k in range(peers):
            gathered[k * held * CAP : (k + 1) * held * CAP, :] = results[k][b]
        total = lax.dot_general(
            choose[...], gathered[...], (((0,), (0,)), ((), ())), preferred_element_type=F32
        )
        if incoming == blocks:
            total = total + coming[b][...].astype(F32)
        elif blocks == 1:
            for extra in coming:
                total = total + extra[...].astype(F32)
        outs[b][...] = total.astype(BF16)


def expert_kernel(sizes, peers, held, units, features, order_ref, gain_ref, *refs):
    groups = len(sizes)
    parts = refs[: groups * peers]
    in_ref, out_ref = refs[groups * peers : groups * peers + 2]
    outs = refs[groups * peers + 2 : 2 * groups * peers + 2]
    ready, total, hidden = refs[-3:]
    member, step = pl.program_id(0), pl.program_id(1)

    @pl.when(step == 0)
    def _():
        rows = [
            [
                parts[g * peers + k][b, pl.ds(pl.multiple_of(member * CAP, CAP), CAP), :].astype(F32)
                for g in range(groups)
                for b in range(sizes[g])
            ]
            for k in range(peers)
        ]
        for n in range(sum(sizes)):
            squares = jnp.sum(rows[0][n] * rows[0][n], axis=1, keepdims=True)
            for k in range(1, peers):
                squares = squares + jnp.sum(rows[k][n] * rows[k][n], axis=1, keepdims=True)
            inverse_rms = lax.rsqrt(squares / features + epsilon)
            for k in range(peers):
                ready[k, n * CAP : (n + 1) * CAP, :] = (rows[k][n] * inverse_rms * gain_ref[k]).astype(BF16)

    @pl.when(step < peers)
    def _():
        product = jnp.dot(ready[jnp.minimum(step, peers - 1)], in_ref[0], preferred_element_type=F32)

        @pl.when(step == 0)
        def _():
            total[...] = product

        @pl.when(step > 0)
        def _():
            total[...] = total[...] + product

    @pl.when(step == peers - 1)
    def _():
        gate = total[:, :units]
        hidden[...] = (gate / (1.0 + jnp.exp(-gate)) * total[:, units:]).astype(BF16)

    for k in range(peers):

        @pl.when(step == peers + k)
        def _(k=k):
            value = jnp.dot(hidden[...], out_ref[0], preferred_element_type=F32).astype(BF16)
            n = 0
            for g in range(groups):
                for b in range(sizes[g]):
                    outs[g * peers + k][b, pl.ds(pl.multiple_of(member * CAP, CAP), CAP), :] = value[
                        n * CAP : (n + 1) * CAP, :
                    ]
                    n += 1


def shared_kernel(peers, features, order_ref, gain_ref, *refs):
    parts = refs[:peers]
    in_ref, out_ref = refs[peers : peers + 2]
    outs = refs[peers + 2 : 2 * peers + 2]
    ready, gate, up, hidden = refs[-4:]
    step = pl.program_id(0)

    @pl.when(step == 0)
    def _():
        rows = [part[...].astype(F32) for part in parts]
        squares = sum(jnp.sum(r * r, axis=1, keepdims=True) for r in rows)
        inverse_rms = lax.rsqrt(squares / features + epsilon)
        for k in range(peers):
            ready[k] = (rows[k] * inverse_rms * gain_ref[k]).astype(BF16)

    @pl.when(step < peers)
    def _():
        mine = ready[jnp.minimum(step, peers - 1)]
        gate_part = jnp.dot(mine, in_ref[0], preferred_element_type=F32)
        up_part = jnp.dot(mine, in_ref[1], preferred_element_type=F32)

        @pl.when(step == 0)
        def _():
            gate[...] = gate_part
            up[...] = up_part

        @pl.when(step > 0)
        def _():
            gate[...] = gate[...] + gate_part
            up[...] = up[...] + up_part

    @pl.when(step == peers - 1)
    def _():
        value = gate[...]
        hidden[...] = (value / (1.0 + jnp.exp(-value)) * up[...]).astype(BF16)

    for k in range(peers):

        @pl.when(step == peers + k)
        def _(k=k):
            outs[k][...] = jnp.dot(hidden[...], out_ref[...], preferred_element_type=F32).astype(BF16)


def on_device(
    tokens, norm_gain, expert_ids, gate_weights, shared_in, shared_out, expert_in, expert_out
):
    row_count = lax.axis_size("gx")
    peers = lax.axis_size("gy")
    row, column = lax.axis_index("gx"), lax.axis_index("gy")
    token_count, width = tokens.shape
    top_count = expert_ids.shape[1]
    features = norm_gain.shape[0]
    held = expert_in.shape[0]
    units = expert_out.shape[1]
    slice_count = FF // units
    order = jnp.arange(peers, dtype=jnp.int32) ^ column
    gain = norm_gain.reshape(peers, 1, width)[order]
    slices = ((row * peers + order)[:, None] * held + jnp.arange(held, dtype=jnp.int32)).reshape(-1)
    named = jnp.broadcast_to((slices // slice_count).astype(F32)[:, None], (peers * held, 128))

    right, left = ring_of(row_count)

    def to_peer(value, mask):
        return lax.ppermute(value, "gy", [(s, s ^ mask) for s in range(peers)])

    meta = jnp.concatenate(
        [
            expert_ids.T.astype(BF16),
            gate_weights.T.astype(BF16),
            jnp.zeros((META_ROWS - 2 * top_count, token_count), BF16),
        ],
        axis=0,
    )
    payload = jnp.concatenate([tokens, meta.reshape(-1, width)], axis=0)

    from_left, from_right = [payload], [payload]
    for step in range(1, row_count // 2 + 1):
        from_left.append(lax.ppermute(from_left[-1], "gx", right))
        if step < row_count - row_count // 2:
            from_right.append(lax.ppermute(from_right[-1], "gx", left))
    groups = [[payload]]
    for step in range(1, row_count // 2 + 1):
        groups.append([from_left[step]] + ([from_right[step]] if step < len(from_right) else []))
    sizes = [len(group) for group in groups]
    metas = [[p[token_count:].reshape(META_ROWS, token_count) for p in group] for group in groups]

    parts = []
    for group, group_meta in zip(groups, metas):
        blocks = len(group)
        rows = pl.pallas_call(
            lambda *refs, blocks=blocks: dispatch_kernel(blocks, peers, held, top_count, *refs),
            out_shape=[jax.ShapeDtypeStruct((blocks, held * CAP, width), BF16)] * peers,
            in_specs=[whole] * (1 + 2 * blocks),
            out_specs=[whole] * peers,
            scratch_shapes=[pltpu.VMEM((peers * held * CAP, token_count), BF16)],
            compiler_params=pltpu.CompilerParams(vmem_limit_bytes=32 << 20),
            name="dispatch_rows",
        )(named, *group, *group_meta)
        parts += [rows[0]] + [to_peer(rows[k], k) for k in range(1, peers)]

    total_rows = row_count * CAP
    results = pl.pallas_call(
        lambda *refs: expert_kernel(sizes, peers, held, units, features, *refs),
        grid_spec=pltpu.PrefetchScalarGridSpec(
            num_scalar_prefetch=1,
            grid=(held, 2 * peers),
            in_specs=[whole] * (1 + len(parts))
            + [
                pl.BlockSpec((1, width, 2 * units), lambda h, s, o: (h, o[jnp.minimum(s, peers - 1)], 0)),
                pl.BlockSpec((1, units, width), lambda h, s, o: (h, 0, o[jnp.maximum(s - peers, 0)])),
            ],
            out_specs=[whole] * len(parts),
            scratch_shapes=[
                pltpu.VMEM((peers, total_rows, width), BF16),
                pltpu.VMEM((total_rows, 2 * units), F32),
                pltpu.VMEM((total_rows, units), BF16),
            ],
        ),
        out_shape=[jax.ShapeDtypeStruct(part.shape, BF16) for part in parts],
        compiler_params=pltpu.CompilerParams(vmem_limit_bytes=56 << 20),
        name="expert_slices",
    )(order, gain, *parts, expert_in, expert_out)

    pieces = {0: tokens}
    mask = peers // 2
    while mask:
        for k in list(pieces):
            pieces[k ^ mask] = to_peer(pieces[k], mask)
        mask //= 2
    shared_units = shared_out.shape[0]
    shared_parts = pl.pallas_call(
        lambda *refs: shared_kernel(peers, features, *refs),
        grid_spec=pltpu.PrefetchScalarGridSpec(
            num_scalar_prefetch=1,
            grid=(2 * peers,),
            in_specs=[whole] * (1 + peers)
            + [
                pl.BlockSpec((2, width, shared_units), lambda s, o: (0, o[jnp.minimum(s, peers - 1)], 0)),
                pl.BlockSpec((shared_units, width), lambda s, o: (0, o[jnp.maximum(s - peers, 0)])),
            ],
            out_specs=[whole] * peers,
            scratch_shapes=[
                pltpu.VMEM((peers, token_count, width), BF16),
                pltpu.VMEM((token_count, shared_units), F32),
                pltpu.VMEM((token_count, shared_units), F32),
                pltpu.VMEM((token_count, shared_units), BF16),
            ],
        ),
        out_shape=[jax.ShapeDtypeStruct((token_count, width), BF16)] * peers,
        compiler_params=pltpu.CompilerParams(vmem_limit_bytes=40 << 20),
        name="shared_experts",
    )(
        order,
        gain,
        *[pieces[k] for k in range(peers)],
        lax.all_gather(shared_in, "gx", axis=1, tiled=True),
        lax.all_gather(shared_out, "gx", axis=1, tiled=True),
    )
    shared_parts = list(shared_parts)
    mask, last = 1, None
    while mask < peers:
        kept = [k for k in range(0, peers, 2 * mask)]
        arrived = {k: to_peer(shared_parts[k + mask], mask) for k in kept}
        if 2 * mask == peers:
            last = arrived[0]
        else:
            for k in kept:
                shared_parts[k] = (shared_parts[k].astype(F32) + arrived[k].astype(F32)).astype(BF16)
        mask *= 2

    def combine(group_number, coming):
        size = sizes[group_number]
        back = results[group_number * peers : (group_number + 1) * peers]
        back = [back[0]] + [to_peer(back[k], k) for k in range(1, peers)]
        return pl.pallas_call(
            lambda *refs: combine_kernel(size, len(coming), peers, held, top_count, *refs),
            out_shape=[jax.ShapeDtypeStruct((token_count, width), BF16)] * size,
            in_specs=[whole] * (1 + size + peers + len(coming)),
            out_specs=[whole] * size,
            scratch_shapes=[
                pltpu.VMEM((peers * held * CAP, token_count), BF16),
                pltpu.VMEM((peers * held * CAP, width), BF16),
            ],
            compiler_params=pltpu.CompilerParams(vmem_limit_bytes=32 << 20),
            name="combine_rows",
        )(named, *metas[group_number], *back, *coming)

    coming_left, coming_right = None, None
    for step in range(row_count // 2, 0, -1):
        coming = [c for c in (coming_left, coming_right) if c is not None]
        sums = combine(step, coming[:0] if coming_left is None and coming_right is None else
                       ([coming_left if coming_left is not None else jnp.zeros_like(tokens), coming_right]))
        if sizes[step] == 1:
            coming_right, coming_left = lax.ppermute(sums[0], "gx", right), None
        else:
            coming_left = lax.ppermute(sums[0], "gx", left)
            coming_right = lax.ppermute(sums[1], "gx", right)
    return combine(0, [coming_left, coming_right, shared_parts[0], last])[0]


def solution(mesh):
    in_specs = (
        P("gx", "gy"),
        P(),
        P("gx", None),
        P("gx", None),
        P(None, "gx", "gy"),
        P("gy", "gx"),
        P(("gx", "gy"), None, None),
        P(("gx", "gy"), None, None),
    )
    out_specs = P("gx", "gy")
    return jax.shard_map(
        on_device, mesh=mesh, in_specs=in_specs, out_specs=out_specs, check_vma=False
    )
```

time: 473 us -> 286 us (0.60)
  waiting for transfers between devices: 292 us -> 145 us
  Pallas kernels: 0 us -> 62.5 us
  local copies, waits for them, and re-layouts: 76 us -> 13.6 us
  matrix products: 52.1 us -> 0 us
  starting transfers between devices: 12.3 us -> 48.9 us
  other arithmetic: 24.9 us -> 0.97 us
    all_to_all x2 -> x0, waiting for transfers between devices: 259 us -> none  [the longest x1 144 us: on_device(): lax.all_to_all(outgoing, 'gx', split_axis=0, concat_axis=0, tiled=True)]
    ppermute x0 -> x50, waiting for transfers between devices: none -> 144 us  [the longest x36 87.5 us: to_peer(): return lax.ppermute(value, 'gy', [(s, s ^ mask) for s in range(peers)])]
    pallas_call x0 -> x12, Pallas kernels: none -> 62.5 us  [the longest x1 38.3 us: on_device(): pl.pallas_call(lambda *refs: expert_kernel(sizes, peers, held, units, fea...]
    gather x7 -> x2, local copies, waits for them, and re-layouts: 53.3 us -> 1.17 us  [on_device(): gain = norm_gain.reshape(peers, 1, width)[order]]
    dot_general x4 -> x0, matrix products: 52.1 us -> none  [the longest x1 21.6 us: on_device(): jnp.einsum('shcd,hdf->shcf', lax.all_to_all(outgoing, 'gx', split_axis=0,...]
    ppermute x0 -> x50, starting transfers between devices: none -> 48.9 us  [the longest x36 24.2 us: to_peer(): return lax.ppermute(value, 'gy', [(s, s ^ mask) for s in range(peers)])]
    reduce_scatter x1 -> x0, waiting for transfers between devices: 30.5 us -> none  [on_device(): lax.psum_scatter(group_sum.astype(jnp.bfloat16), 'gy', scatter_dimension=...]
    another operation x3 -> x0, other arithmetic: 18.8 us -> none
  transfers between devices with their start and end apart: 6 -> 52, of which waited for: 3 -> 24; matrix products, arithmetic and copies ran while one was open for 28% -> 2% of each run, Pallas kernels for 0% -> 21%
where the time goes in v1:
time: 286 us; the launch traced here: 285 us
  waiting for transfers between devices  145 us (51%)
  Pallas kernels  62.5 us (22%)
  starting transfers between devices  48.9 us (17%)
  between operations  13.9 us (5%)
  local copies, waits for them, and re-layouts  13.6 us (5%)
    ppermute x36, waiting for transfers between devices, to_peer(): return lax.ppermute(value, 'gy', [(s, s ^ mask) for s in range(peers)])  87.5 us
    ppermute x4, waiting for transfers between devices, on_device(): from_left.append(lax.ppermute(from_left[-1], 'gx', right))  52.3 us
    pallas_call x1, Pallas kernels, on_device(): pl.pallas_call(lambda *refs: expert_kernel(sizes, peers, held, units, fea...  38.3 us
    ppermute x36, starting transfers between devices, to_peer(): return lax.ppermute(value, 'gy', [(s, s ^ mask) for s in range(peers)])  24.2 us
    ppermute x4, starting transfers between devices, on_device(): from_left.append(lax.ppermute(from_left[-1], 'gx', right))  14.4 us
    unnamed x77, local copies, waits for them, and re-layouts  10.7 us
    pallas_call x1, Pallas kernels, on_device(): pl.pallas_call(lambda *refs: shared_kernel(peers, features, *refs), grid_...  10.1 us
    pallas_call x5, Pallas kernels, combine(): pl.pallas_call(lambda *refs: combine_kernel(size, len(coming), peers, hel...  7.62 us
  transfers between devices with their start and end apart: 52, of which 24 were waited for; matrix products, arithmetic and copies ran while one was open for 2% of the time, Pallas kernels for 21%

profile of v1, /device:TPU:0, one launch (start us, length us, event | category | flops | bytes accessed | tf_op | source)
XLA Modules:
  0.0 284.6 jit_solution(8369273352907099715)
XLA Ops:
  9.8 3.1 %collective-permute-start.3 = (bf16[528,512]{1,0:T(8,128)(2,1)S(1)}, bf16[528,512]{1,0:T(8,128)(2,1)S(1)}, u32[]{:S(2)}, u32[]{:S(2)}) collective-permute-start(bf16[528,512]{1,0:T(8,128)(2,1)S(1)} %pad_maximum_fusion.refs_1_), channel_id=1, source_target_pairs={{0,8},{8,16},{16,24},{24,28},{28,20},{20,12},{12,4},{4,0},{1,9},{9... | collective-permute-start | bytes 1622024 | tf_op jit(solution)/shard_map/ppermute | solution.py:225
  12.9 15.4 %collective-permute-done.3.refs_1_ = bf16[528,512]{1,0:T(8,128)(2,1)S(1)} collective-permute-done((bf16[528,512]{1,0:T(8,128)(2,1)S(1)}, bf16[528,512]{1,0:T(8,128)(2,1)S(1)}, u32[]{:S(2)}, u32[]{:S(2)}) %collective-permute-start.3) | collective-permute-done | bytes 540704 | tf_op jit(solution)/shard_map/ppermute | solution.py:225
  28.3 2.5 collective-permute-start.8
  30.9 17.4 %collective-permute-done.8.refs_1_ = bf16[528,512]{1,0:T(8,128)(2,1)S(1)} collective-permute-done((bf16[528,512]{1,0:T(8,128)(2,1)S(1)}, bf16[528,512]{1,0:T(8,128)(2,1)S(1)}, u32[]{:S(2)}, u32[]{:S(2)}) %collective-permute-start.8) | collective-permute-done | bytes 540704 | tf_op jit(solution)/shard_map/ppermute | solution.py:225
  48.3 2.5 collective-permute-start.13
  53.6 19.5 %collective-permute-done.13.refs_1_ = bf16[528,512]{1,0:T(8,128)(2,1)S(1)} collective-permute-done((bf16[528,512]{1,0:T(8,128)(2,1)S(1)}, bf16[528,512]{1,0:T(8,128)(2,1)S(1)}, u32[]{:S(2)}, u32[]{:S(2)}) %collective-permute-start.13) | collective-permute-done | bytes 540704 | tf_op jit(solution)/shard_map/ppermute | solution.py:225
  73.1 6.4 %collective-permute-start.18 = (bf16[528,512]{1,0:T(8,128)(2,1)S(1)}, bf16[528,512]{1,0:T(8,128)(2,1)S(1)}, u32[]{:S(2)}, u32[]{:S(2)}) collective-permute-start(bf16[528,512]{1,0:T(8,128)(2,1)S(1)} %collective-permute-done.13.refs_1_), channel_id=1, source_target_pairs={{0,8},{8,16},{16,24},{24,28},{28,20},{20,12},{12,4},{4,0},{1,9},{9... | collective-permute-start | bytes 1622024 | tf_op jit(solution)/shard_map/ppermute | solution.py:225
  92.4 4.6 %collective-permute-done.7.refs_9_ = bf16[2,128,512]{2,1,0:T(8,128)(2,1)S(1)} collective-permute-done((bf16[2,128,512]{2,1,0:T(8,128)(2,1)S(1)}, bf16[2,128,512]{2,1,0:T(8,128)(2,1)S(1)}, u32[]{:S(2)}, u32[]{:S(2)}) %collective-permute-start.7) | collective-permute-done | bytes 262176 | tf_op jit(solution)/shard_map/ppermute | solution.py:211
  100.5 3.1 %collective-permute-done.11.refs_12_ = bf16[2,128,512]{2,1,0:T(8,128)(2,1)S(1)} collective-permute-done((bf16[2,128,512]{2,1,0:T(8,128)(2,1)S(1)}, bf16[2,128,512]{2,1,0:T(8,128)(2,1)S(1)}, u32[]{:S(2)}, u32[]{:S(2)}) %collective-permute-start.11) | collective-permute-done | bytes 262176 | tf_op jit(solution)/shard_map/ppermute | solution.py:211
  103.5 4.7 %collective-permute-done.12.refs_13_ = bf16[2,128,512]{2,1,0:T(8,128)(2,1)S(1)} collective-permute-done((bf16[2,128,512]{2,1,0:T(8,128)(2,1)S(1)}, bf16[2,128,512]{2,1,0:T(8,128)(2,1)S(1)}, u32[]{:S(2)}, u32[]{:S(2)}) %collective-permute-start.12) | collective-permute-done | bytes 262176 | tf_op jit(solution)/shard_map/ppermute | solution.py:211
  114.8 4.8 %collective-permute-done.17.refs_17_ = bf16[2,128,512]{2,1,0:T(8,128)(2,1)} collective-permute-done((bf16[2,128,512]{2,1,0:T(8,128)(2,1)S(1)}, bf16[2,128,512]{2,1,0:T(8,128)(2,1)}, u32[]{:S(2)}, u32[]{:S(2)}) %collective-permute-start.17) | collective-permute-done | bytes 262176 | tf_op jit(solution)/shard_map/ppermute | solution.py:211
  119.6 3.6 %collective-permute-done.20.refs_20_ = bf16[1,128,512]{2,1,0:T(8,128)(2,1)S(1)} collective-permute-done((bf16[1,128,512]{2,1,0:T(8,128)(2,1)S(1)}, bf16[1,128,512]{2,1,0:T(8,128)(2,1)S(1)}, u32[]{:S(2)}, u32[]{:S(2)}) %collective-permute-start.20) | collective-permute-done | bytes 131104 | tf_op jit(solution)/shard_map/ppermute | solution.py:211
  125.7 38.3 %expert_slices.1 = (bf16[1,128,512]{2,1,0:T(8,128)(2,1)}, bf16[1,128,512]{2,1,0:T(8,128)(2,1)}, bf16[1,128,512]{2,1,0:T(8,128)(2,1)}, bf16[1,128,512]{2,1,0:T(8,...) custom-call(s32[4]{0:T(128)} %iota_xor_fusion.refs_0_, ...), custom_call_target="tpu_custom_call" | custom-call | tf_op jit(solution)/shard_map/expert_slices/pallas_call | solution.py:249
  166.2 5.1 %collective-permute-done.35.refs_4_ = bf16[1,128,512]{2,1,0:T(8,128)(2,1)S(1)} collective-permute-done((bf16[1,128,512]{2,1,0:T(8,128)(2,1)}, bf16[1,128,512]{2,1,0:T(8,128)(2,1)S(1)}, u32[]{:S(2)}, u32[]{:S(2)}) %collective-permute-start.35) | collective-permute-done | bytes 131104 | tf_op jit(solution)/shard_map/ppermute | solution.py:211
  174.0 2.4 collective-permute-start.37
  180.4 16.4 %collective-permute-done.32.refs_5_ = bf16[2,128,512]{2,1,0:T(8,128)(2,1)S(1)} collective-permute-done((bf16[2,128,512]{2,1,0:T(8,128)(2,1)}, bf16[2,128,512]{2,1,0:T(8,128)(2,1)S(1)}, u32[]{:S(2)}, u32[]{:S(2)}) %collective-permute-start.32) | collective-permute-done | bytes 262176 | tf_op jit(solution)/shard_map/ppermute | solution.py:211
  198.2 4.0 %collective-permute-done.33.refs_6_ = bf16[2,128,512]{2,1,0:T(8,128)(2,1)S(1)} collective-permute-done((bf16[2,128,512]{2,1,0:T(8,128)(2,1)}, bf16[2,128,512]{2,1,0:T(8,128)(2,1)S(1)}, u32[]{:S(2)}, u32[]{:S(2)}) %collective-permute-start.33) | collective-permute-done | bytes 262176 | tf_op jit(solution)/shard_map/ppermute | solution.py:211
  203.4 3.5 %collective-permute-start.38 = (bf16[512,512]{1,0:T(8,128)(2,1)S(1)}, bf16[512,512]{1,0:T(8,128)(2,1)S(1)}, u32[]{:S(2)}, u32[]{:S(2)}) collective-permute-start(bf16[512,512]{1,0:T(8,128)(2,1)S(1)} %get-tuple-element.95), channel_id=1, source_target_pairs={{8,0},{16,8},{24,16},{28,24},{20,28},{12,20},{4,12},{0,4},{9,1},{1... | collective-permute-start | bytes 1572872 | tf_op jit(solution)/shard_map/ppermute | solution.py:343
  208.8 7.6 %collective-permute-done.30.refs_6_ = bf16[2,128,512]{2,1,0:T(8,128)(2,1)S(1)} collective-permute-done((bf16[2,128,512]{2,1,0:T(8,128)(2,1)S(1)}, bf16[2,128,512]{2,1,0:T(8,128)(2,1)S(1)}, u32[]{:S(2)}, u32[]{:S(2)}) %collective-permute-start.30) | collective-permute-done | bytes 262176 | tf_op jit(solution)/shard_map/ppermute | solution.py:211
  224.9 2.8 copy-done
  229.5 10.1 %shared_experts.1 = (bf16[512,512]{1,0:T(8,128)(2,1)S(1)}, bf16[512,512]{1,0:T(8,128)(2,1)S(1)}, bf16[512,512]{1,0:T(8,128)(2,1)S(1)}, bf16[512,512]{1,0:T(8,128)(2,1)S(1)}) custom-call(s32[4]{0:T(128)S(1)} %copy-done.14, f32[4,1,512]{2,1,0:T(1,128)S(1)} %copy-done.13, bf16[512,512]{1,0:T(8,128)(2,1)S(1)} %copy-done.2, ...), custom_call_target="tpu_custom_call" | custom-call | tf_op jit(solution)/shard_map/shared_experts/pallas_call | solution.py:278
  241.5 7.3 %collective-permute-done.26.refs_5_ = bf16[2,128,512]{2,1,0:T(8,128)(2,1)S(1)} collective-permute-done((bf16[2,128,512]{2,1,0:T(8,128)(2,1)S(1)}, bf16[2,128,512]{2,1,0:T(8,128)(2,1)S(1)}, u32[]{:S(2)}, u32[]{:S(2)}) %collective-permute-start.26) | collective-permute-done | bytes 262176 | tf_op jit(solution)/shard_map/ppermute | solution.py:211
  248.8 4.7 %collective-permute-done.27.refs_6_ = bf16[2,128,512]{2,1,0:T(8,128)(2,1)S(1)} collective-permute-done((bf16[2,128,512]{2,1,0:T(8,128)(2,1)S(1)}, bf16[2,128,512]{2,1,0:T(8,128)(2,1)S(1)}, u32[]{:S(2)}, u32[]{:S(2)}) %collective-permute-start.27) | collective-permute-done | bytes 262176 | tf_op jit(solution)/shard_map/ppermute | solution.py:211
  262.4 13.2 %collective-permute-done.23.refs_4_ = bf16[1,128,512]{2,1,0:T(8,128)(2,1)S(1)} collective-permute-done((bf16[1,128,512]{2,1,0:T(8,128)(2,1)S(1)}, bf16[1,128,512]{2,1,0:T(8,128)(2,1)S(1)}, u32[]{:S(2)}, u32[]{:S(2)}) %collective-permute-start.23) | collective-permute-done | bytes 131104 | tf_op jit(solution)/shard_map/ppermute | solution.py:211
  (196 shorter events, 67.8 us)
Async XLA Ops:
  6.5 218.3 %all-gather.5.cloned.1.call-start = ((), (), s32[]{:S(2)}) async-start(), calls=%async_computation.1 | async-start | bytes 3244032 | tf_op jit(solution)/shard_map/all_gather | solution.py:304
  7.3 217.5 %all-gather.3.cloned.1.call-start = ((), (), s32[]{:S(2)}) async-start(), calls=%async_computation | async-start | bytes 7077888 | tf_op jit(solution)/shard_map/all_gather | solution.py:303
  9.8 18.5 %collective-permute-start.3 = (bf16[528,512]{1,0:T(8,128)(2,1)S(1)}, bf16[528,512]{1,0:T(8,128)(2,1)S(1)}, u32[]{:S(2)}, u32[]{:S(2)}) collective-permute-start(bf16[528,512]{1,0:T(8,128)(2,1)S(1)} %pad_maximum_fusion.refs_1_), channel_id=1, source_target_pairs={{0,8},{8,16},{16,24},{24,28},{28,20},{20,12},{12,4},{4,0},{1,9},{9... | collective-permute-start | bytes 1622024 | tf_op jit(solution)/shard_map/ppermute | solution.py:225
  28.3 20.0 %collective-permute-start.8 = (bf16[528,512]{1,0:T(8,128)(2,1)S(1)}, bf16[528,512]{1,0:T(8,128)(2,1)S(1)}, u32[]{:S(2)}, u32[]{:S(2)}) collective-permute-start(bf16[528,512]{1,0:T(8,128)(2,1)S(1)} %collective-permute-done.3.refs_1_), channel_id=1, source_target_pairs={{0,8},{8,16},{16,24},{24,28},{28,20},{20,12},{12,4},{4,0},{1,9},{9... | collective-permute-start | bytes 1622024 | tf_op jit(solution)/shard_map/ppermute | solution.py:225
  30.8 20.0 %collective-permute-start.9 = (bf16[528,512]{1,0:T(8,128)(2,1)}, bf16[528,512]{1,0:T(8,128)(2,1)S(1)}, u32[]{:S(2)}, u32[]{:S(2)}) collective-permute-start(bf16[528,512]{1,0:T(8,128)(2,1)} %collective-permute-done.4.refs_2_), channel_id=1, source_target_pairs={{8,0},{16,8},{24,16},{28,24},{20,28},{12,20},{4,12},{0,4},{9,1},{1... | collective-permute-start | bytes 1622024 | tf_op jit(solution)/shard_map/ppermute | solution.py:227
  48.3 24.9 %collective-permute-start.13 = (bf16[528,512]{1,0:T(8,128)(2,1)S(1)}, bf16[528,512]{1,0:T(8,128)(2,1)S(1)}, u32[]{:S(2)}, u32[]{:S(2)}) collective-permute-start(bf16[528,512]{1,0:T(8,128)(2,1)S(1)} %collective-permute-done.8.refs_1_), channel_id=1, source_target_pairs={{0,8},{8,16},{16,24},{24,28},{28,20},{20,12},{12,4},{4,0},{1,9},{9... | collective-permute-start | bytes 1622024 | tf_op jit(solution)/shard_map/ppermute | solution.py:225
  50.8 36.1 %collective-permute-start.14 = (bf16[528,512]{1,0:T(8,128)(2,1)S(1)}, bf16[528,512]{1,0:T(8,128)(2,1)}, u32[]{:S(2)}, u32[]{:S(2)}) collective-permute-start(bf16[528,512]{1,0:T(8,128)(2,1)S(1)} %collective-permute-done.9.refs_2_), channel_id=1, source_target_pairs={{8,0},{16,8},{24,16},{28,24},{20,28},{12,20},{4,12},{0,4},{9,1},{1... | collective-permute-start | bytes 1622024 | tf_op jit(solution)/shard_map/ppermute | solution.py:227
  51.7 31.4 %collective-permute-start = (bf16[1,128,512]{2,1,0:T(8,128)(2,1)S(1)}, bf16[1,128,512]{2,1,0:T(8,128)(2,1)S(1)}, u32[]{:S(2)}, u32[]{:S(2)}) collective-permute-start(bf16[1,128,512]{2,1,0:T(8,128)(2,1)S(1)} %get-tuple-element.56), channel_id=1, source_target_pairs={{0,1},{1,0},{2,3},{3,2},{4,5},{5,4},{6,7},{7,6},{8,9},{9,8},{10,11... | collective-permute-start | bytes 393224 | tf_op jit(solution)/shard_map/ppermute | solution.py:211
  51.7 31.3 %collective-permute-start.1 = (bf16[1,128,512]{2,1,0:T(8,128)(2,1)S(1)}, bf16[1,128,512]{2,1,0:T(8,128)(2,1)S(1)}, u32[]{:S(2)}, u32[]{:S(2)}) collective-permute-start(bf16[1,128,512]{2,1,0:T(8,128)(2,1)S(1)} %get-tuple-element.57), channel_id=1, source_target_pairs={{0,2},{1,3},{2,0},{3,1},{4,6},{5,7},{6,4},{7,5},{8,10},{9,11},{10,... | collective-permute-start | bytes 393224 | tf_op jit(solution)/shard_map/ppermute | solution.py:211
  53.3 31.2 %collective-permute-start.2 = (bf16[1,128,512]{2,1,0:T(8,128)(2,1)S(1)}, bf16[1,128,512]{2,1,0:T(8,128)(2,1)S(1)}, u32[]{:S(2)}, u32[]{:S(2)}) collective-permute-start(bf16[1,128,512]{2,1,0:T(8,128)(2,1)S(1)} %get-tuple-element.58), channel_id=1, source_target_pairs={{0,3},{1,2},{2,1},{3,0},{4,7},{5,6},{6,5},{7,4},{8,11},{9,10},{10,... | collective-permute-start | bytes 393224 | tf_op jit(solution)/shard_map/ppermute | solution.py:211
  73.1 25.9 %collective-permute-start.18 = (bf16[528,512]{1,0:T(8,128)(2,1)S(1)}, bf16[528,512]{1,0:T(8,128)(2,1)S(1)}, u32[]{:S(2)}, u32[]{:S(2)}) collective-permute-start(bf16[528,512]{1,0:T(8,128)(2,1)S(1)} %collective-permute-done.13.refs_1_), channel_id=1, source_target_pairs={{0,8},{8,16},{16,24},{24,28},{28,20},{20,12},{12,4},{4,0},{1,9},{9... | collective-permute-start | bytes 1622024 | tf_op jit(solution)/shard_map/ppermute | solution.py:225
  99.0 20.5 %collective-permute-start.17 = (bf16[2,128,512]{2,1,0:T(8,128)(2,1)S(1)}, bf16[2,128,512]{2,1,0:T(8,128)(2,1)}, u32[]{:S(2)}, u32[]{:S(2)}) collective-permute-start(bf16[2,128,512]{2,1,0:T(8,128)(2,1)S(1)} %get-tuple-element.70), channel_id=1, source_target_pairs={{0,3},{1,2},{2,1},{3,0},{4,7},{5,6},{6,5},{7,4},{8,11},{9,10},{10,... | collective-permute-start | bytes 786440 | tf_op jit(solution)/shard_map/ppermute | solution.py:211
  174.0 28.2 %collective-permute-start.37 = (bf16[512,512]{1,0:T(8,128)(2,1)S(1)}, bf16[512,512]{1,0:T(8,128)(2,1)S(1)}, u32[]{:S(2)}, u32[]{:S(2)}) collective-permute-start(bf16[512,512]{1,0:T(8,128)(2,1)S(1)} %combine_rows.5), channel_id=1, source_target_pairs={{0,8},{8,16},{16,24},{24,28},{28,20},{20,12},{12,4},{4,0},{1,9},{9... | collective-permute-start | bytes 1572872 | tf_op jit(solution)/shard_map/ppermute | solution.py:341
  176.4 30.6 %collective-permute-start.45 = (bf16[512,512]{1,0:T(8,128)(2,1)S(1)}, bf16[512,512]{1,0:T(8,128)(2,1)S(1)}, u32[]{:S(2)}, u32[]{:S(2)}) collective-permute-start(bf16[512,512]{1,0:T(8,128)(2,1)S(1)} %copy-done.2), channel_id=1, source_target_pairs={{0,2},{1,3},{2,0},{3,1},{4,6},{5,7},{6,4},{7,5},{8,10},{9,11},{10,... | collective-permute-start | bytes 1572872 | tf_op jit(solution)/shard_map/ppermute | solution.py:211
  178.3 18.6 %collective-permute-start.32 = (bf16[2,128,512]{2,1,0:T(8,128)(2,1)}, bf16[2,128,512]{2,1,0:T(8,128)(2,1)S(1)}, u32[]{:S(2)}, u32[]{:S(2)}) collective-permute-start(bf16[2,128,512]{2,1,0:T(8,128)(2,1)} %get-tuple-element.89), channel_id=1, source_target_pairs={{0,2},{1,3},{2,0},{3,1},{4,6},{5,7},{6,4},{7,5},{8,10},{9,11},{10,... | collective-permute-start | bytes 786440 | tf_op jit(solution)/shard_map/ppermute | solution.py:211
  179.0 23.2 %collective-permute-start.33 = (bf16[2,128,512]{2,1,0:T(8,128)(2,1)}, bf16[2,128,512]{2,1,0:T(8,128)(2,1)S(1)}, u32[]{:S(2)}, u32[]{:S(2)}) collective-permute-start(bf16[2,128,512]{2,1,0:T(8,128)(2,1)} %get-tuple-element.90), channel_id=1, source_target_pairs={{0,3},{1,2},{2,1},{3,0},{4,7},{5,6},{6,5},{7,4},{8,11},{9,10},{10,... | collective-permute-start | bytes 786440 | tf_op jit(solution)/shard_map/ppermute | solution.py:211
  179.7 27.4 %collective-permute-start.28 = (bf16[2,128,512]{2,1,0:T(8,128)(2,1)}, bf16[2,128,512]{2,1,0:T(8,128)(2,1)S(1)}, u32[]{:S(2)}, u32[]{:S(2)}) collective-permute-start(bf16[2,128,512]{2,1,0:T(8,128)(2,1)} %get-tuple-element.84), channel_id=1, source_target_pairs={{0,1},{1,0},{2,3},{3,2},{4,5},{5,4},{6,7},{7,6},{8,9},{9,8},{10,11... | collective-permute-start | bytes 786440 | tf_op jit(solution)/shard_map/ppermute | solution.py:211
  216.4 24.7 %collective-permute-start.25 = (bf16[2,128,512]{2,1,0:T(8,128)(2,1)}, bf16[2,128,512]{2,1,0:T(8,128)(2,1)}, u32[]{:S(2)}, u32[]{:S(2)}) collective-permute-start(bf16[2,128,512]{2,1,0:T(8,128)(2,1)} %get-tuple-element.80), channel_id=1, source_target_pairs={{0,1},{1,0},{2,3},{3,2},{4,5},{5,4},{6,7},{7,6},{8,9},{9,8},{10,11... | collective-permute-start | bytes 786440 | tf_op jit(solution)/shard_map/ppermute | solution.py:211
  222.8 30.7 %collective-permute-start.40 = (bf16[512,512]{1,0:T(8,128)(2,1)}, bf16[512,512]{1,0:T(8,128)(2,1)S(1)}, u32[]{:S(2)}, u32[]{:S(2)}) collective-permute-start(bf16[512,512]{1,0:T(8,128)(2,1)} %get-tuple-element.97), channel_id=1, source_target_pairs={{8,0},{16,8},{24,16},{28,24},{20,28},{12,20},{4,12},{0,4},{9,1},{1... | collective-permute-start | bytes 1572872 | tf_op jit(solution)/shard_map/ppermute | solution.py:343
  223.6 29.9 %collective-permute-start.41 = (bf16[512,512]{1,0:T(8,128)(2,1)}, bf16[512,512]{1,0:T(8,128)(2,1)S(1)}, u32[]{:S(2)}, u32[]{:S(2)}) collective-permute-start(bf16[512,512]{1,0:T(8,128)(2,1)} %get-tuple-element.98), channel_id=1, source_target_pairs={{0,8},{8,16},{16,24},{24,28},{28,20},{20,12},{12,4},{4,0},{1,9},{9... | collective-permute-start | bytes 1572872 | tf_op jit(solution)/shard_map/ppermute | solution.py:344
  239.5 18.2 %collective-permute-start.48 = (bf16[512,512]{1,0:T(8,128)(2,1)S(1)}, bf16[512,512]{1,0:T(8,128)(2,1)S(1)}, u32[]{:S(2)}, u32[]{:S(2)}) collective-permute-start(bf16[512,512]{1,0:T(8,128)(2,1)S(1)} %get-tuple-element.104), channel_id=1, source_target_pairs={{0,1},{1,0},{2,3},{3,2},{4,5},{5,4},{6,7},{7,6},{8,9},{9,8},{10,11... | collective-permute-start | bytes 1572872 | tf_op jit(solution)/shard_map/ppermute | solution.py:211
  255.7 20.4 %collective-permute-start.42 = (bf16[512,512]{1,0:T(8,128)(2,1)S(1)}, bf16[512,512]{1,0:T(8,128)(2,1)S(1)}, u32[]{:S(2)}, u32[]{:S(2)}) collective-permute-start(bf16[512,512]{1,0:T(8,128)(2,1)S(1)} %get-tuple-element.99), channel_id=1, source_target_pairs={{8,0},{16,8},{24,16},{28,24},{20,28},{12,20},{4,12},{0,4},{9,1},{1... | collective-permute-start | bytes 1572872 | tf_op jit(solution)/shard_map/ppermute | solution.py:343
  256.6 19.5 %collective-permute-start.43 = (bf16[512,512]{1,0:T(8,128)(2,1)S(1)}, bf16[512,512]{1,0:T(8,128)(2,1)S(1)}, u32[]{:S(2)}, u32[]{:S(2)}) collective-permute-start(bf16[512,512]{1,0:T(8,128)(2,1)S(1)} %get-tuple-element.100), channel_id=1, source_target_pairs={{0,8},{8,16},{16,24},{24,28},{28,20},{20,12},{12,4},{4,0},{1,9},{9... | collective-permute-start | bytes 1572872 | tf_op jit(solution)/shard_map/ppermute | solution.py:344
  257.9 18.2 %collective-permute-start.49 = (bf16[512,512]{1,0:T(8,128)(2,1)S(1)}, bf16[512,512]{1,0:T(8,128)(2,1)S(1)}, u32[]{:S(2)}, u32[]{:S(2)}) collective-permute-start(bf16[512,512]{1,0:T(8,128)(2,1)S(1)} %add_convert_fusion), channel_id=1, source_target_pairs={{0,2},{1,3},{2,0},{3,1},{4,6},{5,7},{6,4},{7,5},{8,10},{9,11},{10,... | collective-permute-start | bytes 1572872 | tf_op jit(solution)/shard_map/ppermute | solution.py:211
  (66 other events, 762.2 us)
Sparse Core Ops, SparseCore 0:
  9.4 85.4 all-gather.4
  97.1 106.9 all-gather.2

commit v2 on v0

v2 whole, which is shorter than its diff:
```python
import jax
import jax.numpy as jnp
from jax import lax
from jax.experimental import pallas as pl
from jax.experimental.pallas import tpu as pltpu
from jax.sharding import PartitionSpec as P

FF = 1408
CAP = 64
META_ROWS = 16
BF16 = jnp.bfloat16
F32 = jnp.float32

epsilon = 1e-06


def block_of(shape, first=0):
    return pl.BlockSpec(shape, lambda *_: (first,) + (0,) * (len(shape) - 1))


LONG = pl.CostEstimate(flops=40_000_000_000, bytes_accessed=100_000_000, transcendentals=0)


def in_hbm(values):
    return [pltpu.with_memory_space_constraint(v, pltpu.HBM) for v in values]


anywhere = pl.BlockSpec(memory_space=pl.ANY)
smem = pl.BlockSpec(memory_space=pltpu.SMEM)
LANES = 128


def ring_of(count):
    order = list(range(0, count, 2)) + list(range(1, count, 2))[::-1]
    right = [(order[p], order[(p + 1) % count]) for p in range(count)]
    left = [(b, a) for a, b in right]
    return right, left


def slot_ranks(meta, named, top_count):
    token_count = meta.shape[1]
    hit = jnp.zeros((named.shape[0], token_count), F32)
    for r in range(top_count):
        hit = hit + jnp.where(meta[r : r + 1, :] == named[:, :1], 1.0, 0.0)
    before = lax.broadcasted_iota(jnp.int32, (token_count, token_count), 0) < (
        lax.broadcasted_iota(jnp.int32, (token_count, token_count), 1)
    )
    rank = jnp.dot(hit.astype(BF16), jnp.where(before, 1.0, 0.0).astype(BF16), preferred_element_type=F32)
    return jnp.where(hit > 0.0, rank, -1.0)


def dispatch_kernel(forms, peers, held, top_count, *refs):
    named_ref = refs[0]
    blocks = len(forms)
    payloads = refs[1 : 1 + sum(forms)]
    metas = refs[1 + sum(forms) : -2 - peers]
    outs = refs[-2 - peers : -2]
    table, choose = refs[-2:]
    slices = peers * held
    token_count = choose.shape[1]
    first = 0
    for b in range(blocks):
        mine = payloads[first : first + forms[b]]
        first += forms[b]
        meta = (metas[b][...] if metas else mine[0][:META_ROWS]).astype(F32)
        skipped = META_ROWS * token_count // outs[0].shape[2]
        named = named_ref[...]
        ranks = slot_ranks(meta, named, top_count)
        weight = jnp.zeros((named.shape[0], token_count), F32)
        for r in range(top_count):
            weight = weight + jnp.where(
                meta[r : r + 1, :] == named[:, :1], meta[top_count + r : top_count + r + 1, :], 0.0
            )
        table[b, :slices] = ranks
        table[b, slices:] = weight
        slot = lax.broadcasted_iota(jnp.int32, (CAP, token_count), 0).astype(F32)
        for c in range(slices):
            choose[c * CAP : (c + 1) * CAP, :] = jnp.where(slot == ranks[c : c + 1, :], 1.0, 0.0).astype(BF16)
        column, rows = 0, 0.0
        for n, part in enumerate(mine):
            start = 0 if n else skipped
            count = part.shape[0] - start
            rows = rows + jnp.dot(
                choose[:, column : column + count], part[start:, :], preferred_element_type=F32
            )
            column += count
        rows = rows.astype(BF16)
        for k in range(peers):
            outs[k][b] = rows[k * held * CAP : (k + 1) * held * CAP, :]


def combine_kernel(blocks, split, peers, held, *refs):
    table = refs[0]
    results = refs[1 : 1 + peers * held]
    outs = refs[1 + peers * held : -2]
    choose, gathered = refs[-2:]
    slices = peers * held
    for b in range(blocks):
        ranks, weight = table[b, :slices], table[b, slices:]
        token_count = ranks.shape[1]
        half = token_count // 2
        slot = lax.broadcasted_iota(jnp.int32, (CAP, token_count), 0).astype(F32)
        for c in range(slices):
            gathered[c * CAP : (c + 1) * CAP, :] = results[c % held * peers + c // held][b]
            choose[c * CAP : (c + 1) * CAP, :] = jnp.where(
                slot == ranks[c : c + 1, :], weight[c : c + 1, :], 0.0
            ).astype(BF16)
        total = lax.dot_general(
            choose[...], gathered[...], (((0,), (0,)), ((), ())), preferred_element_type=F32
        ).astype(BF16)
        if split:
            outs[0][...] = total[:half]
            outs[1][...] = total[half:]
        else:
            outs[b][...] = total


def expert_kernel(sizes, targets, peers, units, features, order_ref, gain_ref, *refs):
    batches = len(sizes)
    parts = refs[: batches * peers]
    in_ref, out_ref = refs[batches * peers : batches * peers + 2]
    outs = refs[batches * peers + 2 : -3]
    ready, total, hidden = refs[-3:]
    step = pl.program_id(0)

    @pl.when(step == 0)
    def _():
        n = 0
        for g in range(batches):
            for b in range(sizes[g]):
                rows = [parts[g * peers + k][b].astype(F32) for k in range(peers)]
                squares = sum(jnp.sum(r * r, axis=1, keepdims=True) for r in rows)
                inverse_rms = lax.rsqrt(squares / features + epsilon)
                for k in range(peers):
                    ready[k, n * CAP : (n + 1) * CAP, :] = (rows[k] * inverse_rms * gain_ref[k]).astype(BF16)
                n += 1

    @pl.when(step < peers)
    def _():
        product = jnp.dot(ready[jnp.minimum(step, peers - 1)], in_ref[0], preferred_element_type=F32)

        @pl.when(step == 0)
        def _():
            total[...] = product

        @pl.when(step > 0)
        def _():
            total[...] = total[...] + product

    @pl.when(step == peers - 1)
    def _():
        gate = total[:, :units]
        hidden[...] = (gate / (1.0 + jnp.exp(-gate)) * total[:, units:]).astype(BF16)

    for k in range(peers):

        @pl.when(step == peers + k)
        def _(k=k):
            value = jnp.dot(hidden[...], out_ref[0], preferred_element_type=F32).astype(BF16)
            for n, (g, b) in enumerate(targets):
                outs[g * peers + k][b] = value[n * CAP : (n + 1) * CAP, :]


def shared_kernel(peers, features, order_ref, block_ref, gain_ref, *refs):
    parts = refs[:peers]
    *weights, ready, gates, ups, downs, sems = refs[peers:]
    outs = weights[-peers:]
    weights = weights[:-peers]
    blocks = downs.shape[0]
    depth = gates.shape[1] // blocks
    copies = []
    for n in range(blocks):
        start = pl.multiple_of(block_ref[n] * depth, depth)
        columns = (gates.at[:, pl.ds(start, depth)], ups.at[:, pl.ds(start, depth)], downs.at[block_ref[n]])
        for m, target in enumerate(columns):
            source = weights[n].at[m] if n < blocks - 1 or m < 2 else weights[blocks].at[0]
            copies.append(pltpu.make_async_copy(source, target, sems.at[3 * n + m]))
    for copy in copies:
        copy.start()
    rows = [part[...].astype(F32) for part in parts]
    squares = sum(jnp.sum(r * r, axis=1, keepdims=True) for r in rows)
    inverse_rms = lax.rsqrt(squares / features + epsilon)
    for k in range(peers):
        ready[order_ref[k]] = (rows[k] * inverse_rms * gain_ref[k]).astype(BF16)
    for copy in copies:
        copy.wait()
    width = ready.shape[2]
    gate, up = 0.0, 0.0
    across = (((1,), (1,)), ((), ()))
    for q in range(peers):
        columns = slice(q * width, (q + 1) * width)
        gate = gate + lax.dot_general(ready[q], gates[:, columns], across, preferred_element_type=F32)
        up = up + lax.dot_general(ready[q], ups[:, columns], across, preferred_element_type=F32)
    hidden = (gate / (1.0 + jnp.exp(-gate)) * up).astype(BF16)
    each = blocks // peers
    for k in range(peers):
        for m in range(each):
            outs[k][:, m * depth : (m + 1) * depth] = jnp.dot(
                hidden, downs[order_ref[k] * each + m], preferred_element_type=F32
            ).astype(BF16)


def on_device(
    tokens, norm_gain, expert_ids, gate_weights, shared_in, shared_out, expert_in, expert_out
):
    row_count = lax.axis_size("gx")
    peers = lax.axis_size("gy")
    row, column = lax.axis_index("gx"), lax.axis_index("gy")
    token_count, width = tokens.shape
    half = token_count // 2
    far = row_count // 2
    top_count = expert_ids.shape[1]
    features = norm_gain.shape[0]
    held = expert_in.shape[0]
    units = expert_out.shape[1]
    slice_count = FF // units
    slices = peers * held
    order = jnp.arange(peers, dtype=jnp.int32) ^ column
    gain = norm_gain.reshape(peers, 1, width)[order]
    slice_numbers = ((row * peers + order)[:, None] * held + jnp.arange(held, dtype=jnp.int32)).reshape(-1)
    named = jnp.broadcast_to((slice_numbers // slice_count).astype(F32)[:, None], (slices, LANES))

    right, left = ring_of(row_count)

    def to_peer(value, mask):
        return lax.ppermute(value, "gy", [(s, s ^ mask) for s in range(peers)])

    def call(kernel, outs, inputs, scratch, name, in_specs=None, scalars=(), limit=40, cost=None):
        return pl.pallas_call(
            kernel,
            grid=(1,),
            out_shape=[pltpu.HBM(shape, dtype) for shape, dtype in outs],
            in_specs=[smem] * len(scalars) + (in_specs or [block_of(v.shape) for v in inputs]),
            out_specs=[block_of(shape) for shape, _ in outs],
            scratch_shapes=scratch,
            compiler_params=pltpu.CompilerParams(vmem_limit_bytes=limit << 20),
            name=name,
            cost_estimate=cost,
        )(*scalars, *in_hbm(inputs))

    def after(values, *others):
        return lax.optimization_barrier((values, others))[0]

    meta = jnp.concatenate(
        [
            expert_ids.T.astype(BF16),
            gate_weights.T.astype(BF16),
            jnp.zeros((META_ROWS - 2 * top_count, token_count), BF16),
        ],
        axis=0,
    ).reshape(-1, width)
    meta_rows = meta.shape[0]
    payload = jnp.concatenate([meta, tokens], axis=0)

    sizes = [1] + [2] * (far - 1) + [1]
    batches = [[g] for g in range(far + 1)]

    parts, tables = {}, {}

    def dispatch(number, group_blocks):
        blocks = [block for g in batches[number] for block in group_blocks[g]]
        metas = [] if width == token_count else [
            block[0][:meta_rows].reshape(META_ROWS, token_count) for block in blocks
        ]
        *rows, tables[number] = call(
            lambda *refs: dispatch_kernel([len(block) for block in blocks], peers, held, top_count, *refs),
            [((len(blocks), held * CAP, width), BF16)] * peers
            + [((len(blocks), 2 * slices, token_count), F32)],
            [named] + [part for block in blocks for part in block] + metas,
            [pltpu.VMEM((slices * CAP, token_count), BF16)],
            "dispatch_rows",
            cost=LONG,
        )
        parts[number] = [rows[0]] + [to_peer(rows[k], k) for k in range(1, peers)]
        return rows[0]

    groups = {0: [(payload,)]}
    at_left, at_right = payload, payload
    sent = 0
    for step in range(1, far + 1):
        if step < far:
            at_left = lax.ppermute(at_left, "gx", right)
            at_right = lax.ppermute(at_right, "gx", left)
            arrived = [(at_left,), (at_right,)]
        else:
            cut = meta_rows + half
            arrived = [(lax.ppermute(at_left[:cut], "gx", right), lax.ppermute(at_right[cut:], "gx", left))]
        done = [parts[sent - 1]] if sent and step < far else []
        if sent < len(batches) and batches[sent][-1] < step:
            done.append(dispatch(sent, groups))
            sent += 1
        groups[step] = after(arrived, done)
        at_left, at_right = groups[step][0][0], groups[step][-1][-1]
    for number in range(sent, len(batches)):
        last_rows = dispatch(number, groups)

    ring_order = [a for a, _ in right]
    nearby = []
    for i in range(row_count):
        p = ring_order.index(i)
        steps = [0] + [d for s in range(1, far) for d in (-s, s)] + [-far]
        nearby.append([ring_order[(p + d) % row_count] for d in steps])
    block_rows = jnp.asarray(nearby, jnp.int32)[row]
    shared = jnp.concatenate([jnp.swapaxes(shared_in, 1, 2), shared_out[None]], axis=0)
    weights = {0: [shared]}

    def weights_step(step, start):
        left_one, right_one = start
        if step < far:
            weights[step] = [lax.ppermute(left_one, "gx", right), lax.ppermute(right_one, "gx", left)]
        else:
            weights[step] = [
                lax.ppermute(left_one[:2], "gx", right),
                lax.ppermute(right_one[2:], "gx", left),
            ]
        return weights[step]

    listed = list(range(far - 1, 0, -1)) + [far, 0]
    near_groups, far_groups = list(range(far - 2, 0, -1)) + [0], [far - 1, far]

    def places_of(batches_out):
        found = {}
        for number, batch in enumerate(batches_out):
            start = 0
            for g in batch:
                found[g] = (number, start)
                start += sizes[g]
        return found

    def experts(h, inputs, batches_out):
        found = places_of(batches_out)
        counts = [sizes[g] for g in listed]
        targets = [(found[g][0], found[g][1] + b) for g in listed for b in range(sizes[g])]
        outs = [(sum(sizes[g] for g in batch), CAP, width) for batch in batches_out for _ in range(peers)]
        return pl.pallas_call(
            lambda *refs: expert_kernel(counts, targets, peers, units, features, *refs),
            grid_spec=pltpu.PrefetchScalarGridSpec(
                num_scalar_prefetch=1,
                grid=(2 * peers,),
                in_specs=[block_of(gain.shape)]
                + [pl.BlockSpec((part.shape[0], CAP, width), lambda s, o: (0, h, 0)) for part in inputs]
                + [
                    pl.BlockSpec((1, width, 2 * units), lambda s, o: (h, o[jnp.minimum(s, peers - 1)], 0)),
                    pl.BlockSpec((1, units, width), lambda s, o: (h, 0, o[jnp.maximum(s - peers, 0)])),
                ],
                out_specs=[block_of(shape) for shape in outs],
                scratch_shapes=[
                    pltpu.VMEM((peers, row_count * CAP, width), BF16),
                    pltpu.VMEM((row_count * CAP, 2 * units), F32),
                    pltpu.VMEM((row_count * CAP, units), BF16),
                ],
            ),
            out_shape=[pltpu.HBM(shape, BF16) for shape in outs],
            compiler_params=pltpu.CompilerParams(vmem_limit_bytes=56 << 20),
            name="expert_slice",
            cost_estimate=LONG,
        )(order, *in_hbm([gain] + inputs + [expert_in, expert_out]))

    def back(values):
        return [values[0]] + [to_peer(values[k], k) for k in range(1, peers)]

    inputs = [part for g in listed for part in parts[g]]
    ahead = weights_step(1, after((shared, shared), groups[far]))
    inputs, ahead = after((inputs, ahead), last_rows)
    early, next_step = [], 2
    for h in range(held):
        if next_step <= far:
            ahead = weights_step(next_step, ahead)
            next_step += 1
        if h < held - 1:
            result = experts(h, inputs, [listed])
        else:
            result = experts(h, inputs, [far_groups, near_groups])
        result, inputs, early, ahead = after((result, inputs, early, ahead), None)
        if h < held - 1:
            early.append(back(result))
    late = [back(result[:peers]), back(result[peers:])]
    for step in range(next_step, far + 1):
        ahead = weights_step(step, ahead)
    early_places, late_places = places_of([listed]), places_of([far_groups, near_groups])

    pieces = {0: tokens}
    mask = peers // 2
    while mask:
        for k in list(pieces):
            pieces[k ^ mask] = to_peer(pieces[k], mask)
        mask //= 2
    shared_units, depth = shared_out.shape
    shared_parts = call(
        lambda *refs: shared_kernel(peers, features, *refs),
        [((token_count, width), BF16)] * peers,
        [gain] + [pieces[k] for k in range(peers)] + [w for step in range(far + 1) for w in weights[step]],
        [
            pltpu.VMEM((peers, token_count, width), BF16),
            pltpu.VMEM((shared_units, features), BF16),
            pltpu.VMEM((shared_units, features), BF16),
            pltpu.VMEM((row_count, shared_units, depth), BF16),
            pltpu.SemaphoreType.DMA((3 * row_count,)),
        ],
        "shared_experts",
        [block_of(gain.shape)] + [block_of(tokens.shape)] * peers + [anywhere] * (row_count + 1),
        [order, block_rows],
    )
    shared_parts = list(shared_parts)
    mask, last = 1, None
    while mask < peers:
        kept = range(0, peers, 2 * mask)
        arrived = {k: to_peer(shared_parts[k + mask], mask) for k in kept}
        if 2 * mask == peers:
            last = arrived[0]
        else:
            for k in kept:
                shared_parts[k] = (shared_parts[k].astype(F32) + arrived[k].astype(F32)).astype(BF16)
        mask *= 2

    def combine(g):
        size = sizes[g]
        number, place = late_places[g]
        sources = [(member, early_places[g][1]) for member in early] + [(late[number], place)]
        outs = [((half, width), BF16)] * 2 if g == far else [((token_count, width), BF16)] * size
        return call(
            lambda *refs: combine_kernel(size, g == far, peers, held, *refs),
            outs,
            [tables[g]] + [value for values, _ in sources for value in values],
            [pltpu.VMEM((slices * CAP, token_count), BF16), pltpu.VMEM((slices * CAP, width), BF16)],
            "combine_rows",
            [block_of(tables[g].shape)]
            + [block_of((size, CAP, width), start // size) for _, start in sources for _ in range(peers)],
        )

    def add(*values):
        return sum(v.astype(F32) for v in values).astype(BF16)

    top, bottom = combine(far)
    top, bottom = lax.ppermute(top, "gx", right), lax.ppermute(bottom, "gx", left)
    going_left, going_right = combine(far - 1)
    going_left = jnp.concatenate([going_left[:half], add(going_left[half:], bottom)])
    going_right = jnp.concatenate([add(going_right[:half], top), going_right[half:]])
    for g in range(far - 2, -1, -1):
        from_left, from_right = lax.ppermute(going_right, "gx", right), lax.ppermute(going_left, "gx", left)
        own = combine(g)
        if g:
            going_left, going_right = add(own[0], from_right), add(own[1], from_left)
    return add(own[0], from_left, from_right, shared_parts[0], last)


def solution(mesh):
    in_specs = (
        P("gx", "gy"),
        P(),
        P("gx", None),
        P("gx", None),
        P(None, "gx", "gy"),
        P("gy", "gx"),
        P(("gx", "gy"), None, None),
        P(("gx", "gy"), None, None),
    )
    out_specs = P("gx", "gy")
    return jax.shard_map(
        on_device, mesh=mesh, in_specs=in_specs, out_specs=out_specs, check_vma=False
    )
```

time: 473 us -> 226 us (0.48)
  waiting for transfers between devices: 292 us -> 79.3 us
  Pallas kernels: 0 us -> 79.7 us
  local copies, waits for them, and re-layouts: 76 us -> 8.66 us
  matrix products: 52.1 us -> 0 us
  starting transfers between devices: 12.3 us -> 48.7 us
  other arithmetic: 24.9 us -> 8.72 us
  between operations: 15.1 us -> 0.56 us
    all_to_all x2 -> x0, waiting for transfers between devices: 259 us -> none  [the longest x1 144 us: on_device(): lax.all_to_all(outgoing, 'gx', split_axis=0, concat_axis=0, tiled=True)]
    pallas_call x0 -> x13, Pallas kernels: none -> 79.7 us  [the longest x2 40.6 us: experts(): pl.pallas_call(lambda *refs: expert_kernel(counts, targets, peers, units,...]
    ppermute x0 -> x54, waiting for transfers between devices: none -> 79.3 us  [the longest x30 20.2 us: to_peer(): return lax.ppermute(value, 'gy', [(s, s ^ mask) for s in range(peers)])]
    gather x7 -> x2, local copies, waits for them, and re-layouts: 53.3 us -> 1.16 us  [on_device(): gain = norm_gain.reshape(peers, 1, width)[order]]
    dot_general x4 -> x0, matrix products: 52.1 us -> none  [the longest x1 21.6 us: on_device(): jnp.einsum('shcd,hdf->shcf', lax.all_to_all(outgoing, 'gx', split_axis=0,...]
    ppermute x0 -> x54, starting transfers between devices: none -> 48.7 us  [the longest x30 22.8 us: to_peer(): return lax.ppermute(value, 'gy', [(s, s ^ mask) for s in range(peers)])]
    reduce_scatter x1 -> x0, waiting for transfers between devices: 30.5 us -> none  [on_device(): lax.psum_scatter(group_sum.astype(jnp.bfloat16), 'gy', scatter_dimension=...]
    another operation x3 -> x0, other arithmetic: 18.8 us -> none
  transfers between devices with their start and end apart: 6 -> 54, of which waited for: 3 -> 24; matrix products, arithmetic and copies ran while one was open for 28% -> 5% of each run, Pallas kernels for 0% -> 35%
where the time goes in v2:
time: 226 us
  Pallas kernels  79.7 us (35%)
  waiting for transfers between devices  79.3 us (35%)
  starting transfers between devices  48.7 us (22%)
  other arithmetic  8.72 us (4%)
  local copies, waits for them, and re-layouts  8.66 us (4%)
    pallas_call x2, Pallas kernels, experts(): pl.pallas_call(lambda *refs: expert_kernel(counts, targets, peers, units,...  40.6 us
    pallas_call x11, Pallas kernels, call(): pl.pallas_call(kernel, grid=(1,), out_shape=[pltpu.HBM(shape, dtype) for...  39.1 us
    ppermute x30, starting transfers between devices, to_peer(): return lax.ppermute(value, 'gy', [(s, s ^ mask) for s in range(peers)])  22.8 us
    ppermute x30, waiting for transfers between devices, to_peer(): return lax.ppermute(value, 'gy', [(s, s ^ mask) for s in range(peers)])  20.2 us
    ppermute x3, waiting for transfers between devices, on_device(): lax.ppermute(going_right, 'gx', right)  19.1 us
    ppermute x3, waiting for transfers between devices, on_device(): at_left = lax.ppermute(at_left, 'gx', right)  15.9 us
    ppermute x3, waiting for transfers between devices, weights_step(): lax.ppermute(left_one, 'gx', right)  10.9 us
    ppermute x3, starting transfers between devices, on_device(): at_left = lax.ppermute(at_left, 'gx', right)  6.28 us
  transfers between devices with their start and end apart: 54, of which 24 were waited for; matrix products, arithmetic and copies ran while one was open for 5% of the time, Pallas kernels for 35%

profile of v2, /device:TPU:0, one launch (start us, length us, event | category | flops | bytes accessed | tf_op | source)
XLA Modules:
  0.0 225.6 jit_solution(7084502119368944894)
XLA Ops:
  2.8 3.1 %collective-permute-start = (bf16[528,512]{1,0:T(8,128)(2,1)S(1)}, bf16[528,512]{1,0:T(8,128)(2,1)S(1)}, u32[]{:S(2)}, u32[]{:S(2)}) collective-permute-start(bf16[528,512]{1,0:T(8,128)(2,1)S(1)} %pad_maximum_fusion.1.refs_1_), channel_id=1, source_target_pairs={{0,8},{8,16},{16,24},{24,28},{28,20},{20,12},{12,4},{4,0},{1,9},{9... | collective-permute-start | bytes 1622024 | tf_op jit(solution)/shard_map/ppermute | solution.py:282
  11.9 6.1 %collective-permute-done.refs_1_ = bf16[528,512]{1,0:T(8,128)(2,1)S(1)} collective-permute-done((bf16[528,512]{1,0:T(8,128)(2,1)S(1)}, bf16[528,512]{1,0:T(8,128)(2,1)S(1)}, u32[]{:S(2)}, u32[]{:S(2)}) %collective-permute-start) | collective-permute-done | bytes 540704 | tf_op jit(solution)/shard_map/ppermute | solution.py:282
  21.6 3.2 %dispatch_rows.6 = (bf16[2,128,512]{2,1,0:T(8,128)(2,1)}, bf16[2,128,512]{2,1,0:T(8,128)(2,1)}, bf16[2,128,512]{2,1,0:T(8,128)(2,1)}, bf16[2,128,512]{2,1,0:T(8,128)(2,1)}, f32[2,16,512]{2,1,0:T(8,128)}) custom-call(f32[8,128]{1,0:T(8,128)} %broadcast_in_dim.6.refs_0_, bf16[528,512]{1,0:T(8,128)(2,1)} %copy-done.35, bf16[528,512]{1,0:T(8,128)(2,1)} %copy-done.36), custom_call_target="tpu_custom_call" | custom-call | flops 40000000000 | bytes 100000000 | tf_op jit(solution)/shard_map/dispatch_rows/pallas_call | solution.py:229
  27.0 5.4 %collective-permute-done.2.refs_1_ = bf16[528,512]{1,0:T(8,128)(2,1)S(1)} collective-permute-done((bf16[528,512]{1,0:T(8,128)(2,1)S(1)}, bf16[528,512]{1,0:T(8,128)(2,1)S(1)}, u32[]{:S(2)}, u32[]{:S(2)}) %collective-permute-start.2) | collective-permute-done | bytes 540704 | tf_op jit(solution)/shard_map/ppermute | solution.py:282
  35.8 3.2 %dispatch_rows.7 = (bf16[2,128,512]{2,1,0:T(8,128)(2,1)}, bf16[2,128,512]{2,1,0:T(8,128)(2,1)}, bf16[2,128,512]{2,1,0:T(8,128)(2,1)}, bf16[2,128,512]{2,1,0:T(8,128)(2,1)}, f32[2,16,512]{2,1,0:T(8,128)}) custom-call(f32[8,128]{1,0:T(8,128)} %broadcast_in_dim.6.refs_0_, bf16[528,512]{1,0:T(8,128)(2,1)} %copy-done.37, bf16[528,512]{1,0:T(8,128)(2,1)} %copy-done.38), custom_call_target="tpu_custom_call" | custom-call | flops 40000000000 | bytes 100000000 | tf_op jit(solution)/shard_map/dispatch_rows/pallas_call | solution.py:229
  40.9 4.4 %collective-permute-done.7.refs_1_ = bf16[528,512]{1,0:T(8,128)(2,1)S(1)} collective-permute-done((bf16[528,512]{1,0:T(8,128)(2,1)S(1)}, bf16[528,512]{1,0:T(8,128)(2,1)S(1)}, u32[]{:S(2)}, u32[]{:S(2)}) %collective-permute-start.7) | collective-permute-done | bytes 540704 | tf_op jit(solution)/shard_map/ppermute | solution.py:282
  48.8 3.2 %dispatch_rows.8 = (bf16[2,128,512]{2,1,0:T(8,128)(2,1)}, bf16[2,128,512]{2,1,0:T(8,128)(2,1)}, bf16[2,128,512]{2,1,0:T(8,128)(2,1)}, bf16[2,128,512]{2,1,0:T(8,128)(2,1)}, f32[2,16,512]{2,1,0:T(8,128)}) custom-call(f32[8,128]{1,0:T(8,128)} %broadcast_in_dim.6.refs_0_, bf16[528,512]{1,0:T(8,128)(2,1)} %copy-done.31, bf16[528,512]{1,0:T(8,128)(2,1)} %copy-done.32), custom_call_target="tpu_custom_call" | custom-call | flops 40000000000 | bytes 100000000 | tf_op jit(solution)/shard_map/dispatch_rows/pallas_call | solution.py:229
  52.0 2.8 %collective-permute-done.19.refs_2_ = bf16[256,512]{1,0:T(8,128)(2,1)S(1)} collective-permute-done((bf16[256,512]{1,0:T(8,128)(2,1)S(1)}, bf16[256,512]{1,0:T(8,128)(2,1)S(1)}, u32[]{:S(2)}, u32[]{:S(2)}) %collective-permute-start.19) | collective-permute-done | bytes 262176 | tf_op jit(solution)/shard_map/ppermute | solution.py:287
  61.5 2.8 %collective-permute-done.13.refs_4_ = bf16[2,128,512]{2,1,0:T(8,128)(2,1)S(1)} collective-permute-done((bf16[2,128,512]{2,1,0:T(8,128)(2,1)}, bf16[2,128,512]{2,1,0:T(8,128)(2,1)S(1)}, u32[]{:S(2)}, u32[]{:S(2)}) %collective-permute-start.13) | collective-permute-done | bytes 262176 | tf_op jit(solution)/shard_map/ppermute | solution.py:226
  65.8 3.2 %collective-permute-done.14.refs_5_ = bf16[2,128,512]{2,1,0:T(8,128)(2,1)S(1)} collective-permute-done((bf16[2,128,512]{2,1,0:T(8,128)(2,1)}, bf16[2,128,512]{2,1,0:T(8,128)(2,1)S(1)}, u32[]{:S(2)}, u32[]{:S(2)}) %collective-permute-start.14) | collective-permute-done | bytes 262176 | tf_op jit(solution)/shard_map/ppermute | solution.py:226
  74.7 8.3 %collective-permute-done.23.refs_8_ = bf16[3,704,256]{2,1,0:T(8,128)(2,1)S(1)} collective-permute-done((bf16[3,704,256]{2,1,0:T(8,128)(2,1)S(1)}, bf16[3,704,256]{2,1,0:T(8,128)(2,1)S(1)}, u32[]{:S(2)}, u32[]{:S(2)}) %collective-permute-start.23) | collective-permute-done | bytes 1081376 | tf_op jit(solution)/shard_map/ppermute | solution.py:310
  85.9 20.3 %expert_slice.2 = (bf16[8,64,512]{2,1,0:T(8,128)(2,1)}, bf16[8,64,512]{2,1,0:T(8,128)(2,1)}, bf16[8,64,512]{2,1,0:T(8,128)(2,1)}, bf16[8,64,512]{2,1,0:T(8,128)(2,1)}) custom-call(s32[4]{0:T(128)} %iota_xor_fusion.refs_0_, f32[4,1,512]{2,1,0:T(1,128)} %reshape.41.refs_1_.refs_2_, bf16[2,128,512]{2,1,0:T(8,128)(2,1)} %get-tuple-element.183.refs_2_, ...), custom_call_target="tpu_custom_call" | custom-call | flops 40000000000 | bytes 100000000 | tf_op jit(solution)/shard_map/expert_slice/pallas_call | solution.py:335
  106.2 2.7 %collective-permute-done.25.refs_10_ = bf16[3,704,256]{2,1,0:T(8,128)(2,1)S(1)} collective-permute-done((bf16[3,704,256]{2,1,0:T(8,128)(2,1)S(1)}, bf16[3,704,256]{2,1,0:T(8,128)(2,1)S(1)}, u32[]{:S(2)}, u32[]{:S(2)}) %collective-permute-start.25) | collective-permute-done | bytes 1081376 | tf_op jit(solution)/shard_map/ppermute | solution.py:310
  113.2 20.3 %expert_slice.3 = (bf16[3,64,512]{2,1,0:T(8,128)(2,1)}, bf16[3,64,512]{2,1,0:T(8,128)(2,1)}, bf16[3,64,512]{2,1,0:T(8,128)(2,1)}, bf16[3,64,512]{2,1,0:T(8,128)(...) custom-call(s32[4]{0:T(128)} %iota_xor_fusion.refs_0_, ...), custom_call_target="tpu_custom_call" | custom-call | flops 40000000000 | bytes 100000000 | tf_op jit(solution)/shard_map/expert_slice/pallas_call | solution.py:335
  133.6 3.1 %collective-permute-done.29.refs_4_ = bf16[8,64,512]{2,1,0:T(8,128)(2,1)S(1)} collective-permute-done((bf16[8,64,512]{2,1,0:T(8,128)(2,1)}, bf16[8,64,512]{2,1,0:T(8,128)(2,1)S(1)}, u32[]{:S(2)}, u32[]{:S(2)}) %collective-permute-start.29) | collective-permute-done | bytes 524320 | tf_op jit(solution)/shard_map/ppermute | solution.py:226
  140.2 4.8 %collective-permute-done.36.refs_7_ = bf16[3,64,512]{2,1,0:T(8,128)(2,1)S(1)} collective-permute-done((bf16[3,64,512]{2,1,0:T(8,128)(2,1)}, bf16[3,64,512]{2,1,0:T(8,128)(2,1)S(1)}, u32[]{:S(2)}, u32[]{:S(2)}) %collective-permute-start.36) | collective-permute-done | bytes 196640 | tf_op jit(solution)/shard_map/ppermute | solution.py:226
  145.0 3.3 %collective-permute-done.37.refs_8_ = bf16[3,64,512]{2,1,0:T(8,128)(2,1)S(1)} collective-permute-done((bf16[3,64,512]{2,1,0:T(8,128)(2,1)}, bf16[3,64,512]{2,1,0:T(8,128)(2,1)S(1)}, u32[]{:S(2)}, u32[]{:S(2)}) %collective-permute-start.37) | collective-permute-done | bytes 196640 | tf_op jit(solution)/shard_map/ppermute | solution.py:226
  155.7 2.9 %combine_rows.8 = (bf16[512,512]{1,0:T(8,128)(2,1)}, bf16[512,512]{1,0:T(8,128)(2,1)}) custom-call(f32[2,16,512]{2,1,0:T(8,128)} %get-tuple-element.229.refs_0_, bf16[8,64,512]{2,1,0:T(8,128)(2,1)} %get-tuple-element.217.refs_1_, bf16[8,64,512]{2,1,0:T(8,128)(2,1)} %copy-done.1, bf16[8,64,512]{2,1,0:T(8,128)(2,1)} %copy-done.2, ...), custom_call_target="tpu_custom_call" | custom-call | tf_op jit(solution)/shard_map/combine_rows/pallas_call | solution.py:229
  165.1 4.0 %collective-permute-done.42 = bf16[256,512]{1,0:T(8,128)(2,1)S(1)} collective-permute-done((bf16[256,512]{1,0:T(8,128)(2,1)S(1)}, bf16[256,512]{1,0:T(8,128)(2,1)S(1)}, u32[]{:S(2)}, u32[]{:S(2)}) %collective-permute-start.42) | collective-permute-done | bytes 262176 | tf_op jit(solution)/shard_map/ppermute | solution.py:435
  175.5 2.8 %combine_rows.7 = (bf16[512,512]{1,0:T(8,128)(2,1)}, bf16[512,512]{1,0:T(8,128)(2,1)}) custom-call(f32[2,16,512]{2,1,0:T(8,128)} %get-tuple-element.227.refs_0_, bf16[8,64,512]{2,1,0:T(8,128)(2,1)} %get-tuple-element.217.refs_1_, bf16[8,64,512]{2,1,0:T(8,128)(2,1)} %copy-done.1, bf16[8,64,512]{2,1,0:T(8,128)(2,1)} %copy-done.2, ...), custom_call_target="tpu_custom_call" | custom-call | tf_op jit(solution)/shard_map/combine_rows/pallas_call | solution.py:229
  178.3 2.9 %combine_rows.6 = (bf16[512,512]{1,0:T(8,128)(2,1)}, bf16[512,512]{1,0:T(8,128)(2,1)}) custom-call(f32[2,16,512]{2,1,0:T(8,128)} %get-tuple-element.225.refs_0_, bf16[8,64,512]{2,1,0:T(8,128)(2,1)} %get-tuple-element.217.refs_1_, bf16[8,64,512]{2,1,0:T(8,128)(2,1)} %copy-done.1, bf16[8,64,512]{2,1,0:T(8,128)(2,1)} %copy-done.2, ...), custom_call_target="tpu_custom_call" | custom-call | tf_op jit(solution)/shard_map/combine_rows/pallas_call | solution.py:229
  182.9 11.2 %shared_experts.1 = (bf16[512,512]{1,0:T(8,128)(2,1)}, bf16[512,512]{1,0:T(8,128)(2,1)}, bf16[512,512]{1,0:T(8,128)(2,1)}, bf16[512,512]{1,0:T(8,128)(2,1)}) custom-call(s32[4]{0:T(128)S(1)} %copy-done, s32[8]{0:T(128)S(1)} %dynamic-slice_bitcast_fusion.refs_1_, f32[4,1,512]{2,1,0:T(1,128)} %reshape.41.refs_1_.refs_2_, bf16[512,512]{1,0:T(8,128)(2,1)} %refs_3_.1, ...), custom_call_target="tpu_custom_call" | custom-call | tf_op jit(solution)/shard_map/shared_experts/pallas_call | solution.py:229
  199.0 10.2 %collective-permute-done.40 = bf16[512,512]{1,0:T(8,128)(2,1)S(1)} collective-permute-done((bf16[512,512]{1,0:T(8,128)(2,1)S(1)}, bf16[512,512]{1,0:T(8,128)(2,1)S(1)}, u32[]{:S(2)}, u32[]{:S(2)}) %collective-permute-start.40) | collective-permute-done | bytes 524320 | tf_op jit(solution)/shard_map/ppermute | solution.py:440
  214.1 8.9 %collective-permute-done.41 = bf16[512,512]{1,0:T(8,128)(2,1)S(1)} collective-permute-done((bf16[512,512]{1,0:T(8,128)(2,1)S(1)}, bf16[512,512]{1,0:T(8,128)(2,1)S(1)}, u32[]{:S(2)}, u32[]{:S(2)}) %collective-permute-start.41) | collective-permute-done | bytes 524320 | tf_op jit(solution)/shard_map/ppermute | solution.py:440
  (250 shorter events, 82.0 us)
Async XLA Ops:
  2.8 15.3 %collective-permute-start = (bf16[528,512]{1,0:T(8,128)(2,1)S(1)}, bf16[528,512]{1,0:T(8,128)(2,1)S(1)}, u32[]{:S(2)}, u32[]{:S(2)}) collective-permute-start(bf16[528,512]{1,0:T(8,128)(2,1)S(1)} %pad_maximum_fusion.1.refs_1_), channel_id=1, source_target_pairs={{0,8},{8,16},{16,24},{24,28},{28,20},{20,12},{12,4},{4,0},{1,9},{9... | collective-permute-start | bytes 1622024 | tf_op jit(solution)/shard_map/ppermute | solution.py:282
  9.2 15.6 %collective-permute-start.4 = (bf16[1,128,512]{2,1,0:T(8,128)(2,1)}, bf16[1,128,512]{2,1,0:T(8,128)(2,1)S(1)}, u32[]{:S(2)}, u32[]{:S(2)}) collective-permute-start(bf16[1,128,512]{2,1,0:T(8,128)(2,1)} %get-tuple-element.130), channel_id=1, source_target_pairs={{0,1},{1,0},{2,3},{3,2},{4,5},{5,4},{6,7},{7,6},{8,9},{9,8},{10,11... | collective-permute-start | bytes 393224 | tf_op jit(solution)/shard_map/ppermute | solution.py:226
  9.2 17.2 %collective-permute-start.5 = (bf16[1,128,512]{2,1,0:T(8,128)(2,1)}, bf16[1,128,512]{2,1,0:T(8,128)(2,1)S(1)}, u32[]{:S(2)}, u32[]{:S(2)}) collective-permute-start(bf16[1,128,512]{2,1,0:T(8,128)(2,1)} %get-tuple-element.131), channel_id=1, source_target_pairs={{0,2},{1,3},{2,0},{3,1},{4,6},{5,7},{6,4},{7,5},{8,10},{9,11},{10,... | collective-permute-start | bytes 393224 | tf_op jit(solution)/shard_map/ppermute | solution.py:226
  11.1 15.2 %collective-permute-start.6 = (bf16[1,128,512]{2,1,0:T(8,128)(2,1)}, bf16[1,128,512]{2,1,0:T(8,128)(2,1)S(1)}, u32[]{:S(2)}, u32[]{:S(2)}) collective-permute-start(bf16[1,128,512]{2,1,0:T(8,128)(2,1)} %get-tuple-element.132), channel_id=1, source_target_pairs={{0,3},{1,2},{2,1},{3,0},{4,7},{5,6},{6,5},{7,4},{8,11},{9,10},{10,... | collective-permute-start | bytes 393224 | tf_op jit(solution)/shard_map/ppermute | solution.py:226
  39.0 17.5 %collective-permute-start.15 = (bf16[2,128,512]{2,1,0:T(8,128)(2,1)}, bf16[2,128,512]{2,1,0:T(8,128)(2,1)S(1)}, u32[]{:S(2)}, u32[]{:S(2)}) collective-permute-start(bf16[2,128,512]{2,1,0:T(8,128)(2,1)} %get-tuple-element.146), channel_id=1, source_target_pairs={{0,1},{1,0},{2,3},{3,2},{4,5},{5,4},{6,7},{7,6},{8,9},{9,8},{10,11... | collective-permute-start | bytes 786440 | tf_op jit(solution)/shard_map/ppermute | solution.py:226
  39.1 17.8 %collective-permute-start.16 = (bf16[2,128,512]{2,1,0:T(8,128)(2,1)}, bf16[2,128,512]{2,1,0:T(8,128)(2,1)S(1)}, u32[]{:S(2)}, u32[]{:S(2)}) collective-permute-start(bf16[2,128,512]{2,1,0:T(8,128)(2,1)} %get-tuple-element.147), channel_id=1, source_target_pairs={{0,2},{1,3},{2,0},{3,1},{4,6},{5,7},{6,4},{7,5},{8,10},{9,11},{10,... | collective-permute-start | bytes 786440 | tf_op jit(solution)/shard_map/ppermute | solution.py:226
  40.6 17.2 %collective-permute-start.17 = (bf16[2,128,512]{2,1,0:T(8,128)(2,1)}, bf16[2,128,512]{2,1,0:T(8,128)(2,1)S(1)}, u32[]{:S(2)}, u32[]{:S(2)}) collective-permute-start(bf16[2,128,512]{2,1,0:T(8,128)(2,1)} %get-tuple-element.148), channel_id=1, source_target_pairs={{0,3},{1,2},{2,1},{3,0},{4,7},{5,6},{6,5},{7,4},{8,11},{9,10},{10,... | collective-permute-start | bytes 786440 | tf_op jit(solution)/shard_map/ppermute | solution.py:226
  56.9 26.1 %collective-permute-start.23 = (bf16[3,704,256]{2,1,0:T(8,128)(2,1)S(1)}, bf16[3,704,256]{2,1,0:T(8,128)(2,1)S(1)}, u32[]{:S(2)}, u32[]{:S(2)}) collective-permute-start(bf16[3,704,256]{2,1,0:T(8,128)(2,1)S(1)} %pad_maximum_fusion.refs_7_), channel_id=1, source_target_pairs={{0,8},{8,16},{16,24},{24,28},{28,20},{20,12},{12,4},{4,0},{1,9},{9... | collective-permute-start | bytes 3244040 | tf_op jit(solution)/shard_map/ppermute | solution.py:310
  57.8 26.0 %collective-permute-start.24 = (bf16[3,704,256]{2,1,0:T(8,128)(2,1)S(1)}, bf16[3,704,256]{2,1,0:T(8,128)(2,1)}, u32[]{:S(2)}, u32[]{:S(2)}) collective-permute-start(bf16[3,704,256]{2,1,0:T(8,128)(2,1)S(1)} %pad_maximum_fusion.refs_7_), channel_id=1, source_target_pairs={{8,0},{16,8},{24,16},{28,24},{20,28},{12,20},{4,12},{0,4},{9,1},{1... | collective-permute-start | bytes 3244040 | tf_op jit(solution)/shard_map/ppermute | solution.py:310
  83.8 25.0 %collective-permute-start.25 = (bf16[3,704,256]{2,1,0:T(8,128)(2,1)S(1)}, bf16[3,704,256]{2,1,0:T(8,128)(2,1)S(1)}, u32[]{:S(2)}, u32[]{:S(2)}) collective-permute-start(bf16[3,704,256]{2,1,0:T(8,128)(2,1)S(1)} %collective-permute-done.23.refs_8_), channel_id=1, source_target_pairs={{0,8},{8,16},{16,24},{24,28},{28,20},{20,12},{12,4},{4,0},{1,9},{9... | collective-permute-start | bytes 3244040 | tf_op jit(solution)/shard_map/ppermute | solution.py:310
  84.4 24.9 %collective-permute-start.26 = (bf16[3,704,256]{2,1,0:T(8,128)(2,1)}, bf16[3,704,256]{2,1,0:T(8,128)(2,1)S(1)}, u32[]{:S(2)}, u32[]{:S(2)}) collective-permute-start(bf16[3,704,256]{2,1,0:T(8,128)(2,1)} %collective-permute-done.24.refs_9_), channel_id=1, source_target_pairs={{8,0},{16,8},{24,16},{28,24},{20,28},{12,20},{4,12},{0,4},{9,1},{1... | collective-permute-start | bytes 3244040 | tf_op jit(solution)/shard_map/ppermute | solution.py:310
  109.4 27.4 %collective-permute-start.30 = (bf16[3,704,256]{2,1,0:T(8,128)(2,1)S(1)}, bf16[3,704,256]{2,1,0:T(8,128)(2,1)S(1)}, u32[]{:S(2)}, u32[]{:S(2)}) collective-permute-start(bf16[3,704,256]{2,1,0:T(8,128)(2,1)S(1)} %collective-permute-done.25.refs_10_), channel_id=1, source_target_pairs={{0,8},{8,16},{16,24},{24,28},{28,20},{20,12},{12,4},{4,0},{1,9},{9... | collective-permute-start | bytes 3244040 | tf_op jit(solution)/shard_map/ppermute | solution.py:310
  109.9 26.9 %collective-permute-start.31 = (bf16[3,704,256]{2,1,0:T(8,128)(2,1)S(1)}, bf16[3,704,256]{2,1,0:T(8,128)(2,1)S(1)}, u32[]{:S(2)}, u32[]{:S(2)}) collective-permute-start(bf16[3,704,256]{2,1,0:T(8,128)(2,1)S(1)} %collective-permute-done.26.refs_11_), channel_id=1, source_target_pairs={{8,0},{16,8},{24,16},{28,24},{20,28},{12,20},{4,12},{0,4},{9,1},{1... | collective-permute-start | bytes 3244040 | tf_op jit(solution)/shard_map/ppermute | solution.py:310
  111.4 22.2 %collective-permute-start.27 = (bf16[8,64,512]{2,1,0:T(8,128)(2,1)}, bf16[8,64,512]{2,1,0:T(8,128)(2,1)S(1)}, u32[]{:S(2)}, u32[]{:S(2)}) collective-permute-start(bf16[8,64,512]{2,1,0:T(8,128)(2,1)} %get-tuple-element.212), channel_id=1, source_target_pairs={{0,1},{1,0},{2,3},{3,2},{4,5},{5,4},{6,7},{7,6},{8,9},{9,8},{10,11... | collective-permute-start | bytes 1572872 | tf_op jit(solution)/shard_map/ppermute | solution.py:226
  111.4 22.2 %collective-permute-start.28 = (bf16[8,64,512]{2,1,0:T(8,128)(2,1)}, bf16[8,64,512]{2,1,0:T(8,128)(2,1)S(1)}, u32[]{:S(2)}, u32[]{:S(2)}) collective-permute-start(bf16[8,64,512]{2,1,0:T(8,128)(2,1)} %get-tuple-element.213), channel_id=1, source_target_pairs={{0,2},{1,3},{2,0},{3,1},{4,6},{5,7},{6,4},{7,5},{8,10},{9,11},{10,... | collective-permute-start | bytes 1572872 | tf_op jit(solution)/shard_map/ppermute | solution.py:226
  112.9 23.9 %collective-permute-start.29 = (bf16[8,64,512]{2,1,0:T(8,128)(2,1)}, bf16[8,64,512]{2,1,0:T(8,128)(2,1)S(1)}, u32[]{:S(2)}, u32[]{:S(2)}) collective-permute-start(bf16[8,64,512]{2,1,0:T(8,128)(2,1)} %get-tuple-element.214), channel_id=1, source_target_pairs={{0,3},{1,2},{2,1},{3,0},{4,7},{5,6},{6,5},{7,4},{8,11},{9,10},{10,... | collective-permute-start | bytes 1572872 | tf_op jit(solution)/shard_map/ppermute | solution.py:226
  138.7 23.6 %collective-permute-start.47 = (bf16[512,512]{1,0:T(8,128)(2,1)S(1)}, bf16[512,512]{1,0:T(8,128)(2,1)}, u32[]{:S(2)}, u32[]{:S(2)}) collective-permute-start(bf16[512,512]{1,0:T(8,128)(2,1)S(1)} %copy-done.9), channel_id=1, source_target_pairs={{0,2},{1,3},{2,0},{3,1},{4,6},{5,7},{6,4},{7,5},{8,10},{9,11},{10,... | collective-permute-start | bytes 1572872 | tf_op jit(solution)/shard_map/ppermute | solution.py:226
  152.5 17.1 %collective-permute-start.33 = (bf16[5,64,512]{2,1,0:T(8,128)(2,1)S(1)}, bf16[5,64,512]{2,1,0:T(8,128)(2,1)S(1)}, u32[]{:S(2)}, u32[]{:S(2)}) collective-permute-start(bf16[5,64,512]{2,1,0:T(8,128)(2,1)S(1)} %copy-done.40), channel_id=1, source_target_pairs={{0,2},{1,3},{2,0},{3,1},{4,6},{5,7},{6,4},{7,5},{8,10},{9,11},{10,... | collective-permute-start | bytes 983048 | tf_op jit(solution)/shard_map/ppermute | solution.py:226
  162.3 19.3 %collective-permute-start.49 = (bf16[2,704,256]{2,1,0:T(8,128)(2,1)}, bf16[2,704,256]{2,1,0:T(8,128)(2,1)S(1)}, u32[]{:S(2)}, u32[]{:S(2)}) collective-permute-start(bf16[2,704,256]{2,1,0:T(8,128)(2,1)} %slice.30), channel_id=1, source_target_pairs={{0,8},{8,16},{16,24},{24,28},{28,20},{20,12},{12,4},{4,0},{1,9},{9... | collective-permute-start | bytes 2162696 | tf_op jit(solution)/shard_map/ppermute | solution.py:313
  163.8 17.4 %collective-permute-start.48 = (bf16[512,512]{1,0:T(8,128)(2,1)}, bf16[512,512]{1,0:T(8,128)(2,1)S(1)}, u32[]{:S(2)}, u32[]{:S(2)}) collective-permute-start(bf16[512,512]{1,0:T(8,128)(2,1)} %collective-permute-done.47.refs_5_), channel_id=1, source_target_pairs={{0,1},{1,0},{2,3},{3,2},{4,5},{5,4},{6,7},{7,6},{8,9},{9,8},{10,11... | collective-permute-start | bytes 1572872 | tf_op jit(solution)/shard_map/ppermute | solution.py:226
  169.1 25.7 %collective-permute-start.39 = (bf16[512,512]{1,0:T(8,128)(2,1)}, bf16[512,512]{1,0:T(8,128)(2,1)S(1)}, u32[]{:S(2)}, u32[]{:S(2)}) collective-permute-start(bf16[512,512]{1,0:T(8,128)(2,1)} %pad_maximum_fusion.2), channel_id=1, source_target_pairs={{0,8},{8,16},{16,24},{24,28},{28,20},{20,12},{12,4},{4,0},{1,9},{9... | collective-permute-start | bytes 1572872 | tf_op jit(solution)/shard_map/ppermute | solution.py:440
  173.3 22.2 %collective-permute-start.43 = (bf16[512,512]{1,0:T(8,128)(2,1)}, bf16[512,512]{1,0:T(8,128)(2,1)S(1)}, u32[]{:S(2)}, u32[]{:S(2)}) collective-permute-start(bf16[512,512]{1,0:T(8,128)(2,1)} %pad_maximum_fusion.3), channel_id=1, source_target_pairs={{8,0},{16,8},{24,16},{28,24},{20,28},{12,20},{4,12},{0,4},{9,1},{1... | collective-permute-start | bytes 1572872 | tf_op jit(solution)/shard_map/ppermute | solution.py:440
  194.7 19.4 %collective-permute-start.51 = (bf16[512,512]{1,0:T(8,128)(2,1)}, bf16[512,512]{1,0:T(8,128)(2,1)S(1)}, u32[]{:S(2)}, u32[]{:S(2)}) collective-permute-start(bf16[512,512]{1,0:T(8,128)(2,1)} %get-tuple-element.244), channel_id=1, source_target_pairs={{0,1},{1,0},{2,3},{3,2},{4,5},{5,4},{6,7},{7,6},{8,9},{9,8},{10,11... | collective-permute-start | bytes 1572872 | tf_op jit(solution)/shard_map/ppermute | solution.py:226
  197.4 16.7 %collective-permute-start.53 = (bf16[512,512]{1,0:T(8,128)(2,1)S(1)}, bf16[512,512]{1,0:T(8,128)(2,1)S(1)}, u32[]{:S(2)}, u32[]{:S(2)}) collective-permute-start(bf16[512,512]{1,0:T(8,128)(2,1)S(1)} %add_convert_fusion.1), channel_id=1, source_target_pairs={{0,2},{1,3},{2,0},{3,1},{4,6},{5,7},{6,4},{7,5},{8,10},{9,11},{10,... | collective-permute-start | bytes 1572872 | tf_op jit(solution)/shard_map/ppermute | solution.py:226
  (90 other events, 888.5 us)

commit v3 on v2

--- a/solution.py
+++ b/solution.py
@@ -28,6 +28,7 @@
 anywhere = pl.BlockSpec(memory_space=pl.ANY)
 smem = pl.BlockSpec(memory_space=pltpu.SMEM)
 LANES = 128
+ACROSS = (((1,), (1,)), ((), ()))
 
 
 def ring_of(count):
@@ -89,7 +90,7 @@
             outs[k][b] = rows[k * held * CAP : (k + 1) * held * CAP, :]
 
 
-def combine_kernel(blocks, split, peers, held, *refs):
+def combine_kernel(blocks, peers, held, *refs):
     table = refs[0]
     results = refs[1 : 1 + peers * held]
     outs = refs[1 + peers * held : -2]
@@ -108,11 +109,8 @@
         total = lax.dot_general(
             choose[...], gathered[...], (((0,), (0,)), ((), ())), preferred_element_type=F32
         ).astype(BF16)
-        if split:
-            outs[0][...] = total[:half]
-            outs[1][...] = total[half:]
-        else:
-            outs[b][...] = total
+        outs[2 * b][...] = total[:half]
+        outs[2 * b + 1][...] = total[half:]
 
 
 def expert_kernel(sizes, targets, peers, units, features, order_ref, gain_ref, *refs):
@@ -161,38 +159,70 @@
                 outs[g * peers + k][b] = value[n * CAP : (n + 1) * CAP, :]
 
 
-def shared_kernel(peers, features, order_ref, block_ref, gain_ref, *refs):
+def shared_first_kernel(peers, features, order_ref, block_ref, gain_ref, *refs):
     parts = refs[:peers]
-    *weights, ready, gates, ups, downs, sems = refs[peers:]
-    outs = weights[-peers:]
-    weights = weights[:-peers]
-    blocks = downs.shape[0]
-    depth = gates.shape[1] // blocks
+    *weights, gate, up, last_rows, ready, gates, ups, sems = refs[peers:]
+    near = len(weights)
+    depth = gates.shape[1] // (near + 1)
     copies = []
-    for n in range(blocks):
-        start = pl.multiple_of(block_ref[n] * depth, depth)
-        columns = (gates.at[:, pl.ds(start, depth)], ups.at[:, pl.ds(start, depth)], downs.at[block_ref[n]])
-        for m, target in enumerate(columns):
-            source = weights[n].at[m] if n < blocks - 1 or m < 2 else weights[blocks].at[0]
-            copies.append(pltpu.make_async_copy(source, target, sems.at[3 * n + m]))
+    for n in range(near):
+        columns = pl.ds(pl.multiple_of(block_ref[n] * depth, depth), depth)
+        for m, matrix in enumerate((gates, ups)):
+            copies.append(
+                pltpu.make_async_copy(weights[n].at[m], matrix.at[:, columns], sems.at[2 * n + m])
+            )
     for copy in copies:
         copy.start()
+    columns = pl.ds(pl.multiple_of(block_ref[near] * depth, depth), depth)
+    for matrix in (gates, ups):
+        matrix[:, columns] = jnp.zeros((matrix.shape[0], depth), BF16)
     rows = [part[...].astype(F32) for part in parts]
     squares = sum(jnp.sum(r * r, axis=1, keepdims=True) for r in rows)
     inverse_rms = lax.rsqrt(squares / features + epsilon)
     for k in range(peers):
         ready[order_ref[k]] = (rows[k] * inverse_rms * gain_ref[k]).astype(BF16)
+    each = (near + 1) // peers
+    start = pl.multiple_of(block_ref[near] % each * depth, depth)
+    last_rows[...] = ready[block_ref[near] // each, :, pl.ds(start, depth)]
     for copy in copies:
         copy.wait()
     width = ready.shape[2]
-    gate, up = 0.0, 0.0
-    across = (((1,), (1,)), ((), ()))
+    gate_sum, up_sum = 0.0, 0.0
     for q in range(peers):
         columns = slice(q * width, (q + 1) * width)
-        gate = gate + lax.dot_general(ready[q], gates[:, columns], across, preferred_element_type=F32)
-        up = up + lax.dot_general(ready[q], ups[:, columns], across, preferred_element_type=F32)
+        gate_sum = gate_sum + lax.dot_general(ready[q], gates[:, columns], ACROSS, preferred_element_type=F32)
+        up_sum = up_sum + lax.dot_general(ready[q], ups[:, columns], ACROSS, preferred_element_type=F32)
+    gate[...] = gate_sum
+    up[...] = up_sum
+
+
+def shared_last_kernel(peers, order_ref, block_ref, gate_ref, up_ref, rows_ref, left_ref, right_ref, *refs):
+    *weights, downs, sems = refs
+    outs = weights[-peers:]
+    weights = weights[:-peers]
+    near = len(weights)
+    depth = downs.shape[2]
+    copies = [
+        pltpu.make_async_copy(weights[n].at[2], downs.at[block_ref[n]], sems.at[n]) for n in range(near)
+    ]
+    for copy in copies:
+        copy.start()
+    gate, up = gate_ref[...], up_ref[...]
+    if left_ref.shape[2] < depth:
+        cut = left_ref.shape[2]
+        for n, half in enumerate((left_ref, right_ref)):
+            rows = rows_ref[:, n * cut : (n + 1) * cut]
+            gate = gate + lax.dot_general(rows, half[0], ACROSS, preferred_element_type=F32)
+            up = up + lax.dot_general(rows, half[1], ACROSS, preferred_element_type=F32)
+            downs[block_ref[near], :, n * cut : (n + 1) * cut] = half[2]
+    else:
+        gate = gate + lax.dot_general(rows_ref[...], left_ref[0], ACROSS, preferred_element_type=F32)
+        up = up + lax.dot_general(rows_ref[...], left_ref[1], ACROSS, preferred_element_type=F32)
+        downs[block_ref[near]] = right_ref[0]
     hidden = (gate / (1.0 + jnp.exp(-gate)) * up).astype(BF16)
-    each = blocks // peers
+    for copy in copies:
+        copy.wait()
+    each = (near + 1) // peers
     for k in range(peers):
         for m in range(each):
             outs[k][:, m * depth : (m + 1) * depth] = jnp.dot(
@@ -309,10 +339,12 @@
         if step < far:
             weights[step] = [lax.ppermute(left_one, "gx", right), lax.ppermute(right_one, "gx", left)]
         else:
-            weights[step] = [
-                lax.ppermute(left_one[:2], "gx", right),
-                lax.ppermute(right_one[2:], "gx", left),
-            ]
+            cut = shared.shape[2] // 2
+            if cut % LANES == 0:
+                left_one, right_one = left_one[:, :, :cut], right_one[:, :, cut:]
+            else:
+                left_one, right_one = left_one[:2], right_one[2:]
+            weights[step] = [lax.ppermute(left_one, "gx", right), lax.ppermute(right_one, "gx", left)]
         return weights[step]
 
     listed = list(range(far - 1, 0, -1)) + [far, 0]
@@ -360,8 +392,9 @@
         return [values[0]] + [to_peer(values[k], k) for k in range(1, peers)]
 
     inputs = [part for g in listed for part in parts[g]]
-    ahead = weights_step(1, after((shared, shared), groups[far]))
-    inputs, ahead = after((inputs, ahead), last_rows)
+    ahead = weights_step(1, after((shared, shared), groups[far - 1]))
+    inputs, ahead, own_tokens = after((inputs, ahead, tokens), last_rows)
+    pieces = {k: to_peer(own_tokens, k) if k else tokens for k in range(peers)}
     early, next_step = [], 2
     for h in range(held):
         if next_step <= far:
@@ -371,7 +404,7 @@
             result = experts(h, inputs, [listed])
         else:
             result = experts(h, inputs, [far_groups, near_groups])
-        result, inputs, early, ahead = after((result, inputs, early, ahead), None)
+        result, inputs, early, ahead, pieces = after((result, inputs, early, ahead, pieces), None)
         if h < held - 1:
             early.append(back(result))
     late = [back(result[:peers]), back(result[peers:])]
@@ -379,69 +412,96 @@
         ahead = weights_step(step, ahead)
     early_places, late_places = places_of([listed]), places_of([far_groups, near_groups])
 
-    pieces = {0: tokens}
-    mask = peers // 2
-    while mask:
-        for k in list(pieces):
-            pieces[k ^ mask] = to_peer(pieces[k], mask)
-        mask //= 2
     shared_units, depth = shared_out.shape
-    shared_parts = call(
-        lambda *refs: shared_kernel(peers, features, *refs),
-        [((token_count, width), BF16)] * peers,
-        [gain] + [pieces[k] for k in range(peers)] + [w for step in range(far + 1) for w in weights[step]],
+
+    near_weights = [w for step in range(far) for w in weights[step]]
+    shared_sums = call(
+        lambda *refs: shared_first_kernel(peers, features, *refs),
+        [((token_count, shared_units), F32)] * 2 + [((token_count, depth), BF16)],
+        [gain] + [pieces[k] for k in range(peers)] + near_weights,
         [
             pltpu.VMEM((peers, token_count, width), BF16),
             pltpu.VMEM((shared_units, features), BF16),
             pltpu.VMEM((shared_units, features), BF16),
-            pltpu.VMEM((row_count, shared_units, depth), BF16),
-            pltpu.SemaphoreType.DMA((3 * row_count,)),
+            pltpu.SemaphoreType.DMA((2 * (row_count - 1),)),
         ],
-        "shared_experts",
-        [block_of(gain.shape)] + [block_of(tokens.shape)] * peers + [anywhere] * (row_count + 1),
-        [order, block_rows],
+        "shared_first",
+        in_specs=[block_of(gain.shape)] + [block_of(tokens.shape)] * peers + [anywhere] * (row_count - 1),
+        scalars=[order, block_rows],
     )
-    shared_parts = list(shared_parts)
-    mask, last = 1, None
-    while mask < peers:
-        kept = range(0, peers, 2 * mask)
-        arrived = {k: to_peer(shared_parts[k + mask], mask) for k in kept}
-        if 2 * mask == peers:
-            last = arrived[0]
-        else:
+
+    def shared_experts():
+        inputs = [*shared_sums, *weights[far]]
+        return call(
+            lambda *refs: shared_last_kernel(peers, *refs),
+            [((token_count, width), BF16)] * peers,
+            inputs + near_weights,
+            [
+                pltpu.VMEM((row_count, shared_units, depth), BF16),
+                pltpu.SemaphoreType.DMA((row_count - 1,)),
+            ],
+            "shared_last",
+            in_specs=[block_of(v.shape) for v in inputs] + [anywhere] * (row_count - 1),
+            scalars=[order, block_rows],
+        )
+
+    def reduced(values):
+        values = list(values)
+        mask = 1
+        while True:
+            kept = range(0, peers, 2 * mask)
+            arrived = {k: to_peer(values[k + mask], mask) for k in kept}
+            if 2 * mask == peers:
+                return values[0], arrived[0]
             for k in kept:
-                shared_parts[k] = (shared_parts[k].astype(F32) + arrived[k].astype(F32)).astype(BF16)
-        mask *= 2
+                values[k] = (values[k].astype(F32) + arrived[k].astype(F32)).astype(BF16)
+            mask *= 2
 
     def combine(g):
         size = sizes[g]
         number, place = late_places[g]
         sources = [(member, early_places[g][1]) for member in early] + [(late[number], place)]
-        outs = [((half, width), BF16)] * 2 if g == far else [((token_count, width), BF16)] * size
+        outs = [((half, width), BF16)] * (2 * size)
         return call(
-            lambda *refs: combine_kernel(size, g == far, peers, held, *refs),
+            lambda *refs: combine_kernel(size, peers, held, *refs),
             outs,
             [tables[g]] + [value for values, _ in sources for value in values],
             [pltpu.VMEM((slices * CAP, token_count), BF16), pltpu.VMEM((slices * CAP, width), BF16)],
             "combine_rows",
-            [block_of(tables[g].shape)]
+            cost=LONG,
+            in_specs=[block_of(tables[g].shape)]
             + [block_of((size, CAP, width), start // size) for _, start in sources for _ in range(peers)],
         )
 
     def add(*values):
         return sum(v.astype(F32) for v in values).astype(BF16)
 
-    top, bottom = combine(far)
-    top, bottom = lax.ppermute(top, "gx", right), lax.ppermute(bottom, "gx", left)
-    going_left, going_right = combine(far - 1)
-    going_left = jnp.concatenate([going_left[:half], add(going_left[half:], bottom)])
-    going_right = jnp.concatenate([add(going_right[:half], top), going_right[half:]])
-    for g in range(far - 2, -1, -1):
-        from_left, from_right = lax.ppermute(going_right, "gx", right), lax.ppermute(going_left, "gx", left)
-        own = combine(g)
-        if g:
-            going_left, going_right = add(own[0], from_right), add(own[1], from_left)
-    return add(own[0], from_left, from_right, shared_parts[0], last)
+    def to_right(value):
+        return lax.ppermute(value, "gx", right)
+
+    def to_left(value):
+        return lax.ppermute(value, "gx", left)
+
+    late[0], weights[far], shared_sums = after((late[0], weights[far], shared_sums), None)
+    farthest, sums = combine(far), combine(far - 1)
+    first = [to_right(farthest[0]), to_left(farthest[1])]
+    left_top, left_bottom, right_top, right_bottom = sums
+    left_top, right_bottom = to_left(left_top), to_right(right_bottom)
+    shared_parts = shared_experts()
+    first, late[1], shared_parts = after((first, late[1], shared_parts), None)
+    right_top, left_bottom = to_right(add(right_top, first[0])), to_left(add(left_bottom, first[1]))
+    own_part, last_part = reduced(shared_parts)
+    for g in range(far - 2, 0, -1):
+        sums = combine(g)
+        left_top, left_bottom = to_left(add(sums[0], left_top)), to_left(add(sums[1], left_bottom))
+        right_top, right_bottom = to_right(add(sums[2], right_top)), to_right(add(sums[3], right_bottom))
+    sums = combine(0)
+    return jnp.concatenate(
+        [
+            add(sums[0], left_top, right_top, own_part[:half], last_part[:half]),
+            add(sums[1], left_bottom, right_bottom, own_part[half:], last_part[half:]),
+        ]
+    )
 
 
 def solution(mesh):

time: 226 us -> 217 us (0.960)
  waiting for transfers between devices: 79.3 us -> 65.6 us
  starting transfers between devices: 48.7 us -> 54 us
  Pallas kernels: 79.7 us -> 84.3 us
  other arithmetic: 8.72 us -> 5.96 us
  local copies, waits for them, and re-layouts: 8.66 us -> 5.92 us
    ppermute x30, waiting for transfers between devices: 20.2 us -> 10.2 us  [to_peer(): return lax.ppermute(value, 'gy', [(s, s ^ mask) for s in range(peers)])]
    ppermute x3, waiting for transfers between devices: 15.9 us -> 9.25 us  [on_device(): at_left = lax.ppermute(at_left, 'gx', right)]
    ppermute x10 -> x14, waiting for transfers between devices: 23.9 us -> 19.1 us  [the longest x7 9.98 us: to_left(): return lax.ppermute(value, 'gx', left)]
    pallas_call x11 -> x12, Pallas kernels: 39.1 us -> 43.6 us  [call(): pl.pallas_call(kernel, grid=(1,), out_shape=[pltpu.HBM(shape, dtype) for...]
    ppermute x3, waiting for transfers between devices: 4.1 us -> 8.54 us  [on_device(): at_right = lax.ppermute(at_right, 'gx', left)]
    ppermute x10 -> x14, starting transfers between devices: 10.5 us -> 14.7 us  [the longest x7 9.84 us: to_right(): return lax.ppermute(value, 'gx', right)]
    ppermute x3, starting transfers between devices: 0.91 us -> 5.1 us  [on_device(): at_right = lax.ppermute(at_right, 'gx', left)]
    ppermute x3, starting transfers between devices: 6.28 us -> 2.09 us  [on_device(): at_left = lax.ppermute(at_left, 'gx', right)]
  transfers between devices with their start and end apart: 54 -> 60, of which waited for: 24 -> 25; matrix products, arithmetic and copies ran while one was open for 5% -> 2% of each run, Pallas kernels for 35% -> 39%
where the time goes in v3:
time: 217 us; the launch traced here: 216 us
  Pallas kernels  84.3 us (39%)
  waiting for transfers between devices  65.6 us (30%)
  starting transfers between devices  54 us (25%)
  other arithmetic  5.96 us (3%)
  local copies, waits for them, and re-layouts  5.92 us (3%)
    pallas_call x12, Pallas kernels, call(): pl.pallas_call(kernel, grid=(1,), out_shape=[pltpu.HBM(shape, dtype) for...  43.6 us
    pallas_call x2, Pallas kernels, experts(): pl.pallas_call(lambda *refs: expert_kernel(counts, targets, peers, units,...  40.7 us
    ppermute x30, starting transfers between devices, to_peer(): return lax.ppermute(value, 'gy', [(s, s ^ mask) for s in range(peers)])  21.8 us
    ppermute x4, waiting for transfers between devices, weights_step(): lax.ppermute(left_one, 'gx', right)  12.9 us
    ppermute x30, waiting for transfers between devices, to_peer(): return lax.ppermute(value, 'gy', [(s, s ^ mask) for s in range(peers)])  10.2 us
    ppermute x7, waiting for transfers between devices, to_left(): return lax.ppermute(value, 'gx', left)  9.98 us
    ppermute x7, starting transfers between devices, to_right(): return lax.ppermute(value, 'gx', right)  9.84 us
    ppermute x3, waiting for transfers between devices, on_device(): at_left = lax.ppermute(at_left, 'gx', right)  9.25 us
  transfers between devices with their start and end apart: 60, of which 25 were waited for; matrix products, arithmetic and copies ran while one was open for 2% of the time, Pallas kernels for 39%

profile of v3, /device:TPU:0, one launch (start us, length us, event | category | flops | bytes accessed | tf_op | source)
XLA Modules:
  0.0 216.4 jit_solution(3522143877770402765)
XLA Ops:
  2.8 3.0 %collective-permute-start.1 = (bf16[528,512]{1,0:T(8,128)(2,1)S(1)}, bf16[528,512]{1,0:T(8,128)(2,1)S(1)}, u32[]{:S(2)}, u32[]{:S(2)}) collective-permute-start(bf16[528,512]{1,0:T(8,128)(2,1)S(1)} %pad_maximum_fusion.1.refs_1_), channel_id=1, source_target_pairs={{8,0},{16,8},{24,16},{28,24},{20,28},{12,20},{4,12},{0,4},{9,1},{1... | collective-permute-start | bytes 1622024 | tf_op jit(solution)/shard_map/ppermute | solution.py:313
  6.7 2.5 %dispatch_rows.5 = (bf16[1,128,512]{2,1,0:T(8,128)(2,1)}, bf16[1,128,512]{2,1,0:T(8,128)(2,1)}, bf16[1,128,512]{2,1,0:T(8,128)(2,1)}, bf16[1,128,512]{2,1,0:T(8,128)(2,1)}, f32[1,16,512]{2,1,0:T(8,128)}) custom-call(f32[8,128]{1,0:T(8,128)} %broadcast_in_dim.6.refs_0_, bf16[528,512]{1,0:T(8,128)(2,1)} %copy-done.11), custom_call_target="tpu_custom_call" | custom-call | flops 40000000000 | bytes 100000000 | tf_op jit(solution)/shard_map/dispatch_rows/pallas_call | solution.py:259
  11.9 6.2 %collective-permute-done.1.refs_2_ = bf16[528,512]{1,0:T(8,128)(2,1)S(1)} collective-permute-done((bf16[528,512]{1,0:T(8,128)(2,1)S(1)}, bf16[528,512]{1,0:T(8,128)(2,1)S(1)}, u32[]{:S(2)}, u32[]{:S(2)}) %collective-permute-start.1) | collective-permute-done | bytes 540704 | tf_op jit(solution)/shard_map/ppermute | solution.py:313
  21.5 3.2 %dispatch_rows.6 = (bf16[2,128,512]{2,1,0:T(8,128)(2,1)}, bf16[2,128,512]{2,1,0:T(8,128)(2,1)}, bf16[2,128,512]{2,1,0:T(8,128)(2,1)}, bf16[2,128,512]{2,1,0:T(8,128)(2,1)}, f32[2,16,512]{2,1,0:T(8,128)}) custom-call(f32[8,128]{1,0:T(8,128)} %broadcast_in_dim.6.refs_0_, bf16[528,512]{1,0:T(8,128)(2,1)} %copy-done.35, bf16[528,512]{1,0:T(8,128)(2,1)} %copy-done.34), custom_call_target="tpu_custom_call" | custom-call | flops 40000000000 | bytes 100000000 | tf_op jit(solution)/shard_map/dispatch_rows/pallas_call | solution.py:259
  28.0 4.3 %collective-permute-done.2.refs_1_ = bf16[528,512]{1,0:T(8,128)(2,1)S(1)} collective-permute-done((bf16[528,512]{1,0:T(8,128)(2,1)S(1)}, bf16[528,512]{1,0:T(8,128)(2,1)S(1)}, u32[]{:S(2)}, u32[]{:S(2)}) %collective-permute-start.2) | collective-permute-done | bytes 540704 | tf_op jit(solution)/shard_map/ppermute | solution.py:312
  34.8 3.2 %dispatch_rows.7 = (bf16[2,128,512]{2,1,0:T(8,128)(2,1)}, bf16[2,128,512]{2,1,0:T(8,128)(2,1)}, bf16[2,128,512]{2,1,0:T(8,128)(2,1)}, bf16[2,128,512]{2,1,0:T(8,128)(2,1)}, f32[2,16,512]{2,1,0:T(8,128)}) custom-call(f32[8,128]{1,0:T(8,128)} %broadcast_in_dim.6.refs_0_, bf16[528,512]{1,0:T(8,128)(2,1)} %copy-done.36, bf16[528,512]{1,0:T(8,128)(2,1)} %copy-done.37), custom_call_target="tpu_custom_call" | custom-call | flops 40000000000 | bytes 100000000 | tf_op jit(solution)/shard_map/dispatch_rows/pallas_call | solution.py:259
  41.2 3.5 %collective-permute-done.7.refs_1_ = bf16[528,512]{1,0:T(8,128)(2,1)S(1)} collective-permute-done((bf16[528,512]{1,0:T(8,128)(2,1)S(1)}, bf16[528,512]{1,0:T(8,128)(2,1)S(1)}, u32[]{:S(2)}, u32[]{:S(2)}) %collective-permute-start.7) | collective-permute-done | bytes 540704 | tf_op jit(solution)/shard_map/ppermute | solution.py:312
  48.8 3.2 %dispatch_rows.8 = (bf16[2,128,512]{2,1,0:T(8,128)(2,1)}, bf16[2,128,512]{2,1,0:T(8,128)(2,1)}, bf16[2,128,512]{2,1,0:T(8,128)(2,1)}, bf16[2,128,512]{2,1,0:T(8,128)(2,1)}, f32[2,16,512]{2,1,0:T(8,128)}) custom-call(f32[8,128]{1,0:T(8,128)} %broadcast_in_dim.6.refs_0_, bf16[528,512]{1,0:T(8,128)(2,1)} %copy-done.30, bf16[528,512]{1,0:T(8,128)(2,1)} %copy-done.31), custom_call_target="tpu_custom_call" | custom-call | flops 40000000000 | bytes 100000000 | tf_op jit(solution)/shard_map/dispatch_rows/pallas_call | solution.py:259
  60.6 2.6 %collective-permute-done.13.refs_4_ = bf16[2,128,512]{2,1,0:T(8,128)(2,1)S(1)} collective-permute-done((bf16[2,128,512]{2,1,0:T(8,128)(2,1)}, bf16[2,128,512]{2,1,0:T(8,128)(2,1)S(1)}, u32[]{:S(2)}, u32[]{:S(2)}) %collective-permute-start.13) | collective-permute-done | bytes 262176 | tf_op jit(solution)/shard_map/ppermute | solution.py:256
  64.8 3.2 %collective-permute-done.14.refs_5_ = bf16[2,128,512]{2,1,0:T(8,128)(2,1)S(1)} collective-permute-done((bf16[2,128,512]{2,1,0:T(8,128)(2,1)}, bf16[2,128,512]{2,1,0:T(8,128)(2,1)S(1)}, u32[]{:S(2)}, u32[]{:S(2)}) %collective-permute-start.14) | collective-permute-done | bytes 262176 | tf_op jit(solution)/shard_map/ppermute | solution.py:256
  73.7 8.2 %collective-permute-done.23.refs_8_ = bf16[3,704,256]{2,1,0:T(8,128)(2,1)S(1)} collective-permute-done((bf16[3,704,256]{2,1,0:T(8,128)(2,1)S(1)}, bf16[3,704,256]{2,1,0:T(8,128)(2,1)S(1)}, u32[]{:S(2)}, u32[]{:S(2)}) %collective-permute-start.23) | collective-permute-done | bytes 1081376 | tf_op jit(solution)/shard_map/ppermute | solution.py:340
  86.9 20.3 %expert_slice.2 = (bf16[8,64,512]{2,1,0:T(8,128)(2,1)}, bf16[8,64,512]{2,1,0:T(8,128)(2,1)}, bf16[8,64,512]{2,1,0:T(8,128)(2,1)}, bf16[8,64,512]{2,1,0:T(8,128)(2,1)}) custom-call(s32[4]{0:T(128)} %iota_xor_fusion.refs_0_, f32[4,1,512]{2,1,0:T(1,128)} %reshape.41.refs_1_.refs_2_, bf16[2,128,512]{2,1,0:T(8,128)(2,1)} %get-tuple-element.223.refs_2_, ...), custom_call_target="tpu_custom_call" | custom-call | flops 40000000000 | bytes 100000000 | tf_op jit(solution)/shard_map/expert_slice/pallas_call | solution.py:367
  116.1 20.4 %expert_slice.3 = (bf16[3,64,512]{2,1,0:T(8,128)(2,1)}, bf16[3,64,512]{2,1,0:T(8,128)(2,1)}, bf16[3,64,512]{2,1,0:T(8,128)(2,1)}, bf16[3,64,512]{2,1,0:T(8,128)(...) custom-call(s32[4]{0:T(128)} %iota_xor_fusion.refs_0_, ...), custom_call_target="tpu_custom_call" | custom-call | flops 40000000000 | bytes 100000000 | tf_op jit(solution)/shard_map/expert_slice/pallas_call | solution.py:367
  137.6 2.6 %collective-permute-done.33.refs_12_ = bf16[3,704,256]{2,1,0:T(8,128)(2,1)S(1)} collective-permute-done((bf16[3,704,256]{2,1,0:T(8,128)(2,1)S(1)}, bf16[3,704,256]{2,1,0:T(8,128)(2,1)S(1)}, u32[]{:S(2)}, u32[]{:S(2)}) %collective-permute-start.33) | collective-permute-done | bytes 1081376 | tf_op jit(solution)/shard_map/ppermute | solution.py:340
  147.0 9.1 %shared_first.1 = (f32[512,704]{1,0:T(8,128)}, f32[512,704]{1,0:T(8,128)}, bf16[512,256]{1,0:T(8,128)(2,1)}) custom-call(s32[4]{0:T(128)S(1)} %copy-done, s32[8]{0:T(128)S(1)} %dynamic-slice_bitcast_fusion.refs_1_, f32[4,1,512]{2,1,0:T(1,128)} %reshape.41.refs_1_.refs_2_, bf16[512,512]{1,0:T(8,128)(2,1)} %refs_3_, bf16[512,512]{1,0:T(8,128)(2,1)} %copy-done.16, ...), custom_call_target="tpu_custom_call" | custom-call | tf_op jit(solution)/shard_map/shared_first/pallas_call | solution.py:259
  158.1 2.7 %combine_rows.5 = (bf16[256,512]{1,0:T(8,128)(2,1)}, bf16[256,512]{1,0:T(8,128)(2,1)}) custom-call(f32[1,16,512]{2,1,0:T(8,128)} %get-tuple-element.265.refs_0_, bf16[8,64,512]{2,1,0:T(8,128)(2,1)} %get-tuple-element.261.refs_1_, bf16[8,64,512]{2,1,0:T(8,128)(2,1)} %copy-done.38, bf16[8,64,512]{2,1,0:T(8,128)(2,1)} %copy-done.39, ...), custom_call_target="tpu_custom_call" | custom-call | flops 40000000000 | bytes 100000000 | tf_op jit(solution)/shard_map/combine_rows/pallas_call | solution.py:259
  162.9 2.8 %combine_rows.9 = (bf16[256,512]{1,0:T(8,128)(2,1)}, bf16[256,512]{1,0:T(8,128)(2,1)}, bf16[256,512]{1,0:T(8,128)(2,1)}, bf16[256,512]{1,0:T(8,128)(2,1)}) custom-call(f32[2,16,512]{2,1,0:T(8,128)} %get-tuple-element.307.refs_0_, bf16[8,64,512]{2,1,0:T(8,128)(2,1)} %get-tuple-element.261.refs_1_, bf16[8,64,512]{2,1,0:T(8,128)(2,1)} %copy-done.38, ...), custom_call_target="tpu_custom_call" | custom-call | flops 40000000000 | bytes 100000000 | tf_op jit(solution)/shard_map/combine_rows/pallas_call | solution.py:259
  165.7 6.6 %shared_last.1 = (bf16[512,512]{1,0:T(8,128)(2,1)}, bf16[512,512]{1,0:T(8,128)(2,1)}, bf16[512,512]{1,0:T(8,128)(2,1)}, bf16[512,512]{1,0:T(8,128)(2,1)}) custom-call(s32[4]{0:T(128)S(1)} %copy-done, s32[8]{0:T(128)S(1)} %dynamic-slice_bitcast_fusion.refs_1_, f32[512,704]{1,0:T(8,128)} %get-tuple-element.289.refs_2_, f32[512,704]{1,0:T(8,128)} %get-tuple-element.290.refs_3_, ...), custom_call_target="tpu_custom_call" | custom-call | tf_op jit(solution)/shard_map/shared_last/pallas_call | solution.py:259
  179.1 2.8 %combine_rows.8 = (bf16[256,512]{1,0:T(8,128)(2,1)}, bf16[256,512]{1,0:T(8,128)(2,1)}, bf16[256,512]{1,0:T(8,128)(2,1)}, bf16[256,512]{1,0:T(8,128)(2,1)}) custom-call(f32[2,16,512]{2,1,0:T(8,128)} %get-tuple-element.305.refs_0_, bf16[8,64,512]{2,1,0:T(8,128)(2,1)} %get-tuple-element.261.refs_1_, bf16[8,64,512]{2,1,0:T(8,128)(2,1)} %copy-done.38, ...), custom_call_target="tpu_custom_call" | custom-call | flops 40000000000 | bytes 100000000 | tf_op jit(solution)/shard_map/combine_rows/pallas_call | solution.py:259
  181.9 2.9 %combine_rows.7 = (bf16[256,512]{1,0:T(8,128)(2,1)}, bf16[256,512]{1,0:T(8,128)(2,1)}, bf16[256,512]{1,0:T(8,128)(2,1)}, bf16[256,512]{1,0:T(8,128)(2,1)}) custom-call(f32[2,16,512]{2,1,0:T(8,128)} %get-tuple-element.303.refs_0_, bf16[8,64,512]{2,1,0:T(8,128)(2,1)} %get-tuple-element.261.refs_1_, bf16[8,64,512]{2,1,0:T(8,128)(2,1)} %copy-done.38, ...), custom_call_target="tpu_custom_call" | custom-call | flops 40000000000 | bytes 100000000 | tf_op jit(solution)/shard_map/combine_rows/pallas_call | solution.py:259
  188.1 5.6 %collective-permute-done.46 = bf16[256,512]{1,0:T(8,128)(2,1)S(1)} collective-permute-done((bf16[256,512]{1,0:T(8,128)(2,1)S(1)}, bf16[256,512]{1,0:T(8,128)(2,1)S(1)}, u32[]{:S(2)}, u32[]{:S(2)}) %collective-permute-start.46) | collective-permute-done | bytes 262176 | tf_op jit(solution)/shard_map/ppermute | solution.py:483
  198.4 4.6 %collective-permute-done.49 = bf16[256,512]{1,0:T(8,128)(2,1)S(1)} collective-permute-done((bf16[256,512]{1,0:T(8,128)(2,1)S(1)}, bf16[256,512]{1,0:T(8,128)(2,1)S(1)}, u32[]{:S(2)}, u32[]{:S(2)}) %collective-permute-start.49) | collective-permute-done | bytes 262176 | tf_op jit(solution)/shard_map/ppermute | solution.py:480
  204.5 3.6 %collective-permute-done.55 = bf16[256,512]{1,0:T(8,128)(2,1)S(1)} collective-permute-done((bf16[256,512]{1,0:T(8,128)(2,1)S(1)}, bf16[256,512]{1,0:T(8,128)(2,1)S(1)}, u32[]{:S(2)}, u32[]{:S(2)}) %collective-permute-start.55) | collective-permute-done | bytes 262176 | tf_op jit(solution)/shard_map/ppermute | solution.py:483
  210.4 4.0 %collective-permute-done.50 = bf16[256,512]{1,0:T(8,128)(2,1)S(1)} collective-permute-done((bf16[256,512]{1,0:T(8,128)(2,1)S(1)}, bf16[256,512]{1,0:T(8,128)(2,1)S(1)}, u32[]{:S(2)}, u32[]{:S(2)}) %collective-permute-start.50) | collective-permute-done | bytes 262176 | tf_op jit(solution)/shard_map/ppermute | solution.py:480
  (273 shorter events, 84.5 us)
Async XLA Ops:
  9.2 15.5 %collective-permute-start.4 = (bf16[1,128,512]{2,1,0:T(8,128)(2,1)}, bf16[1,128,512]{2,1,0:T(8,128)(2,1)S(1)}, u32[]{:S(2)}, u32[]{:S(2)}) collective-permute-start(bf16[1,128,512]{2,1,0:T(8,128)(2,1)} %get-tuple-element.169), channel_id=1, source_target_pairs={{0,1},{1,0},{2,3},{3,2},{4,5},{5,4},{6,7},{7,6},{8,9},{9,8},{10,11... | collective-permute-start | bytes 393224 | tf_op jit(solution)/shard_map/ppermute | solution.py:256
  9.2 15.6 %collective-permute-start.5 = (bf16[1,128,512]{2,1,0:T(8,128)(2,1)}, bf16[1,128,512]{2,1,0:T(8,128)(2,1)S(1)}, u32[]{:S(2)}, u32[]{:S(2)}) collective-permute-start(bf16[1,128,512]{2,1,0:T(8,128)(2,1)} %get-tuple-element.170), channel_id=1, source_target_pairs={{0,2},{1,3},{2,0},{3,1},{4,6},{5,7},{6,4},{7,5},{8,10},{9,11},{10,... | collective-permute-start | bytes 393224 | tf_op jit(solution)/shard_map/ppermute | solution.py:256
  11.1 15.9 %collective-permute-start.6 = (bf16[1,128,512]{2,1,0:T(8,128)(2,1)}, bf16[1,128,512]{2,1,0:T(8,128)(2,1)S(1)}, u32[]{:S(2)}, u32[]{:S(2)}) collective-permute-start(bf16[1,128,512]{2,1,0:T(8,128)(2,1)} %get-tuple-element.171), channel_id=1, source_target_pairs={{0,3},{1,2},{2,1},{3,0},{4,7},{5,6},{6,5},{7,4},{8,11},{9,10},{10,... | collective-permute-start | bytes 393224 | tf_op jit(solution)/shard_map/ppermute | solution.py:256
  38.0 17.3 %collective-permute-start.15 = (bf16[2,128,512]{2,1,0:T(8,128)(2,1)}, bf16[2,128,512]{2,1,0:T(8,128)(2,1)S(1)}, u32[]{:S(2)}, u32[]{:S(2)}) collective-permute-start(bf16[2,128,512]{2,1,0:T(8,128)(2,1)} %get-tuple-element.185), channel_id=1, source_target_pairs={{0,1},{1,0},{2,3},{3,2},{4,5},{5,4},{6,7},{7,6},{8,9},{9,8},{10,11... | collective-permute-start | bytes 786440 | tf_op jit(solution)/shard_map/ppermute | solution.py:256
  38.1 18.0 %collective-permute-start.16 = (bf16[2,128,512]{2,1,0:T(8,128)(2,1)}, bf16[2,128,512]{2,1,0:T(8,128)(2,1)}, u32[]{:S(2)}, u32[]{:S(2)}) collective-permute-start(bf16[2,128,512]{2,1,0:T(8,128)(2,1)} %get-tuple-element.186), channel_id=1, source_target_pairs={{0,2},{1,3},{2,0},{3,1},{4,6},{5,7},{6,4},{7,5},{8,10},{9,11},{10,... | collective-permute-start | bytes 786440 | tf_op jit(solution)/shard_map/ppermute | solution.py:256
  39.7 17.9 %collective-permute-start.17 = (bf16[2,128,512]{2,1,0:T(8,128)(2,1)}, bf16[2,128,512]{2,1,0:T(8,128)(2,1)}, u32[]{:S(2)}, u32[]{:S(2)}) collective-permute-start(bf16[2,128,512]{2,1,0:T(8,128)(2,1)} %get-tuple-element.187), channel_id=1, source_target_pairs={{0,3},{1,2},{2,1},{3,0},{4,7},{5,6},{6,5},{7,4},{8,11},{9,10},{10,... | collective-permute-start | bytes 786440 | tf_op jit(solution)/shard_map/ppermute | solution.py:256
  56.1 25.8 %collective-permute-start.23 = (bf16[3,704,256]{2,1,0:T(8,128)(2,1)S(1)}, bf16[3,704,256]{2,1,0:T(8,128)(2,1)S(1)}, u32[]{:S(2)}, u32[]{:S(2)}) collective-permute-start(bf16[3,704,256]{2,1,0:T(8,128)(2,1)S(1)} %pad_maximum_fusion.refs_7_), channel_id=1, source_target_pairs={{0,8},{8,16},{16,24},{24,28},{28,20},{20,12},{12,4},{4,0},{1,9},{9... | collective-permute-start | bytes 3244040 | tf_op jit(solution)/shard_map/ppermute | solution.py:340
  57.6 25.5 %collective-permute-start.24 = (bf16[3,704,256]{2,1,0:T(8,128)(2,1)S(1)}, bf16[3,704,256]{2,1,0:T(8,128)(2,1)S(1)}, u32[]{:S(2)}, u32[]{:S(2)}) collective-permute-start(bf16[3,704,256]{2,1,0:T(8,128)(2,1)S(1)} %pad_maximum_fusion.refs_7_), channel_id=1, source_target_pairs={{8,0},{16,8},{24,16},{28,24},{20,28},{12,20},{4,12},{0,4},{9,1},{1... | collective-permute-start | bytes 3244040 | tf_op jit(solution)/shard_map/ppermute | solution.py:340
  83.1 24.2 %collective-permute-start.29 = (bf16[512,512]{1,0:T(8,128)(2,1)}, bf16[512,512]{1,0:T(8,128)(2,1)S(1)}, u32[]{:S(2)}, u32[]{:S(2)}) collective-permute-start(bf16[512,512]{1,0:T(8,128)(2,1)} %refs_3_), channel_id=1, source_target_pairs={{0,3},{1,2},{2,1},{3,0},{4,7},{5,6},{6,5},{7,4},{8,11},{9,10},{10,... | collective-permute-start | bytes 1572872 | tf_op jit(solution)/shard_map/ppermute | solution.py:256
  84.0 24.7 %collective-permute-start.28 = (bf16[512,512]{1,0:T(8,128)(2,1)}, bf16[512,512]{1,0:T(8,128)(2,1)S(1)}, u32[]{:S(2)}, u32[]{:S(2)}) collective-permute-start(bf16[512,512]{1,0:T(8,128)(2,1)} %refs_3_), channel_id=1, source_target_pairs={{0,2},{1,3},{2,0},{3,1},{4,6},{5,7},{6,4},{7,5},{8,10},{9,11},{10,... | collective-permute-start | bytes 1572872 | tf_op jit(solution)/shard_map/ppermute | solution.py:256
  84.6 24.1 %collective-permute-start.27 = (bf16[512,512]{1,0:T(8,128)(2,1)}, bf16[512,512]{1,0:T(8,128)(2,1)S(1)}, u32[]{:S(2)}, u32[]{:S(2)}) collective-permute-start(bf16[512,512]{1,0:T(8,128)(2,1)} %refs_3_), channel_id=1, source_target_pairs={{0,1},{1,0},{2,3},{3,2},{4,5},{5,4},{6,7},{7,6},{8,9},{9,8},{10,11... | collective-permute-start | bytes 1572872 | tf_op jit(solution)/shard_map/ppermute | solution.py:256
  84.9 25.9 %collective-permute-start.25 = (bf16[3,704,256]{2,1,0:T(8,128)(2,1)S(1)}, bf16[3,704,256]{2,1,0:T(8,128)(2,1)S(1)}, u32[]{:S(2)}, u32[]{:S(2)}) collective-permute-start(bf16[3,704,256]{2,1,0:T(8,128)(2,1)S(1)} %collective-permute-done.23.refs_8_), channel_id=1, source_target_pairs={{0,8},{8,16},{16,24},{24,28},{28,20},{20,12},{12,4},{4,0},{1,9},{9... | collective-permute-start | bytes 3244040 | tf_op jit(solution)/shard_map/ppermute | solution.py:340
  86.5 25.7 %collective-permute-start.26 = (bf16[3,704,256]{2,1,0:T(8,128)(2,1)S(1)}, bf16[3,704,256]{2,1,0:T(8,128)(2,1)S(1)}, u32[]{:S(2)}, u32[]{:S(2)}) collective-permute-start(bf16[3,704,256]{2,1,0:T(8,128)(2,1)S(1)} %collective-permute-done.24.refs_9_), channel_id=1, source_target_pairs={{8,0},{16,8},{24,16},{28,24},{20,28},{12,20},{4,12},{0,4},{9,1},{1... | collective-permute-start | bytes 3244040 | tf_op jit(solution)/shard_map/ppermute | solution.py:340
  112.2 24.4 %collective-permute-start.30 = (bf16[8,64,512]{2,1,0:T(8,128)(2,1)}, bf16[8,64,512]{2,1,0:T(8,128)(2,1)S(1)}, u32[]{:S(2)}, u32[]{:S(2)}) collective-permute-start(bf16[8,64,512]{2,1,0:T(8,128)(2,1)} %get-tuple-element.252), channel_id=1, source_target_pairs={{0,1},{1,0},{2,3},{3,2},{4,5},{5,4},{6,7},{7,6},{8,9},{9,8},{10,11... | collective-permute-start | bytes 1572872 | tf_op jit(solution)/shard_map/ppermute | solution.py:256
  112.2 24.4 %collective-permute-start.31 = (bf16[8,64,512]{2,1,0:T(8,128)(2,1)}, bf16[8,64,512]{2,1,0:T(8,128)(2,1)S(1)}, u32[]{:S(2)}, u32[]{:S(2)}) collective-permute-start(bf16[8,64,512]{2,1,0:T(8,128)(2,1)} %get-tuple-element.253), channel_id=1, source_target_pairs={{0,2},{1,3},{2,0},{3,1},{4,6},{5,7},{6,4},{7,5},{8,10},{9,11},{10,... | collective-permute-start | bytes 1572872 | tf_op jit(solution)/shard_map/ppermute | solution.py:256
  113.6 24.0 %collective-permute-start.32 = (bf16[8,64,512]{2,1,0:T(8,128)(2,1)}, bf16[8,64,512]{2,1,0:T(8,128)(2,1)S(1)}, u32[]{:S(2)}, u32[]{:S(2)}) collective-permute-start(bf16[8,64,512]{2,1,0:T(8,128)(2,1)} %get-tuple-element.254), channel_id=1, source_target_pairs={{0,3},{1,2},{2,1},{3,0},{4,7},{5,6},{6,5},{7,4},{8,11},{9,10},{10,... | collective-permute-start | bytes 1572872 | tf_op jit(solution)/shard_map/ppermute | solution.py:256
  114.1 26.1 %collective-permute-start.33 = (bf16[3,704,256]{2,1,0:T(8,128)(2,1)S(1)}, bf16[3,704,256]{2,1,0:T(8,128)(2,1)S(1)}, u32[]{:S(2)}, u32[]{:S(2)}) collective-permute-start(bf16[3,704,256]{2,1,0:T(8,128)(2,1)S(1)} %collective-permute-done.25.refs_10_), channel_id=1, source_target_pairs={{0,8},{8,16},{16,24},{24,28},{28,20},{20,12},{12,4},{4,0},{1,9},{9... | collective-permute-start | bytes 3244040 | tf_op jit(solution)/shard_map/ppermute | solution.py:340
  115.6 25.8 %collective-permute-start.34 = (bf16[3,704,256]{2,1,0:T(8,128)(2,1)S(1)}, bf16[3,704,256]{2,1,0:T(8,128)(2,1)S(1)}, u32[]{:S(2)}, u32[]{:S(2)}) collective-permute-start(bf16[3,704,256]{2,1,0:T(8,128)(2,1)S(1)} %collective-permute-done.26.refs_11_), channel_id=1, source_target_pairs={{8,0},{16,8},{24,16},{28,24},{20,28},{12,20},{4,12},{0,4},{9,1},{1... | collective-permute-start | bytes 3244040 | tf_op jit(solution)/shard_map/ppermute | solution.py:340
  142.4 15.7 %collective-permute-start.39 = (bf16[3,704,128]{2,1,0:T(8,128)(2,1)S(1)}, bf16[3,704,128]{2,1,0:T(8,128)(2,1)S(1)}, u32[]{:S(2)}, u32[]{:S(2)}) collective-permute-start(bf16[3,704,128]{2,1,0:T(8,128)(2,1)S(1)} %slice.27), channel_id=1, source_target_pairs={{8,0},{16,8},{24,16},{28,24},{20,28},{12,20},{4,12},{0,4},{9,1},{1... | collective-permute-start | bytes 1622024 | tf_op jit(solution)/shard_map/ppermute | solution.py:347
  156.1 16.2 %collective-permute-start.42 = (bf16[5,64,512]{2,1,0:T(8,128)(2,1)S(1)}, bf16[5,64,512]{2,1,0:T(8,128)(2,1)S(1)}, u32[]{:S(2)}, u32[]{:S(2)}) collective-permute-start(bf16[5,64,512]{2,1,0:T(8,128)(2,1)S(1)} %copy-done.45), channel_id=1, source_target_pairs={{0,1},{1,0},{2,3},{3,2},{4,5},{5,4},{6,7},{7,6},{8,9},{9,8},{10,11... | collective-permute-start | bytes 983048 | tf_op jit(solution)/shard_map/ppermute | solution.py:256
  156.5 16.4 %collective-permute-start.43 = (bf16[5,64,512]{2,1,0:T(8,128)(2,1)S(1)}, bf16[5,64,512]{2,1,0:T(8,128)(2,1)S(1)}, u32[]{:S(2)}, u32[]{:S(2)}) collective-permute-start(bf16[5,64,512]{2,1,0:T(8,128)(2,1)S(1)} %copy-done.44), channel_id=1, source_target_pairs={{0,2},{1,3},{2,0},{3,1},{4,6},{5,7},{6,4},{7,5},{8,10},{9,11},{10,... | collective-permute-start | bytes 983048 | tf_op jit(solution)/shard_map/ppermute | solution.py:256
  157.9 16.6 %collective-permute-start.44 = (bf16[5,64,512]{2,1,0:T(8,128)(2,1)S(1)}, bf16[5,64,512]{2,1,0:T(8,128)(2,1)S(1)}, u32[]{:S(2)}, u32[]{:S(2)}) collective-permute-start(bf16[5,64,512]{2,1,0:T(8,128)(2,1)S(1)} %copy-done.43), channel_id=1, source_target_pairs={{0,3},{1,2},{2,1},{3,0},{4,7},{5,6},{6,5},{7,4},{8,11},{9,10},{10,... | collective-permute-start | bytes 983048 | tf_op jit(solution)/shard_map/ppermute | solution.py:256
  176.2 19.1 %collective-permute-start.54 = (bf16[256,512]{1,0:T(8,128)(2,1)S(1)}, bf16[256,512]{1,0:T(8,128)(2,1)S(1)}, u32[]{:S(2)}, u32[]{:S(2)}) collective-permute-start(bf16[256,512]{1,0:T(8,128)(2,1)S(1)} %add_convert_fusion.7), channel_id=1, source_target_pairs={{8,0},{16,8},{24,16},{28,24},{20,28},{12,20},{4,12},{0,4},{9,1},{1... | collective-permute-start | bytes 786440 | tf_op jit(solution)/shard_map/ppermute | solution.py:483
  176.8 32.0 %collective-permute-start.51 = (bf16[512,512]{1,0:T(8,128)(2,1)S(1)}, bf16[512,512]{1,0:T(8,128)(2,1)S(1)}, u32[]{:S(2)}, u32[]{:S(2)}) collective-permute-start(bf16[512,512]{1,0:T(8,128)(2,1)S(1)} %copy-done.41), channel_id=1, source_target_pairs={{0,1},{1,0},{2,3},{3,2},{4,5},{5,4},{6,7},{7,6},{8,9},{9,8},{10,11... | collective-permute-start | bytes 1572872 | tf_op jit(solution)/shard_map/ppermute | solution.py:256
  (100 other events, 948.4 us)

commit v4 on v3

--- a/solution.py
+++ b/solution.py
@@ -252,6 +252,18 @@
 
     right, left = ring_of(row_count)
 
+    def after(values, *others):
+        return lax.optimization_barrier((values, others))[0]
+
+    ring_order = [a for a, _ in right]
+    nearby = []
+    for i in range(row_count):
+        p = ring_order.index(i)
+        steps = [0] + [d for s in range(1, far) for d in (-s, s)] + [-far]
+        nearby.append([ring_order[(p + d) % row_count] for d in steps])
+    block_rows = jnp.asarray(nearby, jnp.int32)[row]
+    named, order, gain, block_rows = after((named, order, gain, block_rows), None)
+
     def to_peer(value, mask):
         return lax.ppermute(value, "gy", [(s, s ^ mask) for s in range(peers)])
 
@@ -268,9 +280,6 @@
             cost_estimate=cost,
         )(*scalars, *in_hbm(inputs))
 
-    def after(values, *others):
-        return lax.optimization_barrier((values, others))[0]
-
     meta = jnp.concatenate(
         [
             expert_ids.T.astype(BF16),
@@ -299,7 +308,7 @@
             [named] + [part for block in blocks for part in block] + metas,
             [pltpu.VMEM((slices * CAP, token_count), BF16)],
             "dispatch_rows",
-            cost=LONG,
+            cost=LONG if number < far else None,
         )
         parts[number] = [rows[0]] + [to_peer(rows[k], k) for k in range(1, peers)]
         return rows[0]
@@ -324,13 +333,6 @@
     for number in range(sent, len(batches)):
         last_rows = dispatch(number, groups)
 
-    ring_order = [a for a, _ in right]
-    nearby = []
-    for i in range(row_count):
-        p = ring_order.index(i)
-        steps = [0] + [d for s in range(1, far) for d in (-s, s)] + [-far]
-        nearby.append([ring_order[(p + d) % row_count] for d in steps])
-    block_rows = jnp.asarray(nearby, jnp.int32)[row]
     shared = jnp.concatenate([jnp.swapaxes(shared_in, 1, 2), shared_out[None]], axis=0)
     weights = {0: [shared]}
 
@@ -493,6 +495,7 @@
     own_part, last_part = reduced(shared_parts)
     for g in range(far - 2, 0, -1):
         sums = combine(g)
+        tables[g - 1] = after(tables[g - 1], (left_top, right_top))
         left_top, left_bottom = to_left(add(sums[0], left_top)), to_left(add(sums[1], left_bottom))
         right_top, right_bottom = to_right(add(sums[2], right_top)), to_right(add(sums[3], right_bottom))
     sums = combine(0)

time: 217 us -> 210 us (0.968)
  waiting for transfers between devices: 65.6 us -> 55.4 us
  other arithmetic: 5.96 us -> 9.35 us
    ppermute x4, waiting for transfers between devices: 12.9 us -> 5.27 us  [weights_step(): lax.ppermute(left_one, 'gx', right)]
    ppermute x7, waiting for transfers between devices: 9.14 us -> 4.93 us  [to_right(): return lax.ppermute(value, 'gx', right)]
    convert_element_type x11, other arithmetic: 1.01 us -> 4.93 us  [add(): return sum((v.astype(F32) for v in values)).astype(BF16)]
    ppermute x30, waiting for transfers between devices: 10.2 us -> 12.5 us  [to_peer(): return lax.ppermute(value, 'gy', [(s, s ^ mask) for s in range(peers)])]
  transfers between devices with their start and end apart: 60 -> 60, of which waited for: 25 -> 25; matrix products, arithmetic and copies ran while one was open for 2% -> 3% of each run, Pallas kernels for 39% -> 40%
where the time goes in v4:
time: 210 us; the launch traced here: 209 us
  Pallas kernels  83.7 us (40%)
  waiting for transfers between devices  55.4 us (26%)
  starting transfers between devices  52.9 us (25%)
  other arithmetic  9.35 us (4%)
  local copies, waits for them, and re-layouts  6.36 us (3%)
    pallas_call x12, Pallas kernels, call(): pl.pallas_call(kernel, grid=(1,), out_shape=[pltpu.HBM(shape, dtype) for...  43 us
    pallas_call x2, Pallas kernels, experts(): pl.pallas_call(lambda *refs: expert_kernel(counts, targets, peers, units,...  40.7 us
    ppermute x30, starting transfers between devices, to_peer(): return lax.ppermute(value, 'gy', [(s, s ^ mask) for s in range(peers)])  20.7 us
    ppermute x30, waiting for transfers between devices, to_peer(): return lax.ppermute(value, 'gy', [(s, s ^ mask) for s in range(peers)])  12.5 us
    ppermute x7, waiting for transfers between devices, to_left(): return lax.ppermute(value, 'gx', left)  11.3 us
    ppermute x7, starting transfers between devices, to_right(): return lax.ppermute(value, 'gx', right)  10.7 us
    ppermute x3, waiting for transfers between devices, on_device(): at_left = lax.ppermute(at_left, 'gx', right)  9.8 us
    ppermute x3, waiting for transfers between devices, on_device(): at_right = lax.ppermute(at_right, 'gx', left)  7 us
  transfers between devices with their start and end apart: 60, of which 25 were waited for; matrix products, arithmetic and copies ran while one was open for 3% of the time, Pallas kernels for 40%

profile of v4, /device:TPU:0, one launch (start us, length us, event | category | flops | bytes accessed | tf_op | source)
XLA Modules:
  0.0 208.5 jit_solution(13349535076102393365)
XLA Ops:
  2.8 3.0 %collective-permute-start.1 = (bf16[528,512]{1,0:T(8,128)(2,1)S(1)}, bf16[528,512]{1,0:T(8,128)(2,1)S(1)}, u32[]{:S(2)}, u32[]{:S(2)}) collective-permute-start(bf16[528,512]{1,0:T(8,128)(2,1)S(1)} %pad_maximum_fusion.1.refs_1_), channel_id=1, source_target_pairs={{8,0},{16,8},{24,16},{28,24},{20,28},{12,20},{4,12},{0,4},{9,1},{1... | collective-permute-start | bytes 1622024 | tf_op jit(solution)/shard_map/ppermute | solution.py:322
  9.1 2.4 %dispatch_rows.5 = (bf16[1,128,512]{2,1,0:T(8,128)(2,1)}, bf16[1,128,512]{2,1,0:T(8,128)(2,1)}, bf16[1,128,512]{2,1,0:T(8,128)(2,1)}, bf16[1,128,512]{2,1,0:T(8,128)(2,1)}, f32[1,16,512]{2,1,0:T(8,128)}) custom-call(f32[8,128]{1,0:T(8,128)} %broadcast_in_dim.6.refs_0_, bf16[528,512]{1,0:T(8,128)(2,1)} %copy-done.12), custom_call_target="tpu_custom_call" | custom-call | flops 40000000000 | bytes 100000000 | tf_op jit(solution)/shard_map/dispatch_rows/pallas_call | solution.py:271
  13.5 4.6 %collective-permute-done.1.refs_2_ = bf16[528,512]{1,0:T(8,128)(2,1)S(1)} collective-permute-done((bf16[528,512]{1,0:T(8,128)(2,1)S(1)}, bf16[528,512]{1,0:T(8,128)(2,1)S(1)}, u32[]{:S(2)}, u32[]{:S(2)}) %collective-permute-start.1) | collective-permute-done | bytes 540704 | tf_op jit(solution)/shard_map/ppermute | solution.py:322
  21.6 3.2 %dispatch_rows.6 = (bf16[2,128,512]{2,1,0:T(8,128)(2,1)}, bf16[2,128,512]{2,1,0:T(8,128)(2,1)}, bf16[2,128,512]{2,1,0:T(8,128)(2,1)}, bf16[2,128,512]{2,1,0:T(8,128)(2,1)}, f32[2,16,512]{2,1,0:T(8,128)}) custom-call(f32[8,128]{1,0:T(8,128)} %broadcast_in_dim.6.refs_0_, bf16[528,512]{1,0:T(8,128)(2,1)} %copy-done.32, bf16[528,512]{1,0:T(8,128)(2,1)} %copy-done.31), custom_call_target="tpu_custom_call" | custom-call | flops 40000000000 | bytes 100000000 | tf_op jit(solution)/shard_map/dispatch_rows/pallas_call | solution.py:271
  27.3 5.0 %collective-permute-done.2.refs_1_ = bf16[528,512]{1,0:T(8,128)(2,1)S(1)} collective-permute-done((bf16[528,512]{1,0:T(8,128)(2,1)S(1)}, bf16[528,512]{1,0:T(8,128)(2,1)S(1)}, u32[]{:S(2)}, u32[]{:S(2)}) %collective-permute-start.2) | collective-permute-done | bytes 540704 | tf_op jit(solution)/shard_map/ppermute | solution.py:321
  34.8 3.2 %dispatch_rows.7 = (bf16[2,128,512]{2,1,0:T(8,128)(2,1)}, bf16[2,128,512]{2,1,0:T(8,128)(2,1)}, bf16[2,128,512]{2,1,0:T(8,128)(2,1)}, bf16[2,128,512]{2,1,0:T(8,128)(2,1)}, f32[2,16,512]{2,1,0:T(8,128)}) custom-call(f32[8,128]{1,0:T(8,128)} %broadcast_in_dim.6.refs_0_, bf16[528,512]{1,0:T(8,128)(2,1)} %copy-done.33, bf16[528,512]{1,0:T(8,128)(2,1)} %copy-done.34), custom_call_target="tpu_custom_call" | custom-call | flops 40000000000 | bytes 100000000 | tf_op jit(solution)/shard_map/dispatch_rows/pallas_call | solution.py:271
  41.3 3.4 %collective-permute-done.7.refs_1_ = bf16[528,512]{1,0:T(8,128)(2,1)S(1)} collective-permute-done((bf16[528,512]{1,0:T(8,128)(2,1)S(1)}, bf16[528,512]{1,0:T(8,128)(2,1)S(1)}, u32[]{:S(2)}, u32[]{:S(2)}) %collective-permute-start.7) | collective-permute-done | bytes 540704 | tf_op jit(solution)/shard_map/ppermute | solution.py:321
  50.9 3.2 %dispatch_rows.8 = (bf16[2,128,512]{2,1,0:T(8,128)(2,1)}, bf16[2,128,512]{2,1,0:T(8,128)(2,1)}, bf16[2,128,512]{2,1,0:T(8,128)(2,1)}, bf16[2,128,512]{2,1,0:T(8,128)(2,1)}, f32[2,16,512]{2,1,0:T(8,128)}) custom-call(f32[8,128]{1,0:T(8,128)} %broadcast_in_dim.6.refs_0_, bf16[528,512]{1,0:T(8,128)(2,1)} %copy-done.28, bf16[528,512]{1,0:T(8,128)(2,1)} %copy-done.29), custom_call_target="tpu_custom_call" | custom-call | flops 40000000000 | bytes 100000000 | tf_op jit(solution)/shard_map/dispatch_rows/pallas_call | solution.py:271
  58.2 2.4 %dispatch_rows.9 = (bf16[1,128,512]{2,1,0:T(8,128)(2,1)}, bf16[1,128,512]{2,1,0:T(8,128)(2,1)}, bf16[1,128,512]{2,1,0:T(8,128)(2,1)}, bf16[1,128,512]{2,1,0:T(8,128)(2,1)}, f32[1,16,512]{2,1,0:T(8,128)}) custom-call(f32[8,128]{1,0:T(8,128)} %broadcast_in_dim.6.refs_0_, bf16[272,512]{1,0:T(8,128)(2,1)} %copy-done.19, bf16[256,512]{1,0:T(8,128)(2,1)} %copy-done.27), custom_call_target="tpu_custom_call" | custom-call | tf_op jit(solution)/shard_map/dispatch_rows/pallas_call | solution.py:271
  61.0 4.5 %collective-permute-done.13.refs_4_ = bf16[2,128,512]{2,1,0:T(8,128)(2,1)S(1)} collective-permute-done((bf16[2,128,512]{2,1,0:T(8,128)(2,1)}, bf16[2,128,512]{2,1,0:T(8,128)(2,1)S(1)}, u32[]{:S(2)}, u32[]{:S(2)}) %collective-permute-start.13) | collective-permute-done | bytes 262176 | tf_op jit(solution)/shard_map/ppermute | solution.py:268
  71.6 3.3 %collective-permute-done.22.refs_17_ = bf16[1,128,512]{2,1,0:T(8,128)(2,1)S(1)} collective-permute-done((bf16[1,128,512]{2,1,0:T(8,128)(2,1)}, bf16[1,128,512]{2,1,0:T(8,128)(2,1)S(1)}, u32[]{:S(2)}, u32[]{:S(2)}) %collective-permute-start.22) | collective-permute-done | bytes 131104 | tf_op jit(solution)/shard_map/ppermute | solution.py:268
  79.3 20.3 %expert_slice.2 = (bf16[8,64,512]{2,1,0:T(8,128)(2,1)}, bf16[8,64,512]{2,1,0:T(8,128)(2,1)}, bf16[8,64,512]{2,1,0:T(8,128)(2,1)}, bf16[8,64,512]{2,1,0:T(8,128)(2,1)}) custom-call(s32[4]{0:T(128)} %get-tuple-element.183.refs_0_, f32[4,1,512]{2,1,0:T(1,128)} %reshape.41.refs_1_.refs_2_, bf16[2,128,512]{2,1,0:T(8,128)(2,1)} %get-tuple-element.233.refs_2_, ...), custom_call_target="tpu_custom_call" | custom-call | flops 40000000000 | bytes 100000000 | tf_op jit(solution)/shard_map/expert_slice/pallas_call | solution.py:369
  100.7 2.8 %collective-permute-done.25.refs_10_ = bf16[3,704,256]{2,1,0:T(8,128)(2,1)S(1)} collective-permute-done((bf16[3,704,256]{2,1,0:T(8,128)(2,1)S(1)}, bf16[3,704,256]{2,1,0:T(8,128)(2,1)S(1)}, u32[]{:S(2)}, u32[]{:S(2)}) %collective-permute-start.25) | collective-permute-done | bytes 1081376 | tf_op jit(solution)/shard_map/ppermute | solution.py:342
  108.7 20.3 %expert_slice.3 = (bf16[3,64,512]{2,1,0:T(8,128)(2,1)}, bf16[3,64,512]{2,1,0:T(8,128)(2,1)}, bf16[3,64,512]{2,1,0:T(8,128)(2,1)}, bf16[3,64,512]{2,1,0:T(8,128)(...) custom-call(s32[4]{0:T(128)} %get-tuple-element.183.refs_0_, ...), custom_call_target="tpu_custom_call" | custom-call | flops 40000000000 | bytes 100000000 | tf_op jit(solution)/shard_map/expert_slice/pallas_call | solution.py:369
  130.2 2.5 %collective-permute-done.33.refs_12_ = bf16[3,704,256]{2,1,0:T(8,128)(2,1)S(1)} collective-permute-done((bf16[3,704,256]{2,1,0:T(8,128)(2,1)S(1)}, bf16[3,704,256]{2,1,0:T(8,128)(2,1)S(1)}, u32[]{:S(2)}, u32[]{:S(2)}) %collective-permute-start.33) | collective-permute-done | bytes 1081376 | tf_op jit(solution)/shard_map/ppermute | solution.py:342
  138.9 9.0 %shared_first.1 = (f32[512,704]{1,0:T(8,128)}, f32[512,704]{1,0:T(8,128)}, bf16[512,256]{1,0:T(8,128)(2,1)}) custom-call(s32[4]{0:T(128)S(1)} %copy-done, s32[8]{0:T(128)S(1)} %dynamic-slice_bitcast_fusion.refs_1_, f32[4,1,512]{2,1,0:T(1,128)} %reshape.41.refs_1_.refs_2_, bf16[512,512]{1,0:T(8,128)(2,1)} %refs_3_, bf16[512,512]{1,0:T(8,128)(2,1)} %copy-done.17, ...), custom_call_target="tpu_custom_call" | custom-call | tf_op jit(solution)/shard_map/shared_first/pallas_call | solution.py:271
  150.3 2.4 %combine_rows.5 = (bf16[256,512]{1,0:T(8,128)(2,1)}, bf16[256,512]{1,0:T(8,128)(2,1)}) custom-call(f32[1,16,512]{2,1,0:T(8,128)} %get-tuple-element.275.refs_0_, bf16[8,64,512]{2,1,0:T(8,128)(2,1)} %get-tuple-element.271.refs_1_, bf16[8,64,512]{2,1,0:T(8,128)(2,1)} %copy-done.35, bf16[8,64,512]{2,1,0:T(8,128)(2,1)} %copy-done.36, ...), custom_call_target="tpu_custom_call" | custom-call | flops 40000000000 | bytes 100000000 | tf_op jit(solution)/shard_map/combine_rows/pallas_call | solution.py:271
  154.8 2.8 %combine_rows.7 = (bf16[256,512]{1,0:T(8,128)(2,1)}, bf16[256,512]{1,0:T(8,128)(2,1)}, bf16[256,512]{1,0:T(8,128)(2,1)}, bf16[256,512]{1,0:T(8,128)(2,1)}) custom-call(f32[2,16,512]{2,1,0:T(8,128)} %get-tuple-element.314.refs_0_, bf16[8,64,512]{2,1,0:T(8,128)(2,1)} %get-tuple-element.271.refs_1_, bf16[8,64,512]{2,1,0:T(8,128)(2,1)} %copy-done.35, ...), custom_call_target="tpu_custom_call" | custom-call | flops 40000000000 | bytes 100000000 | tf_op jit(solution)/shard_map/combine_rows/pallas_call | solution.py:271
  157.6 6.6 %shared_last.1 = (bf16[512,512]{1,0:T(8,128)(2,1)}, bf16[512,512]{1,0:T(8,128)(2,1)}, bf16[512,512]{1,0:T(8,128)(2,1)}, bf16[512,512]{1,0:T(8,128)(2,1)}) custom-call(s32[4]{0:T(128)S(1)} %copy-done, s32[8]{0:T(128)S(1)} %dynamic-slice_bitcast_fusion.refs_1_, f32[512,704]{1,0:T(8,128)} %get-tuple-element.300.refs_2_, f32[512,704]{1,0:T(8,128)} %get-tuple-element.301.refs_3_, ...), custom_call_target="tpu_custom_call" | custom-call | tf_op jit(solution)/shard_map/shared_last/pallas_call | solution.py:271
  168.7 2.8 %combine_rows.6 = (bf16[256,512]{1,0:T(8,128)(2,1)}, bf16[256,512]{1,0:T(8,128)(2,1)}, bf16[256,512]{1,0:T(8,128)(2,1)}, bf16[256,512]{1,0:T(8,128)(2,1)}) custom-call(f32[2,16,512]{2,1,0:T(8,128)} %get-tuple-element.182.refs_0_, bf16[8,64,512]{2,1,0:T(8,128)(2,1)} %get-tuple-element.271.refs_1_, bf16[8,64,512]{2,1,0:T(8,128)(2,1)} %copy-done.35, ...), custom_call_target="tpu_custom_call" | custom-call | flops 40000000000 | bytes 100000000 | tf_op jit(solution)/shard_map/combine_rows/pallas_call | solution.py:271
  176.0 2.4 %collective-permute-done.47 = bf16[256,512]{1,0:T(8,128)(2,1)S(1)} collective-permute-done((bf16[256,512]{1,0:T(8,128)(2,1)S(1)}, bf16[256,512]{1,0:T(8,128)(2,1)S(1)}, u32[]{:S(2)}, u32[]{:S(2)}) %collective-permute-start.47) | collective-permute-done | bytes 262176 | tf_op jit(solution)/shard_map/ppermute | solution.py:482
  180.0 2.8 %combine_rows.9 = (bf16[256,512]{1,0:T(8,128)(2,1)}, bf16[256,512]{1,0:T(8,128)(2,1)}, bf16[256,512]{1,0:T(8,128)(2,1)}, bf16[256,512]{1,0:T(8,128)(2,1)}) custom-call(f32[2,16,512]{2,1,0:T(8,128)} %get-tuple-element.322.refs_0_, bf16[8,64,512]{2,1,0:T(8,128)(2,1)} %get-tuple-element.271.refs_1_, bf16[8,64,512]{2,1,0:T(8,128)(2,1)} %copy-done.35, ...), custom_call_target="tpu_custom_call" | custom-call | flops 40000000000 | bytes 100000000 | tf_op jit(solution)/shard_map/combine_rows/pallas_call | solution.py:271
  194.6 5.0 %collective-permute-done.55 = bf16[256,512]{1,0:T(8,128)(2,1)S(1)} collective-permute-done((bf16[256,512]{1,0:T(8,128)(2,1)S(1)}, bf16[256,512]{1,0:T(8,128)(2,1)S(1)}, u32[]{:S(2)}, u32[]{:S(2)}) %collective-permute-start.55) | collective-permute-done | bytes 262176 | tf_op jit(solution)/shard_map/ppermute | solution.py:485
  202.9 3.5 %collective-permute-done.56 = bf16[256,512]{1,0:T(8,128)(2,1)S(1)} collective-permute-done((bf16[256,512]{1,0:T(8,128)(2,1)S(1)}, bf16[256,512]{1,0:T(8,128)(2,1)S(1)}, u32[]{:S(2)}, u32[]{:S(2)}) %collective-permute-start.56) | collective-permute-done | bytes 262176 | tf_op jit(solution)/shard_map/ppermute | solution.py:485
  (284 shorter events, 86.4 us)
Async XLA Ops:
  2.8 15.4 %collective-permute-start.1 = (bf16[528,512]{1,0:T(8,128)(2,1)S(1)}, bf16[528,512]{1,0:T(8,128)(2,1)S(1)}, u32[]{:S(2)}, u32[]{:S(2)}) collective-permute-start(bf16[528,512]{1,0:T(8,128)(2,1)S(1)} %pad_maximum_fusion.1.refs_1_), channel_id=1, source_target_pairs={{8,0},{16,8},{24,16},{28,24},{20,28},{12,20},{4,12},{0,4},{9,1},{1... | collective-permute-start | bytes 1622024 | tf_op jit(solution)/shard_map/ppermute | solution.py:322
  48.8 26.0 %collective-permute-start.23 = (bf16[3,704,256]{2,1,0:T(8,128)(2,1)S(1)}, bf16[3,704,256]{2,1,0:T(8,128)(2,1)S(1)}, u32[]{:S(2)}, u32[]{:S(2)}) collective-permute-start(bf16[3,704,256]{2,1,0:T(8,128)(2,1)S(1)} %pad_maximum_fusion.refs_7_), channel_id=1, source_target_pairs={{0,8},{8,16},{16,24},{24,28},{28,20},{20,12},{12,4},{4,0},{1,9},{9... | collective-permute-start | bytes 3244040 | tf_op jit(solution)/shard_map/ppermute | solution.py:342
  50.5 24.8 %collective-permute-start.24 = (bf16[3,704,256]{2,1,0:T(8,128)(2,1)S(1)}, bf16[3,704,256]{2,1,0:T(8,128)(2,1)S(1)}, u32[]{:S(2)}, u32[]{:S(2)}) collective-permute-start(bf16[3,704,256]{2,1,0:T(8,128)(2,1)S(1)} %pad_maximum_fusion.refs_7_), channel_id=1, source_target_pairs={{8,0},{16,8},{24,16},{28,24},{20,28},{12,20},{4,12},{0,4},{9,1},{1... | collective-permute-start | bytes 3244040 | tf_op jit(solution)/shard_map/ppermute | solution.py:342
  75.3 24.4 %collective-permute-start.29 = (bf16[512,512]{1,0:T(8,128)(2,1)S(1)}, bf16[512,512]{1,0:T(8,128)(2,1)S(1)}, u32[]{:S(2)}, u32[]{:S(2)}) collective-permute-start(bf16[512,512]{1,0:T(8,128)(2,1)S(1)} %copy-done.8), channel_id=1, source_target_pairs={{0,3},{1,2},{2,1},{3,0},{4,7},{5,6},{6,5},{7,4},{8,11},{9,10},{10,... | collective-permute-start | bytes 1572872 | tf_op jit(solution)/shard_map/ppermute | solution.py:268
  76.4 24.3 %collective-permute-start.28 = (bf16[512,512]{1,0:T(8,128)(2,1)S(1)}, bf16[512,512]{1,0:T(8,128)(2,1)S(1)}, u32[]{:S(2)}, u32[]{:S(2)}) collective-permute-start(bf16[512,512]{1,0:T(8,128)(2,1)S(1)} %copy-done.8), channel_id=1, source_target_pairs={{0,2},{1,3},{2,0},{3,1},{4,6},{5,7},{6,4},{7,5},{8,10},{9,11},{10,... | collective-permute-start | bytes 1572872 | tf_op jit(solution)/shard_map/ppermute | solution.py:268
  77.2 23.5 %collective-permute-start.27 = (bf16[512,512]{1,0:T(8,128)(2,1)S(1)}, bf16[512,512]{1,0:T(8,128)(2,1)S(1)}, u32[]{:S(2)}, u32[]{:S(2)}) collective-permute-start(bf16[512,512]{1,0:T(8,128)(2,1)S(1)} %copy-done.8), channel_id=1, source_target_pairs={{0,1},{1,0},{2,3},{3,2},{4,5},{5,4},{6,7},{7,6},{8,9},{9,8},{10,11... | collective-permute-start | bytes 1572872 | tf_op jit(solution)/shard_map/ppermute | solution.py:268
  77.2 26.3 %collective-permute-start.25 = (bf16[3,704,256]{2,1,0:T(8,128)(2,1)S(1)}, bf16[3,704,256]{2,1,0:T(8,128)(2,1)S(1)}, u32[]{:S(2)}, u32[]{:S(2)}) collective-permute-start(bf16[3,704,256]{2,1,0:T(8,128)(2,1)S(1)} %collective-permute-done.23.refs_8_), channel_id=1, source_target_pairs={{0,8},{8,16},{16,24},{24,28},{28,20},{20,12},{12,4},{4,0},{1,9},{9... | collective-permute-start | bytes 3244040 | tf_op jit(solution)/shard_map/ppermute | solution.py:342
  78.8 25.9 %collective-permute-start.26 = (bf16[3,704,256]{2,1,0:T(8,128)(2,1)S(1)}, bf16[3,704,256]{2,1,0:T(8,128)(2,1)S(1)}, u32[]{:S(2)}, u32[]{:S(2)}) collective-permute-start(bf16[3,704,256]{2,1,0:T(8,128)(2,1)S(1)} %collective-permute-done.24.refs_9_), channel_id=1, source_target_pairs={{8,0},{16,8},{24,16},{28,24},{20,28},{12,20},{4,12},{0,4},{9,1},{1... | collective-permute-start | bytes 3244040 | tf_op jit(solution)/shard_map/ppermute | solution.py:342
  104.8 24.3 %collective-permute-start.30 = (bf16[8,64,512]{2,1,0:T(8,128)(2,1)}, bf16[8,64,512]{2,1,0:T(8,128)(2,1)S(1)}, u32[]{:S(2)}, u32[]{:S(2)}) collective-permute-start(bf16[8,64,512]{2,1,0:T(8,128)(2,1)} %get-tuple-element.262), channel_id=1, source_target_pairs={{0,1},{1,0},{2,3},{3,2},{4,5},{5,4},{6,7},{7,6},{8,9},{9,8},{10,11... | collective-permute-start | bytes 1572872 | tf_op jit(solution)/shard_map/ppermute | solution.py:268
  104.8 24.3 %collective-permute-start.31 = (bf16[8,64,512]{2,1,0:T(8,128)(2,1)}, bf16[8,64,512]{2,1,0:T(8,128)(2,1)S(1)}, u32[]{:S(2)}, u32[]{:S(2)}) collective-permute-start(bf16[8,64,512]{2,1,0:T(8,128)(2,1)} %get-tuple-element.263), channel_id=1, source_target_pairs={{0,2},{1,3},{2,0},{3,1},{4,6},{5,7},{6,4},{7,5},{8,10},{9,11},{10,... | collective-permute-start | bytes 1572872 | tf_op jit(solution)/shard_map/ppermute | solution.py:268
  106.0 24.2 %collective-permute-start.32 = (bf16[8,64,512]{2,1,0:T(8,128)(2,1)}, bf16[8,64,512]{2,1,0:T(8,128)(2,1)S(1)}, u32[]{:S(2)}, u32[]{:S(2)}) collective-permute-start(bf16[8,64,512]{2,1,0:T(8,128)(2,1)} %get-tuple-element.264), channel_id=1, source_target_pairs={{0,3},{1,2},{2,1},{3,0},{4,7},{5,6},{6,5},{7,4},{8,11},{9,10},{10,... | collective-permute-start | bytes 1572872 | tf_op jit(solution)/shard_map/ppermute | solution.py:268
  106.7 26.1 %collective-permute-start.33 = (bf16[3,704,256]{2,1,0:T(8,128)(2,1)S(1)}, bf16[3,704,256]{2,1,0:T(8,128)(2,1)S(1)}, u32[]{:S(2)}, u32[]{:S(2)}) collective-permute-start(bf16[3,704,256]{2,1,0:T(8,128)(2,1)S(1)} %collective-permute-done.25.refs_10_), channel_id=1, source_target_pairs={{0,8},{8,16},{16,24},{24,28},{28,20},{20,12},{12,4},{4,0},{1,9},{9... | collective-permute-start | bytes 3244040 | tf_op jit(solution)/shard_map/ppermute | solution.py:342
  108.2 25.8 %collective-permute-start.34 = (bf16[3,704,256]{2,1,0:T(8,128)(2,1)S(1)}, bf16[3,704,256]{2,1,0:T(8,128)(2,1)S(1)}, u32[]{:S(2)}, u32[]{:S(2)}) collective-permute-start(bf16[3,704,256]{2,1,0:T(8,128)(2,1)S(1)} %collective-permute-done.26.refs_11_), channel_id=1, source_target_pairs={{8,0},{16,8},{24,16},{28,24},{20,28},{12,20},{4,12},{0,4},{9,1},{1... | collective-permute-start | bytes 3244040 | tf_op jit(solution)/shard_map/ppermute | solution.py:342
  135.0 15.0 %collective-permute-start.39 = (bf16[3,704,128]{2,1,0:T(8,128)(2,1)S(1)}, bf16[3,704,128]{2,1,0:T(8,128)(2,1)S(1)}, u32[]{:S(2)}, u32[]{:S(2)}) collective-permute-start(bf16[3,704,128]{2,1,0:T(8,128)(2,1)S(1)} %slice.27), channel_id=1, source_target_pairs={{8,0},{16,8},{24,16},{28,24},{20,28},{12,20},{4,12},{0,4},{9,1},{1... | collective-permute-start | bytes 1622024 | tf_op jit(solution)/shard_map/ppermute | solution.py:349
  135.5 14.5 %collective-permute-start.38 = (bf16[3,704,128]{2,1,0:T(8,128)(2,1)S(1)}, bf16[3,704,128]{2,1,0:T(8,128)(2,1)S(1)}, u32[]{:S(2)}, u32[]{:S(2)}) collective-permute-start(bf16[3,704,128]{2,1,0:T(8,128)(2,1)S(1)} %slice.26), channel_id=1, source_target_pairs={{0,8},{8,16},{16,24},{24,28},{28,20},{20,12},{12,4},{4,0},{1,9},{9... | collective-permute-start | bytes 1622024 | tf_op jit(solution)/shard_map/ppermute | solution.py:349
  147.9 16.3 %collective-permute-start.42 = (bf16[5,64,512]{2,1,0:T(8,128)(2,1)S(1)}, bf16[5,64,512]{2,1,0:T(8,128)(2,1)S(1)}, u32[]{:S(2)}, u32[]{:S(2)}) collective-permute-start(bf16[5,64,512]{2,1,0:T(8,128)(2,1)S(1)} %copy-done.45), channel_id=1, source_target_pairs={{0,1},{1,0},{2,3},{3,2},{4,5},{5,4},{6,7},{7,6},{8,9},{9,8},{10,11... | collective-permute-start | bytes 983048 | tf_op jit(solution)/shard_map/ppermute | solution.py:268
  148.4 16.4 %collective-permute-start.43 = (bf16[5,64,512]{2,1,0:T(8,128)(2,1)S(1)}, bf16[5,64,512]{2,1,0:T(8,128)(2,1)S(1)}, u32[]{:S(2)}, u32[]{:S(2)}) collective-permute-start(bf16[5,64,512]{2,1,0:T(8,128)(2,1)S(1)} %copy-done.44), channel_id=1, source_target_pairs={{0,2},{1,3},{2,0},{3,1},{4,6},{5,7},{6,4},{7,5},{8,10},{9,11},{10,... | collective-permute-start | bytes 983048 | tf_op jit(solution)/shard_map/ppermute | solution.py:268
  149.6 16.7 %collective-permute-start.44 = (bf16[5,64,512]{2,1,0:T(8,128)(2,1)S(1)}, bf16[5,64,512]{2,1,0:T(8,128)(2,1)S(1)}, u32[]{:S(2)}, u32[]{:S(2)}) collective-permute-start(bf16[5,64,512]{2,1,0:T(8,128)(2,1)S(1)} %copy-done.43), channel_id=1, source_target_pairs={{0,3},{1,2},{2,1},{3,0},{4,7},{5,6},{6,5},{7,4},{8,11},{9,10},{10,... | collective-permute-start | bytes 983048 | tf_op jit(solution)/shard_map/ppermute | solution.py:268
  168.1 18.3 %collective-permute-start.54 = (bf16[256,512]{1,0:T(8,128)(2,1)S(1)}, bf16[256,512]{1,0:T(8,128)(2,1)S(1)}, u32[]{:S(2)}, u32[]{:S(2)}) collective-permute-start(bf16[256,512]{1,0:T(8,128)(2,1)S(1)} %add_convert_fusion.7), channel_id=1, source_target_pairs={{8,0},{16,8},{24,16},{28,24},{20,28},{12,20},{4,12},{0,4},{9,1},{1... | collective-permute-start | bytes 786440 | tf_op jit(solution)/shard_map/ppermute | solution.py:485
  168.7 20.8 %collective-permute-start.51 = (bf16[512,512]{1,0:T(8,128)(2,1)S(1)}, bf16[512,512]{1,0:T(8,128)(2,1)S(1)}, u32[]{:S(2)}, u32[]{:S(2)}) collective-permute-start(bf16[512,512]{1,0:T(8,128)(2,1)S(1)} %copy-done.38), channel_id=1, source_target_pairs={{0,1},{1,0},{2,3},{3,2},{4,5},{5,4},{6,7},{7,6},{8,9},{9,8},{10,11... | collective-permute-start | bytes 1572872 | tf_op jit(solution)/shard_map/ppermute | solution.py:268
  173.4 14.2 %collective-permute-start.52 = (bf16[512,512]{1,0:T(8,128)(2,1)S(1)}, bf16[512,512]{1,0:T(8,128)(2,1)S(1)}, u32[]{:S(2)}, u32[]{:S(2)}) collective-permute-start(bf16[512,512]{1,0:T(8,128)(2,1)S(1)} %copy-done.39), channel_id=1, source_target_pairs={{0,1},{1,0},{2,3},{3,2},{4,5},{5,4},{6,7},{7,6},{8,9},{9,8},{10,11... | collective-permute-start | bytes 1572872 | tf_op jit(solution)/shard_map/ppermute | solution.py:268
  186.4 16.2 %collective-permute-start.49 = (bf16[256,512]{1,0:T(8,128)(2,1)S(1)}, bf16[256,512]{1,0:T(8,128)(2,1)S(1)}, u32[]{:S(2)}, u32[]{:S(2)}) collective-permute-start(bf16[256,512]{1,0:T(8,128)(2,1)S(1)} %add_convert_fusion.10), channel_id=1, source_target_pairs={{8,0},{16,8},{24,16},{28,24},{20,28},{12,20},{4,12},{0,4},{9,1},{1... | collective-permute-start | bytes 786440 | tf_op jit(solution)/shard_map/ppermute | solution.py:485
  187.7 14.9 %collective-permute-start.59 = (bf16[256,512]{1,0:T(8,128)(2,1)S(1)}, bf16[256,512]{1,0:T(8,128)(2,1)S(1)}, u32[]{:S(2)}, u32[]{:S(2)}) collective-permute-start(bf16[256,512]{1,0:T(8,128)(2,1)S(1)} %add_convert_fusion.3), channel_id=1, source_target_pairs={{0,8},{8,16},{16,24},{24,28},{28,20},{20,12},{12,4},{4,0},{1,9},{9... | collective-permute-start | bytes 786440 | tf_op jit(solution)/shard_map/ppermute | solution.py:482
  189.4 16.9 %collective-permute-start.53 = (bf16[512,512]{1,0:T(8,128)(2,1)S(1)}, bf16[512,512]{1,0:T(8,128)(2,1)S(1)}, u32[]{:S(2)}, u32[]{:S(2)}) collective-permute-start(bf16[512,512]{1,0:T(8,128)(2,1)S(1)} %add_convert_fusion), channel_id=1, source_target_pairs={{0,2},{1,3},{2,0},{3,1},{4,6},{5,7},{6,4},{7,5},{8,10},{9,11},{10,... | collective-permute-start | bytes 1572872 | tf_op jit(solution)/shard_map/ppermute | solution.py:268
  (106 other events, 989.8 us)
